TPU v7x, 256 devices: a whole 4x4x8 slice. The times are simulated.
256 devices in a mesh: section: 32 (over z_lo, x, core), tensor: 8 (over z_hi, y).
Axes of the slice: x: 4, y: 4, z: 8 (z_hi: 2, z_lo: 4; z = z_hi * 4 + z_lo), core: 2. Of those that a mesh axis runs over, the one named last changes fastest.
Arguments:
- stream_two: bfloat16 [32, 128, 4096], P('section', None, 'tensor'), may hold values from -6 to 6
- block_last: bfloat16 [32, 128, 4096], P('section', None, 'tensor'), may hold values from -3 to 3
- incoming_two: bfloat16 [2, 128, 4096], P(None, None, 'tensor'), may hold values from -6 to 6
- incoming_last: bfloat16 [2, 128, 4096], P(None, None, 'tensor'), may hold values from -3 to 3
- norm_gain: bfloat16 [32, 4096], P('section'), may hold values from 0.099609375 to 1.8984375
- w_query: bfloat16 [32, 4096, 4096], P('section', None, 'tensor'), may hold values from -0.09375 to 0.09375
- w_keyval: bfloat16 [32, 4096, 2, 1024], P('section', None, None, 'tensor'), may hold values from -0.09375 to 0.09375
- w_out: bfloat16 [32, 4096, 4096], P('section', 'tensor'), may hold values from -0.09375 to 0.09375
- keys_cache: bfloat16 [32, 3, 512, 1024], P('section', None, None, 'tensor'), may hold values from -500 to 500, as said below
- values_cache: bfloat16 [32, 3, 512, 1024], P('section', None, None, 'tensor'), may hold values from -6 to 6
- cached_len: int32 [34], replicated, may hold values from 128 to 512, as said below
Outputs:
- stream_out: bfloat16 [32, 3, 128, 4096], P('section', None, None, 'tensor')
- block_out: bfloat16 [32, 3, 128, 4096], P('section', None, None, 'tensor')
Inputs may be any that keep to these rules, and one draw needn't show every extreme that they name: `cached_len`: one micro-batch's length is 512 in every draw. `keys_cache`: keys already rotated to their positions.
All inputs are finite; a program needn't handle non-finite values.
Results may differ from a plain program's by a relative error of at most 0.025.
Values may be sent and summed in bfloat16 or wider, within the bound.
No kernel may reach another device: no remote copies, remote signals or barrier semaphores. Data moves between devices by JAX's collectives and lax.ppermute only.
A program may use at most 128 MiB of HBM per device.

v0:
```python
import jax
import jax.numpy as jnp
from jax import lax
from jax.sharding import PartitionSpec as P

HD = 128


rope_base = 500000.0
norm_eps = 1e-05


def from_behind(value, axis, steps):
    count = lax.axis_size(axis)
    leading, last = (max(0, -steps), min(count, count - steps))
    return lax.ppermute(value, axis, [(source, source + steps) for source in range(leading, last)])


def rotate(values, positions):
    half = values.shape[-1] // 2
    index = jnp.arange(half).astype(jnp.float32)
    freqs = jnp.exp(-jnp.log(rope_base) * 2.0 * index / values.shape[-1])
    angles = positions.astype(jnp.float32)[:, None] * freqs[None, :]
    cos_table = jnp.cos(angles)[:, None, :]
    sin_table = jnp.sin(angles)[:, None, :]
    first_half = values[..., :half]
    second_half = values[..., half:]
    return jnp.concatenate(
        [
            first_half * cos_table - second_half * sin_table,
            second_half * cos_table + first_half * sin_table,
        ],
        -1,
    )


def attend(
    whole_rows, scale_gain, wq_local, wkv_local, wo_local, cached_keys, cached_values, length
):
    widened = whole_rows.astype(jnp.float32)
    inverse_rms = lax.rsqrt(jnp.mean(widened * widened, axis=-1, keepdims=True) + norm_eps)
    normed = (widened * inverse_rms * scale_gain.astype(jnp.float32)).astype(jnp.bfloat16)
    row_count = normed.shape[0]
    heads_local = wq_local.shape[1] // HD
    kv_local = cached_keys.shape[1] // HD
    kv_width = kv_local * HD
    queries = jnp.dot(normed, wq_local, preferred_element_type=jnp.float32)
    keyval = jnp.dot(
        normed,
        wkv_local.reshape(wkv_local.shape[0], 2 * kv_width),
        preferred_element_type=jnp.float32,
    )
    positions = length + jnp.arange(row_count)
    queries = rotate(queries.reshape(row_count, heads_local, HD), positions).astype(jnp.bfloat16)
    new_keys = rotate(keyval[:, :kv_width].reshape(row_count, kv_local, HD), positions).astype(
        jnp.bfloat16
    )
    new_values = keyval[:, kv_width:].reshape(row_count, kv_local, HD).astype(jnp.bfloat16)
    slots = cached_keys.shape[0]
    all_keys = jnp.concatenate([cached_keys.reshape(slots, kv_local, HD), new_keys], 0)
    all_values = jnp.concatenate([cached_values.reshape(slots, kv_local, HD), new_values], 0)
    grouped = queries.reshape(row_count, kv_local, heads_local // kv_local, HD)
    scores = jnp.einsum(
        "tkgd,jkd->kgtj", grouped, all_keys, preferred_element_type=jnp.float32
    ) * HD ** (-0.5)
    query_pos = jnp.arange(row_count)[:, None]
    key_pos = jnp.arange(slots + row_count)[None, :]
    visible = jnp.where(key_pos < slots, key_pos < length, key_pos - slots <= query_pos)
    scores = jnp.where(visible, scores, -1e30)
    row_max = jnp.max(scores, axis=-1, keepdims=True)
    exps = jnp.where(visible, jnp.exp(scores - row_max), 0.0)
    attn_probs = (exps / jnp.sum(exps, axis=-1, keepdims=True)).astype(jnp.bfloat16)
    attended = jnp.einsum(
        "kgtj,jkd->tkgd", attn_probs, all_values, preferred_element_type=jnp.float32
    )
    attended = attended.astype(jnp.bfloat16).reshape(row_count, heads_local * HD)
    partial_value = jnp.dot(attended, wo_local, preferred_element_type=jnp.float32).astype(
        jnp.bfloat16
    )
    return lax.optimization_barrier(partial_value).astype(jnp.float32)


def body(
    stream_two,
    block_last,
    incoming_two,
    incoming_last,
    norm_gain,
    w_query,
    w_keyval,
    w_out,
    keys_cache,
    values_cache,
    cached_len,
):
    sections = lax.axis_size("section")
    section_id = lax.axis_index("section")
    lead_section = section_id == 0
    tick_count = keys_cache.shape[1]
    local_width = stream_two.shape[2]
    offset = lax.axis_index("tensor") * local_width
    streams = []
    blocks = []
    stream_full, block_full, fresh_two, fresh_last = (
        lax.all_gather(stream_two, "tensor", axis=2, tiled=True),
        lax.all_gather(block_last, "tensor", axis=2, tiled=True),
        lax.all_gather(incoming_two, "tensor", axis=2, tiled=True),
        lax.all_gather(incoming_last, "tensor", axis=2, tiled=True),
    )
    current = stream_full[0]
    carried = block_full[0]
    for tick_index in range(tick_count):
        length = cached_len[sections - 1 - section_id + tick_index]
        summand = attend(
            current,
            norm_gain[0],
            w_query[0],
            w_keyval[0],
            w_out[0],
            keys_cache[0, tick_index],
            values_cache[0, tick_index],
            length,
        )
        block_total = lax.psum(summand.astype(jnp.bfloat16), "tensor")
        formed = (current.astype(jnp.float32) + carried.astype(jnp.float32)).astype(jnp.bfloat16)
        streams.append(lax.dynamic_slice_in_dim(formed, offset, local_width, 1))
        blocks.append(lax.dynamic_slice_in_dim(block_total, offset, local_width, 1))
        if tick_index + 1 < tick_count:
            moved_stream, moved_block = from_behind((formed, block_total), "section", 1)
            current = jnp.where(lead_section, fresh_two[tick_index], moved_stream)
            carried = jnp.where(lead_section, fresh_last[tick_index], moved_block)
    return (jnp.stack(streams, 0)[None], jnp.stack(blocks, 0)[None])


def solution(mesh):
    placed = (
        P("section", None, "tensor"),
        P("section", None, "tensor"),
        P(None, None, "tensor"),
        P(None, None, "tensor"),
        P("section", None),
        P("section", None, "tensor"),
        P("section", None, None, "tensor"),
        P("section", "tensor", None),
        P("section", None, None, "tensor"),
        P("section", None, None, "tensor"),
        P(),
    )
    return jax.shard_map(
        body,
        mesh=mesh,
        in_specs=placed,
        out_specs=(P("section", None, None, "tensor"), P("section", None, None, "tensor")),
        check_vma=False,
    )
```

profile of v0, /device:TPU:64, one launch (start us, length us, event | category | flops | bytes accessed | tf_op | source)
XLA Modules:
  0.0 598.0 jit_solution(173182570930343904)
XLA Ops:
  7.2 0.7 all-gather.5.cloned.1.call-update
  7.9 0.7 all-gather.7.cloned.1.call-update
  8.7 0.7 mul.408
  9.4 1.1 fusion.111
  10.5 0.8 copy.56
  11.3 6.5 %copy.55 = bf16[512,4096]{1,0:T(8,128)(2,1)} copy(bf16[512,4096]{0,1:T(8,128)(2,1)} %bitcast.170) | data formatting | bytes 8388608 | tf_op jit(solution)/shard_map/dot_general | solution.py:47
  17.7 0.7 fusion.112
  18.4 0.7 add_convert_fusion.5
  19.1 1.3 add_convert_fusion.3
  20.5 1.3 iota_compare_fusion.1
  21.8 0.7 iota_compare_fusion.3
  22.5 1.1 multiply_cosine_fusion
  23.6 1.3 fusion.43
  24.9 0.7 slice_bitcast_fusion.4
  25.7 46.7 %all-gather.5.cloned.1.call-done = bf16[1,128,4096]{2,1,0:T(8,128)(2,1)} async-done(((bf16[1,128,512]{2,1,0:T(8,128)(2,1)}), bf16[1,128,4096]{2,1,0:T(8,128)(2,1)}) %all-gather.5.cloned.1.call-update) | async-done | bytes 1048592 | tf_op jit(solution)/shard_map/all_gather | solution.py:105
  72.4 59.9 %all-gather.7.cloned.1.call-done = bf16[1,128,4096]{2,1,0:T(8,128)(2,1)} async-done(((bf16[1,128,512]{2,1,0:T(8,128)(2,1)}), bf16[1,128,4096]{2,1,0:T(8,128)(2,1)}) %all-gather.7.cloned.1.call-update) | async-done | bytes 1048592 | tf_op jit(solution)/shard_map/all_gather | solution.py:106
  132.3 2.1 fusion.4
  134.4 0.6 fusion.15
  135.3 0.6 fusion.97
  135.9 0.6 slice.118
  136.5 0.9 copy.57
  137.5 0.8 fusion.94
  138.4 0.9 copy.29
  139.4 3.9 fusion.37
  143.4 0.3 fusion.113
  144.2 0.5 convolution_convert_fusion.5
  144.6 1.7 copy-done
  146.4 1.7 convolution_convert_fusion.2
  148.2 0.5 all-gather.9.cloned.1.call-update
  148.7 0.5 all-gather.11.cloned.1.call-update
  149.3 1.9 collective-permute-start
  151.3 106.0 %all-reduce.4.cloned.1.call-done = bf16[128,4096]{1,0:T(8,128)(2,1)} async-done(((bf16[128,4096]{1,0:T(8,128)(2,1)}), bf16[128,4096]{1,0:T(8,128)(2,1)}) %all-reduce.4.cloned.1.call-update) | async-done | bytes 1048592 | tf_op jit(solution)/shard_map/psum | solution.py:124
  257.3 1.9 collective-permute-start.1
  259.2 0.8 copy.60
  260.1 71.6 %all-gather.9.cloned.1.call-done = bf16[2,128,4096]{2,1,0:T(8,128)(2,1)} async-done(((bf16[2,128,512]{2,1,0:T(8,128)(2,1)}), bf16[2,128,4096]{2,1,0:T(8,128)(2,1)}) %all-gather.9.cloned.1.call-update) | async-done | bytes 2097168 | tf_op jit(solution)/shard_map/all_gather | solution.py:107
  331.7 2.0 fusion.8
  333.7 73.1 %all-gather.11.cloned.1.call-done = bf16[2,128,4096]{2,1,0:T(8,128)(2,1)} async-done(((bf16[2,128,512]{2,1,0:T(8,128)(2,1)}), bf16[2,128,4096]{2,1,0:T(8,128)(2,1)}) %all-gather.11.cloned.1.call-update) | async-done | bytes 2097168 | tf_op jit(solution)/shard_map/all_gather | solution.py:108
  406.9 3.0 fusion.7
  409.9 2.1 collective-permute-start.2
  412.0 0.6 fusion.13
  412.6 0.6 copy-done.24
  413.3 0.9 fusion.98
  414.3 3.7 fusion.35
  418.1 10.3 %collective-permute-done.2 = bf16[128,4096]{1,0:T(8,128)(2,1)} collective-permute-done((bf16[128,4096]{1,0:T(8,128)(2,1)}, bf16[128,4096]{1,0:T(8,128)(2,1)}, u32[]{:S(2)}, u32[]{:S(2)}) %collective-permute-start.2) | collective-permute-done | bytes 1048608 | tf_op jit(solution)/shard_map/ppermute | solution.py:16
  428.4 1.7 multiply_reduce_fusion
  430.1 1.3 fusion.33
  431.7 0.6 fusion.11
  433.8 0.5 convolution_convert_fusion.4
  434.2 1.7 copy-done.1
  436.0 1.7 convolution_convert_fusion.1
  437.8 0.3 fusion.115
  438.6 0.5 convolution_convert_fusion.3
  439.1 1.7 convolution_convert_fusion
  440.8 0.9 constant_dynamic-slice_fusion
  441.8 0.9 dynamic-slice_bitcast_fusion.2
  442.7 129.2 %all-reduce.6.cloned.1.call-done = (bf16[128,4096]{1,0:T(8,128)(2,1)}, bf16[128,4096]{1,0:T(8,128)(2,1)}) async-done(((bf16[128,4096]{1,0:T(8,128)(2,1)}, bf16[128,4096]{1,0:T(8,128)(2,1)}), (bf16[128,4096]{1,0:T(8,128)(2,1)}, bf16[128,4096]{1,0:T(8,128)(2,1)})) %all-reduce.6.cloned.1.call-update) | async-done | bytes 2097168 | tf_op jit(solution)/shard_map/psum | solution.py:124
  571.9 1.9 collective-permute-start.3
  573.8 1.3 slice_bitcast_fusion
  575.1 0.9 dynamic-slice_bitcast_fusion.3
  576.0 0.9 dynamic-slice_bitcast_fusion.1
  577.0 0.9 dynamic-slice_bitcast_fusion
  577.9 0.8 maximum_bitcast_fusion.1
  578.7 11.6 %collective-permute-done.3 = bf16[128,4096]{1,0:T(8,128)(2,1)S(1)} collective-permute-done((bf16[128,4096]{1,0:T(8,128)(2,1)}, bf16[128,4096]{1,0:T(8,128)(2,1)S(1)}, u32[]{:S(2)}, u32[]{:S(2)}) %collective-permute-start.3) | collective-permute-done | bytes 1048608 | tf_op jit(solution)/shard_map/ppermute | solution.py:16
  590.4 0.8 maximum_bitcast_fusion
  (103 shorter events, 3.8 us)
Async XLA Ops:
  7.2 65.2 %all-gather.5.cloned.1.call-start = ((), (), s32[]{:S(2)}) async-start(), calls=%async_computation | async-start | bytes 1179648 | tf_op jit(solution)/shard_map/all_gather | solution.py:105
  7.9 124.4 %all-gather.7.cloned.1.call-start = ((), (), s32[]{:S(2)}) async-start(), calls=%async_computation.1 | async-start | bytes 1179648 | tf_op jit(solution)/shard_map/all_gather | solution.py:106
  8.6 248.6 %all-reduce.4.cloned.1.call-start = ((), (), s32[]{:S(2)}) async-start(), calls=%async_computation.4 | async-start | bytes 2097152 | tf_op jit(solution)/shard_map/psum | solution.py:124
  9.4 125.0 %copy-start.11 = (f32[1,4096]{1,0:T(1,128)}, f32[1,4096]{1,0:T(1,128)S(1)}, u32[]{:S(2)}) copy-start(f32[1,4096]{1,0:T(1,128)S(1)} %mul.408) | copy-start | bytes 49156
  11.3 6.5 %copy-start.31 = (s32[34]{0:T(128)S(1)}, s32[34]{0:T(128)}, u32[]{:S(2)}) copy-start(s32[34]{0:T(128)} %param.21) | copy-start | bytes 412
  11.3 13.6 %copy-start.8 = (bf16[1,3,512,128]{3,2,1,0:T(8,128)(2,1)S(1)}, bf16[1,3,512,128]{3,2,1,0:T(8,128)(2,1)}, u32[]{:S(2)}) copy-start(bf16[1,3,512,128]{3,2,1,0:T(8,128)(2,1)} %param.19) | copy-start | bytes 1179652
  18.4 5.1 copy-start.25
  19.1 4.5 copy-start.32
  20.4 3.1 copy-start.27
  20.4 3.1 copy-start.29
  23.6 110.9 %copy-start.4 = (bf16[1,4096,2,128]{3,2,1,0:T(2,128)(2,1)S(1)}, bf16[1,4096,2,128]{3,2,1,0:T(2,128)(2,1)}, u32[]{:S(2)}) copy-start(bf16[1,4096,2,128]{3,2,1,0:T(2,128)(2,1)} %param.17) | copy-start | bytes 6291460
  132.3 2.2 copy-start.7
  134.4 14.9 %copy-start.6 = (bf16[1,128,4096]{2,1,0:T(8,128)(2,1)}, bf16[1,128,4096]{2,1,0:T(8,128)(2,1)S(1)}, u32[]{:S(2)}) copy-start(bf16[1,128,4096]{2,1,0:T(8,128)(2,1)S(1)} %get-tuple-element.9) | copy-start | bytes 3145732
  134.4 0.9 copy-start.33
  139.3 4.0 copy-start.17
  139.3 4.0 copy-start.18
  139.3 4.0 copy-start.10
  139.4 4.0 copy-start.23
  143.3 0.9 copy-start.20
  144.2 2.2 copy-start
  148.1 183.6 %all-gather.9.cloned.1.call-start = ((), (), s32[]{:S(2)}) async-start(), calls=%async_computation.2 | async-start | bytes 2359296 | tf_op jit(solution)/shard_map/all_gather | solution.py:107
  148.7 258.2 %all-gather.11.cloned.1.call-start = ((), (), s32[]{:S(2)}) async-start(), calls=%async_computation.3 | async-start | bytes 2359296 | tf_op jit(solution)/shard_map/all_gather | solution.py:108
  149.3 422.6 %all-reduce.6.cloned.1.call-start = ((), (), s32[]{:S(2)}) async-start(), calls=%async_computation.5 | async-start | bytes 4194304 | tf_op jit(solution)/shard_map/psum | solution.py:124
  149.3 110.8 %collective-permute-start = (bf16[128,4096]{1,0:T(8,128)(2,1)S(1)}, bf16[128,4096]{1,0:T(8,128)(2,1)}, u32[]{:S(2)}, u32[]{:S(2)}) collective-permute-start(bf16[128,4096]{1,0:T(8,128)(2,1)S(1)} %bitcast.174), channel_id=1, source_target_pairs={{0,8},{8,16},{16,24},{24,32},{32,40},{40,48},{48,56},{56,64},{64,7... | collective-permute-start | bytes 3145736 | tf_op jit(solution)/shard_map/ppermute | solution.py:16
  257.3 149.6 %collective-permute-start.1 = (bf16[128,4096]{1,0:T(8,128)(2,1)}, bf16[128,4096]{1,0:T(8,128)(2,1)}, u32[]{:S(2)}, u32[]{:S(2)}) collective-permute-start(bf16[128,4096]{1,0:T(8,128)(2,1)} %all-reduce.4.cloned.1.call-done), channel_id=1, source_target_pairs={{0,8},{8,16},{16,24},{24,32},{32,40},{40,48},{48,56},{56,64},{64,7... | collective-permute-start | bytes 3145736 | tf_op jit(solution)/shard_map/ppermute | solution.py:16
  406.9 5.1 copy-start.12
  409.9 18.5 %collective-permute-start.2 = (bf16[128,4096]{1,0:T(8,128)(2,1)}, bf16[128,4096]{1,0:T(8,128)(2,1)}, u32[]{:S(2)}, u32[]{:S(2)}) collective-permute-start(bf16[128,4096]{1,0:T(8,128)(2,1)} %fusion.7), channel_id=1, source_target_pairs={{0,8},{8,16},{16,24},{24,32},{32,40},{40,48},{48,56},{56,64},{64,7... | collective-permute-start | bytes 3145736 | tf_op jit(solution)/shard_map/ppermute | solution.py:16
  412.6 0.7 copy-start.24
  414.3 3.7 copy-start.15
  414.3 3.7 copy-start.16
  414.3 14.1 %copy-start.3 = (bf16[2,128,4096]{2,1,0:T(8,128)(2,1)S(1)}, bf16[2,128,4096]{2,1,0:T(8,128)(2,1)}, u32[]{:S(2)}) copy-start(bf16[2,128,4096]{2,1,0:T(8,128)(2,1)} %all-gather.9.cloned.1.call-done) | copy-start | bytes 6291460
  418.1 12.0 %copy-start.2 = (bf16[512,4096]{1,0:T(8,128)(2,1)S(1)}, bf16[512,4096]{1,0:T(8,128)(2,1)}, u32[]{:S(2)}) copy-start(bf16[512,4096]{1,0:T(8,128)(2,1)} %copy.55) | copy-start | bytes 12582916
  430.1 1.6 copy-start.5
  431.7 0.7 copy-start.26
  431.7 0.7 copy-start.28
  431.7 0.8 copy-start.30
  431.7 1.5 copy-start.9
  431.7 1.5 copy-start.22
  433.8 2.2 copy-start.1
  436.0 1.7 copy-start.13
  436.0 1.7 copy-start.14
  436.0 1.8 copy-start.21
  437.7 0.9 copy-start.19
  571.9 18.4 %collective-permute-start.3 = (bf16[128,4096]{1,0:T(8,128)(2,1)}, bf16[128,4096]{1,0:T(8,128)(2,1)S(1)}, u32[]{:S(2)}, u32[]{:S(2)}) collective-permute-start(bf16[128,4096]{1,0:T(8,128)(2,1)} %get-tuple-element.2), channel_id=1, source_target_pairs={{0,8},{8,16},{16,24},{24,32},{32,40},{40,48},{48,56},{56,64},{64,7... | collective-permute-start | bytes 3145736 | tf_op jit(solution)/shard_map/ppermute | solution.py:16
Sparse Core Ops, SparseCore 0:
  10.5 61.8 all-gather.4
  74.9 57.3 all-gather.6
  148.2 109.0 all-reduce.3
  259.6 72.0 all-gather.8
  334.0 72.7 all-gather.10
  440.9 130.9 all-reduce.5
where the time goes:
time: 599 us; the launch traced here: 598 us
  waiting for transfers between devices  511 us (85%)
  local copies, waits for them, and re-layouts  26.3 us (4%)
  other arithmetic  19.6 us (3%)
  matrix products  18.2 us (3%)
  between operations  14.8 us (2%)
  starting transfers between devices  8.06 us (1%)
    psum x2, waiting for transfers between devices, body(): block_total = lax.psum(summand.astype(jnp.bfloat16), 'tensor')  235 us
    all_gather x1, waiting for transfers between devices, body(): lax.all_gather(incoming_last, 'tensor', axis=2, tiled=True)  73.1 us
    all_gather x1, waiting for transfers between devices, body(): lax.all_gather(incoming_two, 'tensor', axis=2, tiled=True)  71.6 us
    all_gather x1, waiting for transfers between devices, body(): lax.all_gather(block_last, 'tensor', axis=2, tiled=True)  59.9 us
    all_gather x1, waiting for transfers between devices, body(): lax.all_gather(stream_two, 'tensor', axis=2, tiled=True)  46.7 us
    ppermute x4, waiting for transfers between devices, from_behind(): lax.ppermute(value, axis, [(source, source + steps) for source in range(l...  22 us
  transfers between devices with their start and end apart: 10, of which 8 were waited for; matrix products, arithmetic and copies ran while one was open for 5% of the time, Pallas kernels for 0%

commit v1 on v0

v1 whole, which is shorter than its diff:
```python
import functools

import jax
import jax.numpy as jnp
from jax import lax
from jax.experimental import pallas as pl
from jax.experimental.pallas import tpu as pltpu
from jax.sharding import PartitionSpec as P

HD = 128
rope_base = 500000.0
norm_eps = 1e-05
bf16 = jnp.bfloat16
f32 = jnp.float32
Y = 4


def move(value, sections, tensors, target):
    pairs = []
    for s in range(sections):
        for t in range(tensors):
            s2, t2 = target(s, t)
            pairs.append((s * tensors + t, (s2 % sections) * tensors + t2))
    return lax.ppermute(value, ("section", "tensor"), pairs)


def y_shift(k):
    return lambda s, t: (s, (t & ~3) | ((t + k) & 3))


def hop(n, other=False):
    return lambda s, t: (s + n, t ^ 4 if other else t)


def rope_tables(length, rows):
    half = HD // 2
    index = jnp.arange(half).astype(f32)
    freqs = jnp.exp(-jnp.log(rope_base) * 2.0 * index / HD)
    positions = length + jnp.arange(rows)
    angles = positions.astype(f32)[:, None] * freqs[None, :]
    c, s = jnp.cos(angles), jnp.sin(angles)
    return jnp.concatenate([c, c], 1), jnp.concatenate([-s, s], 1)


def attend_kernel(
    scalars, g0, g1, g2, g3, gain, wq, wkv, wo, kc, vc, cos, sin, o0, o1, o2, o3, normed, att
):
    length, high, low = scalars[0], scalars[1], scalars[2]
    rows, width = g0.shape[1], g0.shape[2]
    pieces = (g0, g1, g2, g3)

    def chunk(slot, y):
        return ((high ^ slot) * Y + (y & (Y - 1))) * width

    total = jnp.zeros((rows, width), f32)
    for ref in pieces:
        for slot in range(2):
            v = ref[slot].astype(f32)
            total = total + v * v
    mean = jnp.sum(total, axis=-1, keepdims=True) / (2 * Y * width)
    inverse = lax.rsqrt(mean + norm_eps)
    for k, ref in enumerate(pieces):
        for slot in range(2):
            at = pl.ds(pl.multiple_of(chunk(slot, low - k + Y), width), width)
            scaled = ref[slot].astype(f32) * inverse * gain[:, at].astype(f32)
            normed[:, at] = scaled.astype(bf16)
    n = normed[...]
    q = jnp.dot(n, wq[...], preferred_element_type=f32)
    kv = jnp.dot(n, wkv[...], preferred_element_type=f32)
    cos_t, sin_t = cos[...], sin[...]

    def rotate(v):
        return (v * cos_t + pltpu.roll(v, HD // 2, 1) * sin_t).astype(bf16)

    heads = q.shape[1] // HD
    qs = jnp.concatenate([rotate(q[:, h * HD : (h + 1) * HD]) for h in range(heads)], 0)
    nk = rotate(kv[:, :HD])
    nv = kv[:, HD:].astype(bf16)
    contract = (((1,), (1,)), ((), ()))
    scale = HD ** (-0.5)
    s1 = lax.dot_general(qs, kc[...], contract, preferred_element_type=f32) * scale
    s2 = lax.dot_general(qs, nk, contract, preferred_element_type=f32) * scale
    seen1 = lax.broadcasted_iota(jnp.int32, s1.shape, 1) < length
    row = lax.broadcasted_iota(jnp.int32, s2.shape, 0) & (rows - 1)
    seen2 = lax.broadcasted_iota(jnp.int32, s2.shape, 1) <= row
    s1 = jnp.where(seen1, s1, -1e30)
    s2 = jnp.where(seen2, s2, -1e30)
    top = jnp.maximum(
        jnp.max(s1, axis=-1, keepdims=True), jnp.max(s2, axis=-1, keepdims=True)
    )
    e1 = jnp.where(seen1, jnp.exp(s1 - top), 0.0)
    e2 = jnp.where(seen2, jnp.exp(s2 - top), 0.0)
    norm = jnp.sum(e1, axis=-1, keepdims=True) + jnp.sum(e2, axis=-1, keepdims=True)
    p1 = (e1 / norm).astype(bf16)
    p2 = (e2 / norm).astype(bf16)
    out = jnp.dot(p1, vc[...], preferred_element_type=f32) + jnp.dot(
        p2, nv, preferred_element_type=f32
    )
    out = out.astype(bf16)
    for h in range(heads):
        att[:, h * HD : (h + 1) * HD] = out[h * rows : (h + 1) * rows]
    a = att[...]
    for k, ref in enumerate((o0, o1, o2, o3)):
        for slot in (1, 0):
            at = pl.ds(pl.multiple_of(chunk(slot, low + k), width), width)
            ref[slot] = jnp.dot(a, wo[:, at], preferred_element_type=f32).astype(bf16)


def attend(scalars, gathered, gain, wq, wkv, wo, kc, vc, cos, sin):
    _, rows, width = gathered[0].shape
    vmem = pl.BlockSpec(memory_space=pltpu.VMEM)
    cols = wq.shape[0]
    flops = 2 * rows * cols * (2 * wq.shape[1] + wkv.shape[1])
    return pl.pallas_call(
        attend_kernel,
        out_shape=[jax.ShapeDtypeStruct((2, rows, width), bf16)] * Y,
        in_specs=[pl.BlockSpec(memory_space=pltpu.SMEM)] + [vmem] * 12,
        out_specs=[vmem] * Y,
        scratch_shapes=[
            pltpu.VMEM((rows, cols), bf16),
            pltpu.VMEM((rows, wq.shape[1]), bf16),
        ],
        compiler_params=pltpu.CompilerParams(vmem_limit_bytes=40 * 1024 * 1024),
        cost_estimate=pl.CostEstimate(
            flops=flops, bytes_accessed=24 * 1024 * 1024, transcendentals=512 * 640
        ),
    )(scalars, *gathered, gain, wq, wkv, wo, kc, vc, cos, sin)


def body(
    stream_two, block_last, incoming_two, incoming_last, norm_gain,
    w_query, w_keyval, w_out, keys_cache, values_cache, cached_len,
):
    sections = lax.axis_size("section")
    tensors = lax.axis_size("tensor")
    sid = lax.axis_index("section")
    tid = lax.axis_index("tensor")
    rows = stream_two.shape[1]
    send = functools.partial(lambda v, f: move(v, sections, tensors, f))
    last = sections - 1

    def gather(pair):
        return [pair] + [send(pair, y_shift(k)) for k in range(1, Y)]

    def scatter(parts):
        got = [parts[0]] + [send(parts[k], y_shift(k)) for k in range(1, Y)]
        mine = sum(g[0].astype(f32) for g in got)
        theirs = sum(g[1].astype(f32) for g in got).astype(bf16)
        return (mine + send(theirs, hop(0, True)).astype(f32)).astype(bf16)

    def add(a, b):
        return (a.astype(f32) + b.astype(f32)).astype(bf16)

    wq, wo = w_query[0], w_out[0]
    wkv = w_keyval[0].reshape(w_keyval.shape[1], -1)

    def block(tick, gathered):
        length = cached_len[last - sid + tick]
        scalars = jnp.stack([length, tid // Y, tid % Y]).astype(jnp.int32)
        cos, sin = rope_tables(length, rows)
        return attend(
            scalars, gathered, norm_gain, wq, wkv, wo,
            keys_cache[0, tick], values_cache[0, tick], cos, sin,
        )

    x0 = stream_two[0]
    s0 = add(x0, block_last[0])
    pair0 = jnp.stack([x0, send(x0, hop(0, True))])
    parts0 = block(0, gather(pair0))

    out1 = jnp.where(sid == last, incoming_two[0], s0)
    a1 = send(out1, hop(1))
    pair1 = jnp.stack([a1, send(out1, hop(1, True))])
    parts1 = block(1, gather(pair1))
    base = send(pair1, hop(1))
    base = jnp.where(sid == 0, jnp.zeros_like(base), base)

    b0 = scatter(parts0)
    out2 = jnp.where(
        sid == last - 1, incoming_two[1], jnp.where(sid == last, incoming_last[0], b0)
    )
    pair2 = add(base, jnp.stack([send(out2, hop(2)), send(out2, hop(2, True))]))
    parts2 = block(2, gather(pair2))

    b1 = scatter(parts1)
    t1 = add(a1, send(jnp.where(sid == last, incoming_last[0], b0), hop(1)))
    t2 = add(pair2[0], send(jnp.where(sid == last, incoming_last[1], b1), hop(1)))
    b2 = scatter(parts2)
    return jnp.stack([s0, t1, t2])[None], jnp.stack([b0, b1, b2])[None]


def solution(mesh):
    placed = (
        P("section", None, "tensor"),
        P("section", None, "tensor"),
        P(None, None, "tensor"),
        P(None, None, "tensor"),
        P("section", None),
        P("section", None, "tensor"),
        P("section", None, None, "tensor"),
        P("section", "tensor", None),
        P("section", None, None, "tensor"),
        P("section", None, None, "tensor"),
        P(),
    )
    out = P("section", None, None, "tensor")
    return jax.shard_map(
        body, mesh=mesh, in_specs=placed, out_specs=(out, out), check_vma=False
    )
```

time: 599 us -> 160 us (0.27)
  the two profiles are of different devices: /device:TPU:64 before, /device:TPU:16 now
where the time goes in v1:
time: 160 us; the launch traced here: 158 us
  waiting for transfers between devices  72.3 us (45%)
  starting transfers between devices  46.2 us (29%)
  other arithmetic  14.3 us (9%)
  Pallas kernels  12.9 us (8%)
  local copies, waits for them, and re-layouts  11.2 us (7%)
    ppermute x29, waiting for transfers between devices, move(): return lax.ppermute(value, ('section', 'tensor'), pairs)  72.3 us
    ppermute x29, starting transfers between devices, move(): return lax.ppermute(value, ('section', 'tensor'), pairs)  46.2 us
    pallas_call x3, Pallas kernels, attend(): pl.pallas_call(attend_kernel, out_shape=[jax.ShapeDtypeStruct((2, rows, w...  12.9 us
    unnamed x49, local copies, waits for them, and re-layouts  8.51 us
  transfers between devices with their start and end apart: 29, of which 16 were waited for; matrix products, arithmetic and copies ran while one was open for 11% of the time, Pallas kernels for 8%

profile of v1, /device:TPU:16, one launch (start us, length us, event | category | flops | bytes accessed | tf_op | source)
XLA Modules:
  0.0 157.8 jit_solution(679116279063259919)
XLA Ops:
  0.6 1.1 fusion.13
  1.7 6.7 %collective-permute-start.10 = (bf16[128,512]{1,0:T(8,128)(2,1)S(1)}, bf16[128,512]{1,0:T(8,128)(2,1)S(1)}, u32[]{:S(2)}, u32[]{:S(2)}) collective-permute-start(bf16[128,512]{1,0:T(8,128)(2,1)S(1)} %fusion.13), channel_id=1, source_target_pairs={{0,12},{1,13},{2,14},{3,15},{4,8},{5,9},{6,10},{7,11},{8,20},{9,21... | collective-permute-start | bytes 393224 | tf_op jit(solution)/shard_map/ppermute | solution.py:24
  8.4 1.6 %collective-permute-start = (bf16[128,512]{1,0:T(8,128)(2,1)S(1)}, bf16[128,512]{1,0:T(8,128)(2,1)S(1)}, u32[]{:S(2)}, u32[]{:S(2)}) collective-permute-start(bf16[128,512]{1,0:T(8,128)(2,1)S(1)} %fusion.13), channel_id=1, source_target_pairs={{0,8},{1,9},{2,10},{3,11},{4,12},{5,13},{6,14},{7,15},{8,16},{9,17... | collective-permute-start | bytes 393224 | tf_op jit(solution)/shard_map/ppermute | solution.py:24
  10.1 1.4 fusion.19
  11.4 0.6 add_convert_fusion.5
  12.1 0.6 add_convert_fusion.6
  12.7 0.6 add_convert_fusion.7
  13.3 1.3 slice_bitcast_fusion.1
  14.6 1.4 fusion.16
  15.9 8.3 %collective-permute-done.1 = bf16[128,512]{1,0:T(8,128)(2,1)S(1)} collective-permute-done((bf16[128,512]{1,0:T(8,128)(2,1)}, bf16[128,512]{1,0:T(8,128)(2,1)S(1)}, u32[]{:S(2)}, u32[]{:S(2)}) %collective-permute-start.1) | collective-permute-done | bytes 131104 | tf_op jit(solution)/shard_map/ppermute | solution.py:24
  24.2 0.9 pad_maximum_fusion.g0
  25.1 1.4 collective-permute-start.2
  26.5 0.6 collective-permute-start.3
  27.1 1.1 collective-permute-start.4
  28.2 0.1 pad_maximum_fusion.2
  28.4 1.2 collective-permute-start.14
  29.6 0.7 add_add_fusion.scalars
  30.3 1.9 %copy.15 = bf16[512,8,2,128]{3,1,2,0:T(8,128)(2,1)S(1)} copy(bf16[512,8,2,128]{3,2,1,0:T(2,128)(2,1)} %bitcast.96) | data formatting | bytes 4194304
  32.2 3.2 %collective-permute-start.15 = (bf16[2,128,512]{2,1,0:T(8,128)(2,1)S(1)}, bf16[2,128,512]{2,1,0:T(8,128)(2,1)S(1)}, u32[]{:S(2)}, u32[]{:S(2)}) collective-permute-start(bf16[2,128,512]{2,1,0:T(8,128)(2,1)S(1)} %pad_maximum_fusion.1.g0), channel_id=1, source_target_pairs={{0,2},{1,3},{2,0},{3,1},{4,6},{5,7},{6,4},{7,5},{8,10},{9,11},{10,... | collective-permute-start | bytes 786440 | tf_op jit(solution)/shard_map/ppermute | solution.py:24
  35.4 4.7 %collective-permute-done.2.g1 = bf16[2,128,512]{2,1,0:T(8,128)(2,1)} collective-permute-done((bf16[2,128,512]{2,1,0:T(8,128)(2,1)S(1)}, bf16[2,128,512]{2,1,0:T(8,128)(2,1)}, u32[]{:S(2)}, u32[]{:S(2)}) %collective-permute-start.2) | collective-permute-done | bytes 262176 | tf_op jit(solution)/shard_map/ppermute | solution.py:24
  40.1 2.1 %collective-permute-done.4.g3 = bf16[2,128,512]{2,1,0:T(8,128)(2,1)} collective-permute-done((bf16[2,128,512]{2,1,0:T(8,128)(2,1)S(1)}, bf16[2,128,512]{2,1,0:T(8,128)(2,1)}, u32[]{:S(2)}, u32[]{:S(2)}) %collective-permute-start.4) | collective-permute-done | bytes 262176 | tf_op jit(solution)/shard_map/ppermute | solution.py:24
  42.2 2.2 %copy-done.2 = bf16[1,512,4096]{2,1,0:T(8,128)(2,1)S(1)} copy-done((bf16[1,512,4096]{2,1,0:T(8,128)(2,1)S(1)}, bf16[1,512,4096]{2,1,0:T(8,128)(2,1)}, u32[]{:S(2)}) %copy-start.2) | copy-done | bytes 4194328
  44.4 4.8 %shard_map.122 = (bf16[2,128,512]{2,1,0:T(8,128)(2,1)S(1)}, bf16[2,128,512]{2,1,0:T(8,128)(2,1)S(1)}, bf16[2,128,512]{2,1,0:T(8,128)(2,1)S(1)}, bf16[2,128,512]{2,1,0:T(8,128)(2,1)S(1)}) custom-call(s32[3]{0:T(128)S(1)} %add_add_fusion.scalars, bf16[2,128,512]{2,1,0:T(8,128)(2,1)S(1)} %pad_maximum_fusion.g0, bf16[2,128,512]{2,1,0:T(8,128)(2,1)} %collective-permute-done.2.g1, ...), custom_call_target="tpu_custom_call" | custom-call | flops 1342177280 | bytes 25165824 | tf_op jit(solution)/shard_map/pallas_call | solution.py:114
  49.2 1.4 collective-permute-start.7
  50.7 0.6 add_add_fusion.1.scalars
  51.3 4.2 %collective-permute-start.6 = (bf16[2,128,512]{2,1,0:T(8,128)(2,1)S(1)}, bf16[2,128,512]{2,1,0:T(8,128)(2,1)S(1)}, u32[]{:S(2)}, u32[]{:S(2)}) collective-permute-start(bf16[2,128,512]{2,1,0:T(8,128)(2,1)S(1)} %get-tuple-element.16), channel_id=1, source_target_pairs={{0,2},{1,3},{2,0},{3,1},{4,6},{5,7},{6,4},{7,5},{8,10},{9,11},{10,... | collective-permute-start | bytes 786440 | tf_op jit(solution)/shard_map/ppermute | solution.py:24
  55.6 0.1 pad_maximum_fusion.4
  55.7 4.1 %shard_map.123 = (bf16[2,128,512]{2,1,0:T(8,128)(2,1)S(1)}, bf16[2,128,512]{2,1,0:T(8,128)(2,1)S(1)}, bf16[2,128,512]{2,1,0:T(8,128)(2,1)S(1)}, bf16[2,128,512]{2,1,0:T(8,128)(2,1)S(1)}) custom-call(s32[3]{0:T(128)S(1)} %add_add_fusion.1.scalars, bf16[2,128,512]{2,1,0:T(8,128)(2,1)S(1)} %pad_maximum_fusion.1.g0, ...), custom_call_target="tpu_custom_call" | custom-call | flops 1342177280 | bytes 25165824 | tf_op jit(solution)/shard_map/pallas_call | solution.py:114
  59.8 2.1 %collective-permute-start.19 = (bf16[2,128,512]{2,1,0:T(8,128)(2,1)S(1)}, bf16[2,128,512]{2,1,0:T(8,128)(2,1)S(1)}, u32[]{:S(2)}, u32[]{:S(2)}) collective-permute-start(bf16[2,128,512]{2,1,0:T(8,128)(2,1)S(1)} %get-tuple-element.21), channel_id=1, source_target_pairs={{0,3},{1,0},{2,1},{3,2},{4,7},{5,4},{6,5},{7,6},{8,11},{9,8},{10,9... | collective-permute-start | bytes 786440 | tf_op jit(solution)/shard_map/ppermute | solution.py:24
  61.9 1.3 collective-permute-start.18
  63.2 0.9 collective-permute-start.17
  64.1 7.0 %collective-permute-done.5 = bf16[2,128,512]{2,1,0:T(8,128)(2,1)S(1)} collective-permute-done((bf16[2,128,512]{2,1,0:T(8,128)(2,1)S(1)}, bf16[2,128,512]{2,1,0:T(8,128)(2,1)S(1)}, u32[]{:S(2)}, u32[]{:S(2)}) %collective-permute-start.5) | collective-permute-done | bytes 262176 | tf_op jit(solution)/shard_map/ppermute | solution.py:24
  71.1 0.8 fusion.7
  71.9 0.4 collective-permute-done.18
  72.3 2.7 %collective-permute-done.17 = bf16[2,128,512]{2,1,0:T(8,128)(2,1)S(1)} collective-permute-done((bf16[2,128,512]{2,1,0:T(8,128)(2,1)S(1)}, bf16[2,128,512]{2,1,0:T(8,128)(2,1)S(1)}, u32[]{:S(2)}, u32[]{:S(2)}) %collective-permute-start.17) | collective-permute-done | bytes 262176 | tf_op jit(solution)/shard_map/ppermute | solution.py:24
  74.9 0.7 fusion.9
  75.7 3.3 %collective-permute-start.20 = (bf16[128,512]{1,0:T(8,128)(2,1)}, bf16[128,512]{1,0:T(8,128)(2,1)}, u32[]{:S(2)}, u32[]{:S(2)}) collective-permute-start(bf16[128,512]{1,0:T(8,128)(2,1)} %fusion.9), channel_id=1, source_target_pairs={{0,4},{1,5},{2,6},{3,7},{4,0},{5,1},{6,2},{7,3},{8,12},{9,13},{10,... | collective-permute-start | bytes 393224 | tf_op jit(solution)/shard_map/ppermute | solution.py:24
  79.0 3.2 %collective-permute-done.8 = bf16[128,512]{1,0:T(8,128)(2,1)} collective-permute-done((bf16[128,512]{1,0:T(8,128)(2,1)}, bf16[128,512]{1,0:T(8,128)(2,1)}, u32[]{:S(2)}, u32[]{:S(2)}) %collective-permute-start.8) | collective-permute-done | bytes 131104 | tf_op jit(solution)/shard_map/ppermute | solution.py:24
  82.2 4.6 %collective-permute-done.20 = bf16[128,512]{1,0:T(8,128)(2,1)} collective-permute-done((bf16[128,512]{1,0:T(8,128)(2,1)}, bf16[128,512]{1,0:T(8,128)(2,1)}, u32[]{:S(2)}, u32[]{:S(2)}) %collective-permute-start.20) | collective-permute-done | bytes 131104 | tf_op jit(solution)/shard_map/ppermute | solution.py:24
  86.7 2.3 %bitcast_select_fusion.1 = (bf16[128,512]{1,0:T(8,128)(2,1)}, bf16[128,512]{1,0:T(8,128)(2,1)}, bf16[128,512]{1,0:T(8,128)(2,1)S(1)}, bf16[128,512]{1,0:T(8,128)(2,1)}, bf16[128,512]{1,0:T(8,128)(2,1)S(1)}) fusion(bf16[2,128,512]{2,1,0:T(8,128)(2,1)S(1)} %copy-done.11, pred[]{:T(512)S(6)} %eq.18, bf16[2,128,512]{2,1,0:T(8,128)(2,1)} %param.14, pred[]{:T(512)S(6)} %eq.16, ...), kind=kLoop, calls=%fused_computation.32 | loop fusion | flops 1507328 | bytes 2359298 | tf_op jit(solution)/shard_map/jit(_where)/select_n | solution.py:179
  89.1 3.9 %collective-permute-start.13 = (bf16[128,512]{1,0:T(8,128)(2,1)}, bf16[128,512]{1,0:T(8,128)(2,1)S(1)}, u32[]{:S(2)}, u32[]{:S(2)}) collective-permute-start(bf16[128,512]{1,0:T(8,128)(2,1)} %get-tuple-element.26), channel_id=1, source_target_pairs={{0,20},{1,21},{2,22},{3,23},{4,16},{5,17},{6,18},{7,19},{8,28},{9,... | collective-permute-start | bytes 393224 | tf_op jit(solution)/shard_map/ppermute | solution.py:24
  93.0 1.5 collective-permute-start.12
  94.5 3.1 %collective-permute-done.13 = bf16[128,512]{1,0:T(8,128)(2,1)S(1)} collective-permute-done((bf16[128,512]{1,0:T(8,128)(2,1)}, bf16[128,512]{1,0:T(8,128)(2,1)S(1)}, u32[]{:S(2)}, u32[]{:S(2)}) %collective-permute-start.13) | collective-permute-done | bytes 131104 | tf_op jit(solution)/shard_map/ppermute | solution.py:24
  97.7 8.1 %collective-permute-done.12 = bf16[128,512]{1,0:T(8,128)(2,1)S(1)} collective-permute-done((bf16[128,512]{1,0:T(8,128)(2,1)}, bf16[128,512]{1,0:T(8,128)(2,1)S(1)}, u32[]{:S(2)}, u32[]{:S(2)}) %collective-permute-start.12) | collective-permute-done | bytes 131104 | tf_op jit(solution)/shard_map/ppermute | solution.py:24
  106.0 3.5 %collective-permute-start.23 = (bf16[2,128,512]{2,1,0:T(8,128)(2,1)S(1)}, bf16[2,128,512]{2,1,0:T(8,128)(2,1)S(1)}, u32[]{:S(2)}, u32[]{:S(2)}) collective-permute-start(bf16[2,128,512]{2,1,0:T(8,128)(2,1)S(1)} %add_convert_fusion.g0), channel_id=1, source_target_pairs={{0,2},{1,3},{2,0},{3,1},{4,6},{5,7},{6,4},{7,5},{8,10},{9,11},{10,... | collective-permute-start | bytes 786440 | tf_op jit(solution)/shard_map/ppermute | solution.py:24
  109.5 2.5 %collective-permute-start.24 = (bf16[2,128,512]{2,1,0:T(8,128)(2,1)S(1)}, bf16[2,128,512]{2,1,0:T(8,128)(2,1)S(1)}, u32[]{:S(2)}, u32[]{:S(2)}) collective-permute-start(bf16[2,128,512]{2,1,0:T(8,128)(2,1)S(1)} %add_convert_fusion.g0), channel_id=1, source_target_pairs={{0,3},{1,0},{2,1},{3,2},{4,7},{5,4},{6,5},{7,6},{8,11},{9,8},{10,9... | collective-permute-start | bytes 786440 | tf_op jit(solution)/shard_map/ppermute | solution.py:24
  112.0 0.7 add_add_fusion.2.scalars
  112.7 0.9 pad_maximum_fusion.6
  113.8 7.7 %collective-permute-done.23.g2 = bf16[2,128,512]{2,1,0:T(8,128)(2,1)S(1)} collective-permute-done((bf16[2,128,512]{2,1,0:T(8,128)(2,1)S(1)}, bf16[2,128,512]{2,1,0:T(8,128)(2,1)S(1)}, u32[]{:S(2)}, u32[]{:S(2)}) %collective-permute-start.23) | collective-permute-done | bytes 262176 | tf_op jit(solution)/shard_map/ppermute | solution.py:24
  121.5 0.9 collective-permute-done.24.g3
  122.4 2.2 %copy-done.1 = bf16[1,4096,512]{2,1,0:T(8,128)(2,1)S(1)} copy-done((bf16[1,4096,512]{2,1,0:T(8,128)(2,1)S(1)}, bf16[1,4096,512]{2,1,0:T(8,128)(2,1)}, u32[]{:S(2)}) %copy-start.1) | copy-done | bytes 4194328
  124.6 2.2 %copy-done.4 = bf16[1,512,4096]{2,1,0:T(8,128)(2,1)S(1)} copy-done((bf16[1,512,4096]{2,1,0:T(8,128)(2,1)S(1)}, bf16[1,512,4096]{2,1,0:T(8,128)(2,1)}, u32[]{:S(2)}) %copy-start.4) | copy-done | bytes 4194328
  126.8 4.1 %shard_map.124 = (bf16[2,128,512]{2,1,0:T(8,128)(2,1)S(1)}, bf16[2,128,512]{2,1,0:T(8,128)(2,1)S(1)}, bf16[2,128,512]{2,1,0:T(8,128)(2,1)S(1)}, bf16[2,128,512]{2,1,0:T(8,128)(2,1)S(1)}) custom-call(s32[3]{0:T(128)S(1)} %add_add_fusion.2.scalars, bf16[2,128,512]{2,1,0:T(8,128)(2,1)S(1)} %add_convert_fusion.g0, ...), custom_call_target="tpu_custom_call" | custom-call | flops 1342177280 | bytes 25165824 | tf_op jit(solution)/shard_map/pallas_call | solution.py:114
  130.9 1.5 collective-permute-start.27
  132.4 3.6 %collective-permute-start.26 = (bf16[2,128,512]{2,1,0:T(8,128)(2,1)S(1)}, bf16[2,128,512]{2,1,0:T(8,128)(2,1)S(1)}, u32[]{:S(2)}, u32[]{:S(2)}) collective-permute-start(bf16[2,128,512]{2,1,0:T(8,128)(2,1)S(1)} %get-tuple-element.24), channel_id=1, source_target_pairs={{0,2},{1,3},{2,0},{3,1},{4,6},{5,7},{6,4},{7,5},{8,10},{9,11},{10,... | collective-permute-start | bytes 786440 | tf_op jit(solution)/shard_map/ppermute | solution.py:24
  136.0 0.3 collective-permute-start.25
  136.5 4.6 %collective-permute-done.27 = bf16[2,128,512]{2,1,0:T(8,128)(2,1)S(1)} collective-permute-done((bf16[2,128,512]{2,1,0:T(8,128)(2,1)S(1)}, bf16[2,128,512]{2,1,0:T(8,128)(2,1)S(1)}, u32[]{:S(2)}, u32[]{:S(2)}) %collective-permute-start.27) | collective-permute-done | bytes 262176 | tf_op jit(solution)/shard_map/ppermute | solution.py:24
  141.0 2.1 %collective-permute-done.26 = bf16[2,128,512]{2,1,0:T(8,128)(2,1)S(1)} collective-permute-done((bf16[2,128,512]{2,1,0:T(8,128)(2,1)S(1)}, bf16[2,128,512]{2,1,0:T(8,128)(2,1)S(1)}, u32[]{:S(2)}, u32[]{:S(2)}) %collective-permute-start.26) | collective-permute-done | bytes 262176 | tf_op jit(solution)/shard_map/ppermute | solution.py:24
  143.2 4.3 %collective-permute-done.25 = bf16[2,128,512]{2,1,0:T(8,128)(2,1)S(1)} collective-permute-done((bf16[2,128,512]{2,1,0:T(8,128)(2,1)S(1)}, bf16[2,128,512]{2,1,0:T(8,128)(2,1)S(1)}, u32[]{:S(2)}, u32[]{:S(2)}) %collective-permute-start.25) | collective-permute-done | bytes 262176 | tf_op jit(solution)/shard_map/ppermute | solution.py:24
  147.5 0.1 collective-permute-start.28
  147.7 0.8 maximum_bitcast_fusion
  148.5 8.5 %collective-permute-done.28 = bf16[128,512]{1,0:T(8,128)(2,1)S(1)} collective-permute-done((bf16[128,512]{1,0:T(8,128)(2,1)S(1)}, bf16[128,512]{1,0:T(8,128)(2,1)S(1)}, u32[]{:S(2)}, u32[]{:S(2)}) %collective-permute-start.28) | collective-permute-done | bytes 131104 | tf_op jit(solution)/shard_map/ppermute | solution.py:24
  157.0 0.1 fusion.11
  157.0 0.8 maximum_bitcast_fusion.1
  (73 shorter events, 0.7 us)
Async XLA Ops:
  0.6 41.6 %copy-start.6 = (bf16[1,4096]{1,0:T(2,128)(2,1)S(1)}, bf16[1,4096]{1,0:T(2,128)(2,1)}, u32[]{:S(2)}) copy-start(bf16[1,4096]{1,0:T(2,128)(2,1)} %gain.5) | copy-start | bytes 24580
  1.7 26.6 %collective-permute-start.10 = (bf16[128,512]{1,0:T(8,128)(2,1)S(1)}, bf16[128,512]{1,0:T(8,128)(2,1)S(1)}, u32[]{:S(2)}, u32[]{:S(2)}) collective-permute-start(bf16[128,512]{1,0:T(8,128)(2,1)S(1)} %fusion.13), channel_id=1, source_target_pairs={{0,12},{1,13},{2,14},{3,15},{4,8},{5,9},{6,10},{7,11},{8,20},{9,21... | collective-permute-start | bytes 393224 | tf_op jit(solution)/shard_map/ppermute | solution.py:24
  8.4 19.9 %collective-permute-start = (bf16[128,512]{1,0:T(8,128)(2,1)S(1)}, bf16[128,512]{1,0:T(8,128)(2,1)S(1)}, u32[]{:S(2)}, u32[]{:S(2)}) collective-permute-start(bf16[128,512]{1,0:T(8,128)(2,1)S(1)} %fusion.13), channel_id=1, source_target_pairs={{0,8},{1,9},{2,10},{3,11},{4,12},{5,13},{6,14},{7,15},{8,16},{9,17... | collective-permute-start | bytes 393224 | tf_op jit(solution)/shard_map/ppermute | solution.py:24
  10.0 14.1 %collective-permute-start.1 = (bf16[128,512]{1,0:T(8,128)(2,1)}, bf16[128,512]{1,0:T(8,128)(2,1)S(1)}, u32[]{:S(2)}, u32[]{:S(2)}) collective-permute-start(bf16[128,512]{1,0:T(8,128)(2,1)} %bitcast.97), channel_id=1, source_target_pairs={{0,4},{1,5},{2,6},{3,7},{4,0},{5,1},{6,2},{7,3},{8,12},{9,13},{10,... | collective-permute-start | bytes 393224 | tf_op jit(solution)/shard_map/ppermute | solution.py:24
  25.1 15.0 %collective-permute-start.2 = (bf16[2,128,512]{2,1,0:T(8,128)(2,1)S(1)}, bf16[2,128,512]{2,1,0:T(8,128)(2,1)}, u32[]{:S(2)}, u32[]{:S(2)}) collective-permute-start(bf16[2,128,512]{2,1,0:T(8,128)(2,1)S(1)} %pad_maximum_fusion.g0), channel_id=1, source_target_pairs={{0,1},{1,2},{2,3},{3,0},{4,5},{5,6},{6,7},{7,4},{8,9},{9,10},{10,1... | collective-permute-start | bytes 786440 | tf_op jit(solution)/shard_map/ppermute | solution.py:24
  26.5 13.6 %collective-permute-start.3 = (bf16[2,128,512]{2,1,0:T(8,128)(2,1)S(1)}, bf16[2,128,512]{2,1,0:T(8,128)(2,1)}, u32[]{:S(2)}, u32[]{:S(2)}) collective-permute-start(bf16[2,128,512]{2,1,0:T(8,128)(2,1)S(1)} %pad_maximum_fusion.g0), channel_id=1, source_target_pairs={{0,2},{1,3},{2,0},{3,1},{4,6},{5,7},{6,4},{7,5},{8,10},{9,11},{10,... | collective-permute-start | bytes 786440 | tf_op jit(solution)/shard_map/ppermute | solution.py:24
  27.1 15.1 %collective-permute-start.4 = (bf16[2,128,512]{2,1,0:T(8,128)(2,1)S(1)}, bf16[2,128,512]{2,1,0:T(8,128)(2,1)}, u32[]{:S(2)}, u32[]{:S(2)}) collective-permute-start(bf16[2,128,512]{2,1,0:T(8,128)(2,1)S(1)} %pad_maximum_fusion.g0), channel_id=1, source_target_pairs={{0,3},{1,0},{2,1},{3,2},{4,7},{5,4},{6,5},{7,6},{8,11},{9,8},{10,9... | collective-permute-start | bytes 786440 | tf_op jit(solution)/shard_map/ppermute | solution.py:24
  28.3 13.9 %copy-start = (bf16[1,4096,512]{2,1,0:T(8,128)(2,1)S(1)}, bf16[1,4096,512]{2,1,0:T(8,128)(2,1)}, u32[]{:S(2)}) copy-start(bf16[1,4096,512]{2,1,0:T(8,128)(2,1)} %param.16) | copy-start | bytes 12582916
  28.3 2.0 %copy-start.9 = (bf16[128,512]{1,0:T(8,128)(2,1)}, bf16[128,512]{1,0:T(8,128)(2,1)S(1)}, u32[]{:S(2)}) copy-start(bf16[128,512]{1,0:T(8,128)(2,1)S(1)} %collective-permute-done) | copy-start | bytes 393220
  28.4 27.2 %collective-permute-start.14 = (bf16[2,128,512]{2,1,0:T(8,128)(2,1)S(1)}, bf16[2,128,512]{2,1,0:T(8,128)(2,1)S(1)}, u32[]{:S(2)}, u32[]{:S(2)}) collective-permute-start(bf16[2,128,512]{2,1,0:T(8,128)(2,1)S(1)} %pad_maximum_fusion.1.g0), channel_id=1, source_target_pairs={{0,1},{1,2},{2,3},{3,0},{4,5},{5,6},{6,7},{7,4},{8,9},{9,10},{10,1... | collective-permute-start | bytes 786440 | tf_op jit(solution)/shard_map/ppermute | solution.py:24
  32.2 23.5 %collective-permute-start.15 = (bf16[2,128,512]{2,1,0:T(8,128)(2,1)S(1)}, bf16[2,128,512]{2,1,0:T(8,128)(2,1)S(1)}, u32[]{:S(2)}, u32[]{:S(2)}) collective-permute-start(bf16[2,128,512]{2,1,0:T(8,128)(2,1)S(1)} %pad_maximum_fusion.1.g0), channel_id=1, source_target_pairs={{0,2},{1,3},{2,0},{3,1},{4,6},{5,7},{6,4},{7,5},{8,10},{9,11},{10,... | collective-permute-start | bytes 786440 | tf_op jit(solution)/shard_map/ppermute | solution.py:24
  40.1 15.6 %collective-permute-start.16 = (bf16[2,128,512]{2,1,0:T(8,128)(2,1)S(1)}, bf16[2,128,512]{2,1,0:T(8,128)(2,1)S(1)}, u32[]{:S(2)}, u32[]{:S(2)}) collective-permute-start(bf16[2,128,512]{2,1,0:T(8,128)(2,1)S(1)} %pad_maximum_fusion.1.g0), channel_id=1, source_target_pairs={{0,3},{1,0},{2,1},{3,2},{4,7},{5,4},{6,5},{7,6},{8,11},{9,8},{10,9... | collective-permute-start | bytes 786440 | tf_op jit(solution)/shard_map/ppermute | solution.py:24
  42.2 2.2 %copy-start.2 = (bf16[1,512,4096]{2,1,0:T(8,128)(2,1)S(1)}, bf16[1,512,4096]{2,1,0:T(8,128)(2,1)}, u32[]{:S(2)}) copy-start(bf16[1,512,4096]{2,1,0:T(8,128)(2,1)} %param.18) | copy-start | bytes 12582916
  44.4 11.1 %copy-start.20 = (f32[128,64]{1,0:T(8,128)S(1)}, f32[128,64]{1,0:T(8,128)}, u32[]{:S(2)}) copy-start(f32[128,64]{1,0:T(8,128)} %get-tuple-element.48) | copy-start | bytes 98308
  44.4 11.1 %copy-start.21 = (f32[128,64]{1,0:T(8,128)S(1)}, f32[128,64]{1,0:T(8,128)}, u32[]{:S(2)}) copy-start(f32[128,64]{1,0:T(8,128)} %get-tuple-element.49) | copy-start | bytes 98308
  44.4 11.1 %copy-start.22 = (f32[128,64]{1,0:T(8,128)S(1)}, f32[128,64]{1,0:T(8,128)}, u32[]{:S(2)}) copy-start(f32[128,64]{1,0:T(8,128)} %get-tuple-element.50) | copy-start | bytes 98308
  44.4 11.3 %copy-start.3 = (bf16[1,512,4096]{2,1,0:T(8,128)(2,1)S(1)}, bf16[1,512,4096]{2,1,0:T(8,128)(2,1)}, u32[]{:S(2)}) copy-start(bf16[1,512,4096]{2,1,0:T(8,128)(2,1)} %param.18) | copy-start | bytes 12582916
  49.2 21.9 %copy-start.5 = (bf16[2,128,512]{2,1,0:T(8,128)(2,1)}, bf16[2,128,512]{2,1,0:T(8,128)(2,1)S(1)}, u32[]{:S(2)}) copy-start(bf16[2,128,512]{2,1,0:T(8,128)(2,1)S(1)} %get-tuple-element.14) | copy-start | bytes 786436
  49.2 14.0 %collective-permute-start.7 = (bf16[2,128,512]{2,1,0:T(8,128)(2,1)S(1)}, bf16[2,128,512]{2,1,0:T(8,128)(2,1)S(1)}, u32[]{:S(2)}, u32[]{:S(2)}) collective-permute-start(bf16[2,128,512]{2,1,0:T(8,128)(2,1)S(1)} %get-tuple-element.17), channel_id=1, source_target_pairs={{0,3},{1,0},{2,1},{3,2},{4,7},{5,4},{6,5},{7,6},{8,11},{9,8},{10,9... | collective-permute-start | bytes 786440 | tf_op jit(solution)/shard_map/ppermute | solution.py:24
  51.3 12.8 %collective-permute-start.6 = (bf16[2,128,512]{2,1,0:T(8,128)(2,1)S(1)}, bf16[2,128,512]{2,1,0:T(8,128)(2,1)S(1)}, u32[]{:S(2)}, u32[]{:S(2)}) collective-permute-start(bf16[2,128,512]{2,1,0:T(8,128)(2,1)S(1)} %get-tuple-element.16), channel_id=1, source_target_pairs={{0,2},{1,3},{2,0},{3,1},{4,6},{5,7},{6,4},{7,5},{8,10},{9,11},{10,... | collective-permute-start | bytes 786440 | tf_op jit(solution)/shard_map/ppermute | solution.py:24
  55.5 15.6 %collective-permute-start.5 = (bf16[2,128,512]{2,1,0:T(8,128)(2,1)S(1)}, bf16[2,128,512]{2,1,0:T(8,128)(2,1)S(1)}, u32[]{:S(2)}, u32[]{:S(2)}) collective-permute-start(bf16[2,128,512]{2,1,0:T(8,128)(2,1)S(1)} %get-tuple-element.15), channel_id=1, source_target_pairs={{0,1},{1,2},{2,3},{3,0},{4,5},{5,6},{6,7},{7,4},{8,9},{9,10},{10,1... | collective-permute-start | bytes 786440 | tf_op jit(solution)/shard_map/ppermute | solution.py:24
  55.7 31.0 %copy-start.11 = (bf16[2,128,512]{2,1,0:T(8,128)(2,1)S(1)}, bf16[2,128,512]{2,1,0:T(8,128)(2,1)}, u32[]{:S(2)}) copy-start(bf16[2,128,512]{2,1,0:T(8,128)(2,1)} %param.13) | copy-start | bytes 786436
  59.8 52.9 %copy-start.18 = (f32[128,64]{1,0:T(8,128)S(1)}, f32[128,64]{1,0:T(8,128)}, u32[]{:S(2)}) copy-start(f32[128,64]{1,0:T(8,128)} %get-tuple-element.39) | copy-start | bytes 98308
  59.8 52.9 %copy-start.19 = (f32[128,64]{1,0:T(8,128)S(1)}, f32[128,64]{1,0:T(8,128)}, u32[]{:S(2)}) copy-start(f32[128,64]{1,0:T(8,128)} %get-tuple-element.40) | copy-start | bytes 98308
  59.8 12.1 %collective-permute-start.19 = (bf16[2,128,512]{2,1,0:T(8,128)(2,1)S(1)}, bf16[2,128,512]{2,1,0:T(8,128)(2,1)S(1)}, u32[]{:S(2)}, u32[]{:S(2)}) collective-permute-start(bf16[2,128,512]{2,1,0:T(8,128)(2,1)S(1)} %get-tuple-element.21), channel_id=1, source_target_pairs={{0,3},{1,0},{2,1},{3,2},{4,7},{5,4},{6,5},{7,6},{8,11},{9,8},{10,9... | collective-permute-start | bytes 786440 | tf_op jit(solution)/shard_map/ppermute | solution.py:24
  61.9 10.4 %collective-permute-start.18 = (bf16[2,128,512]{2,1,0:T(8,128)(2,1)S(1)}, bf16[2,128,512]{2,1,0:T(8,128)(2,1)S(1)}, u32[]{:S(2)}, u32[]{:S(2)}) collective-permute-start(bf16[2,128,512]{2,1,0:T(8,128)(2,1)S(1)} %get-tuple-element.20), channel_id=1, source_target_pairs={{0,2},{1,3},{2,0},{3,1},{4,6},{5,7},{6,4},{7,5},{8,10},{9,11},{10,... | collective-permute-start | bytes 786440 | tf_op jit(solution)/shard_map/ppermute | solution.py:24
  63.2 11.7 %copy-start.12 = (bf16[2,128,512]{2,1,0:T(8,128)(2,1)}, bf16[2,128,512]{2,1,0:T(8,128)(2,1)S(1)}, u32[]{:S(2)}) copy-start(bf16[2,128,512]{2,1,0:T(8,128)(2,1)S(1)} %collective-permute-done.7) | copy-start | bytes 786436
  63.2 11.7 %collective-permute-start.17 = (bf16[2,128,512]{2,1,0:T(8,128)(2,1)S(1)}, bf16[2,128,512]{2,1,0:T(8,128)(2,1)S(1)}, u32[]{:S(2)}, u32[]{:S(2)}) collective-permute-start(bf16[2,128,512]{2,1,0:T(8,128)(2,1)S(1)} %get-tuple-element.19), channel_id=1, source_target_pairs={{0,1},{1,2},{2,3},{3,0},{4,5},{5,6},{6,7},{7,4},{8,9},{9,10},{10,1... | collective-permute-start | bytes 786440 | tf_op jit(solution)/shard_map/ppermute | solution.py:24
  64.1 10.8 %copy-start.13 = (bf16[2,128,512]{2,1,0:T(8,128)(2,1)}, bf16[2,128,512]{2,1,0:T(8,128)(2,1)S(1)}, u32[]{:S(2)}) copy-start(bf16[2,128,512]{2,1,0:T(8,128)(2,1)S(1)} %collective-permute-done.6) | copy-start | bytes 786436
  71.1 4.6 %copy-start.14 = (bf16[2,128,512]{2,1,0:T(8,128)(2,1)}, bf16[2,128,512]{2,1,0:T(8,128)(2,1)S(1)}, u32[]{:S(2)}) copy-start(bf16[2,128,512]{2,1,0:T(8,128)(2,1)S(1)} %collective-permute-done.5) | copy-start | bytes 786436
  71.9 10.3 %collective-permute-start.8 = (bf16[128,512]{1,0:T(8,128)(2,1)}, bf16[128,512]{1,0:T(8,128)(2,1)}, u32[]{:S(2)}, u32[]{:S(2)}) collective-permute-start(bf16[128,512]{1,0:T(8,128)(2,1)} %fusion.7), channel_id=1, source_target_pairs={{0,4},{1,5},{2,6},{3,7},{4,0},{5,1},{6,2},{7,3},{8,12},{9,13},{10,... | collective-permute-start | bytes 393224 | tf_op jit(solution)/shard_map/ppermute | solution.py:24
  71.9 3.8 %copy-start.15 = (bf16[2,128,512]{2,1,0:T(8,128)(2,1)}, bf16[2,128,512]{2,1,0:T(8,128)(2,1)S(1)}, u32[]{:S(2)}) copy-start(bf16[2,128,512]{2,1,0:T(8,128)(2,1)S(1)} %collective-permute-done.19) | copy-start | bytes 786436
  72.3 9.9 %copy-start.16 = (bf16[2,128,512]{2,1,0:T(8,128)(2,1)}, bf16[2,128,512]{2,1,0:T(8,128)(2,1)S(1)}, u32[]{:S(2)}) copy-start(bf16[2,128,512]{2,1,0:T(8,128)(2,1)S(1)} %collective-permute-done.18) | copy-start | bytes 786436
  74.9 0.8 copy-start.17
  75.7 11.1 %collective-permute-start.20 = (bf16[128,512]{1,0:T(8,128)(2,1)}, bf16[128,512]{1,0:T(8,128)(2,1)}, u32[]{:S(2)}, u32[]{:S(2)}) collective-permute-start(bf16[128,512]{1,0:T(8,128)(2,1)} %fusion.9), channel_id=1, source_target_pairs={{0,4},{1,5},{2,6},{3,7},{4,0},{5,1},{6,2},{7,3},{8,12},{9,13},{10,... | collective-permute-start | bytes 393224 | tf_op jit(solution)/shard_map/ppermute | solution.py:24
  79.0 15.6 %collective-permute-start.11 = (bf16[2,128,512]{2,1,0:T(8,128)(2,1)S(1)}, bf16[2,128,512]{2,1,0:T(8,128)(2,1)}, u32[]{:S(2)}, u32[]{:S(2)}) collective-permute-start(bf16[2,128,512]{2,1,0:T(8,128)(2,1)S(1)} %pad_maximum_fusion.1.g0), channel_id=1, source_target_pairs={{0,8},{1,9},{2,10},{3,11},{4,12},{5,13},{6,14},{7,15},{8,16},{9,17... | collective-permute-start | bytes 786440 | tf_op jit(solution)/shard_map/ppermute | solution.py:24
  89.1 8.6 %collective-permute-start.13 = (bf16[128,512]{1,0:T(8,128)(2,1)}, bf16[128,512]{1,0:T(8,128)(2,1)S(1)}, u32[]{:S(2)}, u32[]{:S(2)}) collective-permute-start(bf16[128,512]{1,0:T(8,128)(2,1)} %get-tuple-element.26), channel_id=1, source_target_pairs={{0,20},{1,21},{2,22},{3,23},{4,16},{5,17},{6,18},{7,19},{8,28},{9,... | collective-permute-start | bytes 393224 | tf_op jit(solution)/shard_map/ppermute | solution.py:24
  93.0 12.8 %collective-permute-start.12 = (bf16[128,512]{1,0:T(8,128)(2,1)}, bf16[128,512]{1,0:T(8,128)(2,1)S(1)}, u32[]{:S(2)}, u32[]{:S(2)}) collective-permute-start(bf16[128,512]{1,0:T(8,128)(2,1)} %get-tuple-element.26), channel_id=1, source_target_pairs={{0,16},{1,17},{2,18},{3,19},{4,20},{5,21},{6,22},{7,23},{8,24},{9,... | collective-permute-start | bytes 393224 | tf_op jit(solution)/shard_map/ppermute | solution.py:24
  105.9 7.9 %collective-permute-start.22 = (bf16[2,128,512]{2,1,0:T(8,128)(2,1)S(1)}, bf16[2,128,512]{2,1,0:T(8,128)(2,1)S(1)}, u32[]{:S(2)}, u32[]{:S(2)}) collective-permute-start(bf16[2,128,512]{2,1,0:T(8,128)(2,1)S(1)} %add_convert_fusion.g0), channel_id=1, source_target_pairs={{0,1},{1,2},{2,3},{3,0},{4,5},{5,6},{6,7},{7,4},{8,9},{9,10},{10,1... | collective-permute-start | bytes 786440 | tf_op jit(solution)/shard_map/ppermute | solution.py:24
  106.0 15.5 %collective-permute-start.23 = (bf16[2,128,512]{2,1,0:T(8,128)(2,1)S(1)}, bf16[2,128,512]{2,1,0:T(8,128)(2,1)S(1)}, u32[]{:S(2)}, u32[]{:S(2)}) collective-permute-start(bf16[2,128,512]{2,1,0:T(8,128)(2,1)S(1)} %add_convert_fusion.g0), channel_id=1, source_target_pairs={{0,2},{1,3},{2,0},{3,1},{4,6},{5,7},{6,4},{7,5},{8,10},{9,11},{10,... | collective-permute-start | bytes 786440 | tf_op jit(solution)/shard_map/ppermute | solution.py:24
  109.5 12.9 %collective-permute-start.24 = (bf16[2,128,512]{2,1,0:T(8,128)(2,1)S(1)}, bf16[2,128,512]{2,1,0:T(8,128)(2,1)S(1)}, u32[]{:S(2)}, u32[]{:S(2)}) collective-permute-start(bf16[2,128,512]{2,1,0:T(8,128)(2,1)S(1)} %add_convert_fusion.g0), channel_id=1, source_target_pairs={{0,3},{1,0},{2,1},{3,2},{4,7},{5,4},{6,5},{7,6},{8,11},{9,8},{10,9... | collective-permute-start | bytes 786440 | tf_op jit(solution)/shard_map/ppermute | solution.py:24
  113.7 22.8 %collective-permute-start.21 = (bf16[128,512]{1,0:T(8,128)(2,1)}, bf16[128,512]{1,0:T(8,128)(2,1)S(1)}, u32[]{:S(2)}, u32[]{:S(2)}) collective-permute-start(bf16[128,512]{1,0:T(8,128)(2,1)} %get-tuple-element.37), channel_id=1, source_target_pairs={{0,8},{1,9},{2,10},{3,11},{4,12},{5,13},{6,14},{7,15},{8,16},{9,17... | collective-permute-start | bytes 393224 | tf_op jit(solution)/shard_map/ppermute | solution.py:24
  122.4 2.2 %copy-start.1 = (bf16[1,4096,512]{2,1,0:T(8,128)(2,1)S(1)}, bf16[1,4096,512]{2,1,0:T(8,128)(2,1)}, u32[]{:S(2)}) copy-start(bf16[1,4096,512]{2,1,0:T(8,128)(2,1)} %param.16) | copy-start | bytes 12582916
  124.6 2.2 %copy-start.4 = (bf16[1,512,4096]{2,1,0:T(8,128)(2,1)S(1)}, bf16[1,512,4096]{2,1,0:T(8,128)(2,1)}, u32[]{:S(2)}) copy-start(bf16[1,512,4096]{2,1,0:T(8,128)(2,1)} %param.18) | copy-start | bytes 12582916
  126.8 9.5 %copy-start.7 = (bf16[1,128,512]{2,1,0:T(8,128)(2,1)S(1)}, bf16[1,128,512]{2,1,0:T(8,128)(2,1)}, u32[]{:S(2)}) copy-start(bf16[1,128,512]{2,1,0:T(8,128)(2,1)} %param.11) | copy-start | bytes 393220
  126.8 9.5 %copy-start.8 = (bf16[1,128,512]{2,1,0:T(8,128)(2,1)S(1)}, bf16[1,128,512]{2,1,0:T(8,128)(2,1)}, u32[]{:S(2)}) copy-start(bf16[1,128,512]{2,1,0:T(8,128)(2,1)} %param.12) | copy-start | bytes 393220
  126.8 9.5 %copy-start.23 = (bf16[128,512]{1,0:T(8,128)(2,1)S(1)}, bf16[128,512]{1,0:T(8,128)(2,1)}, u32[]{:S(2)}) copy-start(bf16[128,512]{1,0:T(8,128)(2,1)} %get-tuple-element.27) | copy-start | bytes 393220
  126.8 20.9 %copy-start.10 = (bf16[128,512]{1,0:T(8,128)(2,1)S(1)}, bf16[128,512]{1,0:T(8,128)(2,1)}, u32[]{:S(2)}) copy-start(bf16[128,512]{1,0:T(8,128)(2,1)} %copy-done.9) | copy-start | bytes 393220
  130.9 10.1 %collective-permute-start.27 = (bf16[2,128,512]{2,1,0:T(8,128)(2,1)S(1)}, bf16[2,128,512]{2,1,0:T(8,128)(2,1)S(1)}, u32[]{:S(2)}, u32[]{:S(2)}) collective-permute-start(bf16[2,128,512]{2,1,0:T(8,128)(2,1)S(1)} %get-tuple-element.25), channel_id=1, source_target_pairs={{0,3},{1,0},{2,1},{3,2},{4,7},{5,4},{6,5},{7,6},{8,11},{9,8},{10,9... | collective-permute-start | bytes 786440 | tf_op jit(solution)/shard_map/ppermute | solution.py:24
  132.4 10.8 %collective-permute-start.26 = (bf16[2,128,512]{2,1,0:T(8,128)(2,1)S(1)}, bf16[2,128,512]{2,1,0:T(8,128)(2,1)S(1)}, u32[]{:S(2)}, u32[]{:S(2)}) collective-permute-start(bf16[2,128,512]{2,1,0:T(8,128)(2,1)S(1)} %get-tuple-element.24), channel_id=1, source_target_pairs={{0,2},{1,3},{2,0},{3,1},{4,6},{5,7},{6,4},{7,5},{8,10},{9,11},{10,... | collective-permute-start | bytes 786440 | tf_op jit(solution)/shard_map/ppermute | solution.py:24
  136.0 11.5 %collective-permute-start.25 = (bf16[2,128,512]{2,1,0:T(8,128)(2,1)S(1)}, bf16[2,128,512]{2,1,0:T(8,128)(2,1)S(1)}, u32[]{:S(2)}, u32[]{:S(2)}) collective-permute-start(bf16[2,128,512]{2,1,0:T(8,128)(2,1)S(1)} %get-tuple-element.23), channel_id=1, source_target_pairs={{0,1},{1,2},{2,3},{3,0},{4,5},{5,6},{6,7},{7,4},{8,9},{9,10},{10,1... | collective-permute-start | bytes 786440 | tf_op jit(solution)/shard_map/ppermute | solution.py:24
  136.3 11.3 %collective-permute-start.9 = (bf16[128,512]{1,0:T(8,128)(2,1)S(1)}, bf16[128,512]{1,0:T(8,128)(2,1)S(1)}, u32[]{:S(2)}, u32[]{:S(2)}) collective-permute-start(bf16[128,512]{1,0:T(8,128)(2,1)S(1)} %copy-done.23), channel_id=1, source_target_pairs={{0,8},{1,9},{2,10},{3,11},{4,12},{5,13},{6,14},{7,15},{8,16},{9,17... | collective-permute-start | bytes 393224 | tf_op jit(solution)/shard_map/ppermute | solution.py:24
  147.5 9.4 %collective-permute-start.28 = (bf16[128,512]{1,0:T(8,128)(2,1)S(1)}, bf16[128,512]{1,0:T(8,128)(2,1)S(1)}, u32[]{:S(2)}, u32[]{:S(2)}) collective-permute-start(bf16[128,512]{1,0:T(8,128)(2,1)S(1)} %fusion.10), channel_id=1, source_target_pairs={{0,4},{1,5},{2,6},{3,7},{4,0},{5,1},{6,2},{7,3},{8,12},{9,13},{10,... | collective-permute-start | bytes 393224 | tf_op jit(solution)/shard_map/ppermute | solution.py:24

commit v2 on v1

v2 whole, which is shorter than its diff:
```python
import functools

import jax
import jax.numpy as jnp
from jax import lax
from jax.experimental import pallas as pl
from jax.experimental.pallas import tpu as pltpu
from jax.sharding import PartitionSpec as P

HD = 128
rope_base = 500000.0
norm_eps = 1e-05
bf16 = jnp.bfloat16
f32 = jnp.float32
Y = 4
ORDER = (3, 1, 2)


def move(value, sections, tensors, target):
    pairs = []
    for s in range(sections):
        for t in range(tensors):
            s2, t2 = target(s, t)
            if s2 >= sections:
                s2, t2 = s2 - sections, t ^ 4
            pairs.append((s * tensors + t, s2 * tensors + t2))
    return lax.ppermute(value, ("section", "tensor"), pairs)


def y_shift(k):
    return lambda s, t: (s, (t & ~3) | ((t + k) & 3))


def hop(n, other=False):
    return lambda s, t: (s + n, t ^ 4 if other else t)


def rope_tables(lengths, rows):
    half = HD // 2
    index = jnp.arange(half).astype(f32)
    freqs = jnp.exp(-jnp.log(rope_base) * 2.0 * index / HD)
    positions = lengths[:, None] + jnp.arange(rows)
    angles = positions.astype(f32)[..., None] * freqs
    return jnp.cos(angles), jnp.sin(angles)


def attend_kernel(tick, *refs):
    scalars, pieces, refs = refs[0], refs[1 : 1 + Y], refs[1 + Y :]
    gain, cos, sin, wq_hbm, wkv_hbm, wo_hbm, kc_hbm, vc_hbm = refs[:8]
    outs, refs = refs[8 : 8 + Y], refs[8 + Y :]
    wq, wkv, wo, kc, vc, att, sems = refs
    length, high, low = scalars[tick], scalars[3], scalars[4]

    taken = {k: [ref.at[0], ref.at[1]] for k, ref in zip((0,) + ORDER, pieces)}
    given = [[ref.at[0], ref.at[1]] for ref in outs]
    rows, width = taken[0][0].shape

    def chunk(slot, y):
        at = ((high ^ slot) * Y + (y & (Y - 1))) * width
        return pl.ds(pl.multiple_of(at, width), width)

    order = [(k, slot) for k in range(Y) for slot in range(2)]
    spots = [chunk(slot, low - k + Y) for k, slot in order]
    loads = []
    for i, at in enumerate(spots):
        loads.append(
            (
                pltpu.make_async_copy(wq_hbm.at[at], wq.at[at], sems.at[2 * i]),
                pltpu.make_async_copy(wkv_hbm.at[at], wkv.at[at], sems.at[2 * i + 1]),
            )
        )
    n = 2 * len(order)
    load_k = pltpu.make_async_copy(kc_hbm.at[0, tick], kc, sems.at[n])
    load_v = pltpu.make_async_copy(vc_hbm.at[0, tick], vc, sems.at[n + 1])
    load_o = pltpu.make_async_copy(wo_hbm, wo, sems.at[n + 2])
    for a, b in loads:
        a.start()
        b.start()
    load_k.start()
    load_v.start()
    load_o.start()

    total = jnp.zeros((rows, width), f32)
    for k, slot in order:
        v = taken[k][slot][...].astype(f32)
        total = total + v * v
    mean = jnp.sum(total, axis=-1, keepdims=True) / (2 * Y * width)
    inverse = lax.rsqrt(mean + norm_eps)
    q = jnp.zeros((rows, wq.shape[1]), f32)
    kv = jnp.zeros((rows, wkv.shape[1]), f32)
    for i, (k, slot) in enumerate(order):
        at = spots[i]
        v = taken[k][slot][...].astype(f32)
        normed = (v * inverse * gain[:, at].astype(f32)).astype(bf16)
        loads[i][0].wait()
        loads[i][1].wait()
        q = q + jnp.dot(normed, wq[at, :], preferred_element_type=f32)
        kv = kv + jnp.dot(normed, wkv[at, :], preferred_element_type=f32)
    c, s = cos[tick], sin[tick]
    cos_t, sin_t = jnp.concatenate([c, c], 1), jnp.concatenate([-s, s], 1)

    def rotate(v):
        return (v * cos_t + pltpu.roll(v, HD // 2, 1) * sin_t).astype(bf16)

    heads = q.shape[1] // HD
    qs = jnp.concatenate([rotate(q[:, h * HD : (h + 1) * HD]) for h in range(heads)], 0)
    nk = rotate(kv[:, :HD])
    nv = kv[:, HD:].astype(bf16)
    contract = (((1,), (1,)), ((), ()))
    scale = HD ** (-0.5)
    load_k.wait()
    s1 = lax.dot_general(qs, kc[...], contract, preferred_element_type=f32) * scale
    s2 = lax.dot_general(qs, nk, contract, preferred_element_type=f32) * scale
    seen1 = lax.broadcasted_iota(jnp.int32, s1.shape, 1) < length
    row = lax.broadcasted_iota(jnp.int32, s2.shape, 0) & (rows - 1)
    seen2 = lax.broadcasted_iota(jnp.int32, s2.shape, 1) <= row
    s1 = jnp.where(seen1, s1, -1e30)
    s2 = jnp.where(seen2, s2, -1e30)
    top = jnp.maximum(
        jnp.max(s1, axis=-1, keepdims=True), jnp.max(s2, axis=-1, keepdims=True)
    )
    e1 = jnp.where(seen1, jnp.exp(s1 - top), 0.0)
    e2 = jnp.where(seen2, jnp.exp(s2 - top), 0.0)
    norm = jnp.sum(e1, axis=-1, keepdims=True) + jnp.sum(e2, axis=-1, keepdims=True)
    p1 = (e1 / norm).astype(bf16)
    p2 = (e2 / norm).astype(bf16)
    load_v.wait()
    out = jnp.dot(p1, vc[...], preferred_element_type=f32) + jnp.dot(
        p2, nv, preferred_element_type=f32
    )
    out = out.astype(bf16)
    for h in range(heads):
        att[:, h * HD : (h + 1) * HD] = out[h * rows : (h + 1) * rows]
    a = att[...]
    load_o.wait()
    for slot in (1, 0):
        for k in range(Y):
            at = chunk(slot, low + k)
            given[k][slot][...] = jnp.dot(a, wo[:, at], preferred_element_type=f32).astype(bf16)


def attend(tick, scalars, gathered, gain, cos, sin, wq, wkv, wo, kc, vc):
    rows, width = gathered[0].shape[-2:]
    vmem, hbm = pl.BlockSpec(memory_space=pltpu.VMEM), pl.BlockSpec(memory_space=pltpu.HBM)
    cols = wq.shape[0]
    out_shape = [jax.ShapeDtypeStruct((2, rows, width), bf16)] * Y
    flops = 2 * rows * cols * (2 * wq.shape[1] + wkv.shape[1])
    return pl.pallas_call(
        functools.partial(attend_kernel, tick),
        out_shape=out_shape,
        in_specs=[pl.BlockSpec(memory_space=pltpu.SMEM)]
        + [vmem] * (len(gathered) + 3)
        + [hbm] * 5,
        out_specs=[vmem] * len(out_shape),
        scratch_shapes=[
            pltpu.VMEM(wq.shape, bf16),
            pltpu.VMEM(wkv.shape, bf16),
            pltpu.VMEM(wo.shape, bf16),
            pltpu.VMEM(kc.shape[2:], bf16),
            pltpu.VMEM(vc.shape[2:], bf16),
            pltpu.VMEM((rows, wq.shape[1]), bf16),
            pltpu.SemaphoreType.DMA((4 * Y + 3,)),
        ],
        compiler_params=pltpu.CompilerParams(vmem_limit_bytes=22 * 1024 * 1024),
        cost_estimate=pl.CostEstimate(
            flops=flops, bytes_accessed=40 * 1024 * 1024, transcendentals=512 * 640
        ),
    )(scalars, *gathered, gain, cos, sin, wq, wkv, wo, kc, vc)


def combine_kernel(where, own, other, base, local, out):
    first, entry = where[0] == 0, where[0] < 2
    for slot in range(2):
        moved = own[slot].astype(f32) + other[1 - slot].astype(f32)
        fresh = local[...] if slot == 0 else own[0]
        moved = jnp.where(entry, fresh, moved.astype(bf16)).astype(f32)
        out[slot] = jnp.where(first, moved, base[slot].astype(f32) + moved).astype(bf16)


def combine(where, own, other, base, local):
    vmem = pl.BlockSpec(memory_space=pltpu.VMEM)
    return pl.pallas_call(
        combine_kernel,
        out_shape=jax.ShapeDtypeStruct(own.shape, own.dtype),
        in_specs=[pl.BlockSpec(memory_space=pltpu.SMEM)] + [vmem] * 4,
        out_specs=vmem,
        compiler_params=pltpu.CompilerParams(vmem_limit_bytes=4 * 1024 * 1024),
    )(where, own, other, base, local)


def body(
    stream_two, block_last, incoming_two, incoming_last, norm_gain,
    w_query, w_keyval, w_out, keys_cache, values_cache, cached_len,
):
    sections = lax.axis_size("section")
    tensors = lax.axis_size("tensor")
    sid = lax.axis_index("section")
    tid = lax.axis_index("tensor")
    rows = stream_two.shape[1]
    send = functools.partial(lambda v, f: move(v, sections, tensors, f))
    last = sections - 1
    first, final = sid == 0, sid == last

    def after(value, *others):
        return lax.optimization_barrier((value, others))[0]

    def exchange(parts):
        return [parts[0]] + [send(parts[k], y_shift(k)) for k in ORDER]

    def gather(pair):
        return exchange([pair] * Y)

    def add(a, b):
        return (a.astype(f32) + b.astype(f32)).astype(bf16)

    def halves(got):
        both = sum(g.astype(f32) for g in got)
        return both[0], both[1].astype(bf16)

    x0 = stream_two[0]
    pair0 = jnp.stack([x0, send(x0, hop(0, True))])
    wq = pltpu.with_memory_space_constraint(w_query[0], pltpu.HBM)
    wo = pltpu.with_memory_space_constraint(w_out[0], pltpu.HBM)

    ticks = keys_cache.shape[1]
    lengths = lax.dynamic_slice_in_dim(cached_len, last - sid, ticks)
    scalars = jnp.concatenate([lengths, jnp.stack([tid // Y, tid % Y]).astype(jnp.int32)])
    cos, sin = rope_tables(lengths, rows)
    wkv = w_keyval[0].reshape(w_keyval.shape[1], -1)

    pair0, scalars, cos, sin, wkv = lax.optimization_barrier(
        (pair0, scalars, cos, sin, wkv)
    )
    all0 = gather(pair0)
    wkv = pltpu.with_memory_space_constraint(wkv, pltpu.HBM)

    def block(tick, gathered):
        return attend(
            tick, scalars, gathered, norm_gain, cos, sin,
            wq, wkv, wo, keys_cache, values_cache,
        )

    parts0 = block(0, all0)
    got0 = exchange(parts0)
    block_late, enter_two, enter_last = after(
        (block_last, incoming_two, incoming_last), parts0
    )
    out1 = jnp.where(final, enter_two[0], add(x0, block_late[0]))
    a1, z1 = send(out1, hop(1)), send(out1, hop(1, True))
    local = jnp.where(first, enter_two[1], enter_last[0])
    entering = jnp.where(final, enter_last[0], enter_two[1])
    got0, local, entering = lax.optimization_barrier((got0, local, entering))
    sums0 = sum(g.astype(f32) for g in got0).astype(bf16)
    out2 = jnp.where(sid >= last - 1, entering[None], sums0)
    own, other = send(out2, hop(2)), send(out2, hop(2, True))
    a1, z1 = after((a1, z1), out2)
    a1 = jnp.where(first, incoming_two[0], a1)
    pair1 = jnp.stack([a1, z1])
    base = send(pair1, hop(1))
    all1 = gather(pair1)
    pair2 = combine(sid.astype(jnp.int32)[None], own, other, base, local)
    all2 = gather(pair2)
    late0, all1 = after((sums0, all1), pair2)
    swapped0 = send(late0[1], hop(0, True))
    parts1 = block(1, all1)
    got1 = exchange(parts1)
    parts2 = block(2, after(all2, parts1))
    swapped0, got1 = after((swapped0, got1), parts2)
    got2 = lax.optimization_barrier(exchange(parts2))

    mine1, theirs1 = halves(got1)
    b1 = (mine1 + send(theirs1, hop(0, True)).astype(f32)).astype(bf16)
    b0 = add(late0[0], swapped0)
    s0 = add(x0, block_last[0])
    t1 = add(a1, jnp.where(first, incoming_last[0], send(b0, hop(1))))
    t2 = add(pair2[0], jnp.where(first, incoming_last[1], send(b1, hop(1))))
    mine2, theirs2 = halves(got2)
    b2 = (mine2 + send(theirs2, hop(0, True)).astype(f32)).astype(bf16)
    return jnp.stack([s0, t1, t2])[None], jnp.stack([b0, b1, b2])[None]


def solution(mesh):
    placed = (
        P("section", None, "tensor"),
        P("section", None, "tensor"),
        P(None, None, "tensor"),
        P(None, None, "tensor"),
        P("section", None),
        P("section", None, "tensor"),
        P("section", None, None, "tensor"),
        P("section", "tensor", None),
        P("section", None, None, "tensor"),
        P("section", None, None, "tensor"),
        P(),
    )
    out = P("section", None, None, "tensor")
    return jax.shard_map(
        body, mesh=mesh, in_specs=placed, out_specs=(out, out), check_vma=False
    )
```

time: 160 us -> 132 us (0.82)
  the two profiles are of different devices: /device:TPU:16 before, /device:TPU:15 now
where the time goes in v2:
time: 132 us
  starting transfers between devices  64.2 us (49%)
  waiting for transfers between devices  42.1 us (32%)
  Pallas kernels  17.7 us (13%)
  local copies, waits for them, and re-layouts  4.05 us (3%)
  other arithmetic  3.32 us (3%)
    ppermute x29, starting transfers between devices, move(): return lax.ppermute(value, ('section', 'tensor'), pairs)  64.2 us
    ppermute x29, waiting for transfers between devices, move(): return lax.ppermute(value, ('section', 'tensor'), pairs)  42.1 us
    pallas_call x3, Pallas kernels, attend(): pl.pallas_call(functools.partial(attend_kernel, tick), out_shape=out_shap...  17.6 us
    unnamed x15, local copies, waits for them, and re-layouts  3.27 us
  transfers between devices with their start and end apart: 29, of which 12 were waited for; matrix products, arithmetic and copies ran while one was open for 5% of the time, Pallas kernels for 9%

profile of v2, /device:TPU:15, one launch (start us, length us, event | category | flops | bytes accessed | tf_op | source)
XLA Modules:
  0.0 132.3 jit_solution(12444660146863468362)
XLA Ops:
  0.7 7.0 %collective-permute-start = (bf16[128,512]{1,0:T(8,128)(2,1)}, bf16[128,512]{1,0:T(8,128)(2,1)S(1)}, u32[]{:S(2)}, u32[]{:S(2)}) collective-permute-start(bf16[128,512]{1,0:T(8,128)(2,1)} %bitcast.89), channel_id=1, source_target_pairs={{0,4},{1,5},{2,6},{3,7},{4,0},{5,1},{6,2},{7,3},{8,12},{9,13},{10,... | collective-permute-start | bytes 393224 | tf_op jit(solution)/shard_map/ppermute | solution.py:27
  7.7 0.7 dynamic_slice.3
  8.4 0.1 add_convert_fusion.3
  8.5 0.8 multiply_sine_fusion
  9.3 3.2 %copy.15 = bf16[512,8,2,128]{3,1,2,0:T(8,128)(2,1)} copy(bf16[512,8,2,128]{3,2,1,0:T(2,128)(2,1)} %bitcast.88) | data formatting | bytes 4194304
  12.5 0.1 pad_add_fusion.refs_0_
  12.6 0.2 collective-permute-start.1
  12.9 1.3 collective-permute-start.2
  14.2 3.2 %collective-permute-start.3 = (bf16[2,128,512]{2,1,0:T(8,128)(2,1)S(1)}, bf16[2,128,512]{2,1,0:T(8,128)(2,1)S(1)}, u32[]{:S(2)}, u32[]{:S(2)}) collective-permute-start(bf16[2,128,512]{2,1,0:T(8,128)(2,1)S(1)} %pad_maximum_fusion.refs_1_), channel_id=1, source_target_pairs={{0,2},{1,3},{2,0},{3,1},{4,6},{5,7},{6,4},{7,5},{8,10},{9,11},{10,... | collective-permute-start | bytes 786440 | tf_op jit(solution)/shard_map/ppermute | solution.py:27
  17.4 2.2 %collective-permute-done.1.refs_2_ = bf16[2,128,512]{2,1,0:T(8,128)(2,1)S(1)} collective-permute-done((bf16[2,128,512]{2,1,0:T(8,128)(2,1)S(1)}, bf16[2,128,512]{2,1,0:T(8,128)(2,1)S(1)}, u32[]{:S(2)}, u32[]{:S(2)}) %collective-permute-start.1) | collective-permute-done | bytes 262176 | tf_op jit(solution)/shard_map/ppermute | solution.py:27
  19.5 1.4 %collective-permute-done.2.refs_3_ = bf16[2,128,512]{2,1,0:T(8,128)(2,1)S(1)} collective-permute-done((bf16[2,128,512]{2,1,0:T(8,128)(2,1)S(1)}, bf16[2,128,512]{2,1,0:T(8,128)(2,1)S(1)}, u32[]{:S(2)}, u32[]{:S(2)}) %collective-permute-start.2) | collective-permute-done | bytes 262176 | tf_op jit(solution)/shard_map/ppermute | solution.py:27
  21.0 5.2 %collective-permute-done.3.refs_4_ = bf16[2,128,512]{2,1,0:T(8,128)(2,1)S(1)} collective-permute-done((bf16[2,128,512]{2,1,0:T(8,128)(2,1)S(1)}, bf16[2,128,512]{2,1,0:T(8,128)(2,1)S(1)}, u32[]{:S(2)}, u32[]{:S(2)}) %collective-permute-start.3) | collective-permute-done | bytes 262176 | tf_op jit(solution)/shard_map/ppermute | solution.py:27
  26.2 0.0 copy-start.4
  26.2 0.0 copy-start.6
  26.2 0.0 copy-start.5
  26.2 5.9 %shard_map.122 = (bf16[2,128,512]{2,1,0:T(8,128)(2,1)S(1)}, bf16[2,128,512]{2,1,0:T(8,128)(2,1)S(1)}, bf16[2,128,512]{2,1,0:T(8,128)(2,1)S(1)}, bf16[2,128,512]{2,1,0:T(8,128)(2,1)S(1)}) custom-call(s32[5]{0:T(128)S(1)} %pad_add_fusion.refs_0_, bf16[2,128,512]{2,1,0:T(8,128)(2,1)S(1)} %pad_maximum_fusion.refs_1_, ...), custom_call_target="tpu_custom_call" | custom-call | flops 1342177280 | bytes 41943040 | tf_op jit(solution)/shard_map/pallas_call | solution.py:148
  32.1 1.9 %collective-permute-start.6 = (bf16[2,128,512]{2,1,0:T(8,128)(2,1)S(1)}, bf16[2,128,512]{2,1,0:T(8,128)(2,1)S(1)}, u32[]{:S(2)}, u32[]{:S(2)}) collective-permute-start(bf16[2,128,512]{2,1,0:T(8,128)(2,1)S(1)} %get-tuple-element.56), channel_id=1, source_target_pairs={{0,3},{1,0},{2,1},{3,2},{4,7},{5,4},{6,5},{7,6},{8,11},{9,8},{10,9... | collective-permute-start | bytes 786440 | tf_op jit(solution)/shard_map/ppermute | solution.py:27
  34.0 0.0 collective-permute-start.7
  34.0 2.0 %collective-permute-start.8 = (bf16[2,128,512]{2,1,0:T(8,128)(2,1)S(1)}, bf16[2,128,512]{2,1,0:T(8,128)(2,1)S(1)}, u32[]{:S(2)}, u32[]{:S(2)}) collective-permute-start(bf16[2,128,512]{2,1,0:T(8,128)(2,1)S(1)} %get-tuple-element.55), channel_id=1, source_target_pairs={{0,2},{1,3},{2,0},{3,1},{4,6},{5,7},{6,4},{7,5},{8,10},{9,11},{10,... | collective-permute-start | bytes 786440 | tf_op jit(solution)/shard_map/ppermute | solution.py:27
  36.0 0.1 fusion.8
  36.0 4.6 %collective-permute-start.4 = (bf16[128,512]{1,0:T(8,128)(2,1)S(1)}, bf16[128,512]{1,0:T(8,128)(2,1)S(1)}, u32[]{:S(2)}, u32[]{:S(2)}) collective-permute-start(bf16[128,512]{1,0:T(8,128)(2,1)S(1)} %fusion.8), channel_id=1, source_target_pairs={{0,8},{1,9},{2,10},{3,11},{4,12},{5,13},{6,14},{7,15},{8,16},{9,17... | collective-permute-start | bytes 393224 | tf_op jit(solution)/shard_map/ppermute | solution.py:27
  40.7 3.3 %collective-permute-start.5 = (bf16[128,512]{1,0:T(8,128)(2,1)S(1)}, bf16[128,512]{1,0:T(8,128)(2,1)S(1)}, u32[]{:S(2)}, u32[]{:S(2)}) collective-permute-start(bf16[128,512]{1,0:T(8,128)(2,1)S(1)} %fusion.8), channel_id=1, source_target_pairs={{0,12},{1,13},{2,14},{3,15},{4,8},{5,9},{6,10},{7,11},{8,20},{9,21... | collective-permute-start | bytes 393224 | tf_op jit(solution)/shard_map/ppermute | solution.py:27
  44.0 1.0 collective-permute-done.8
  45.0 0.2 broadcast_select_fusion
  45.2 0.0 collective-permute-done.4
  45.2 4.1 %collective-permute-done.5 = bf16[128,512]{1,0:T(8,128)(2,1)S(1)} collective-permute-done((bf16[128,512]{1,0:T(8,128)(2,1)S(1)}, bf16[128,512]{1,0:T(8,128)(2,1)S(1)}, u32[]{:S(2)}, u32[]{:S(2)}) %collective-permute-start.5) | collective-permute-done | bytes 131104 | tf_op jit(solution)/shard_map/ppermute | solution.py:27
  49.4 3.4 %collective-permute-start.14 = (bf16[2,128,512]{2,1,0:T(8,128)(2,1)S(1)}, bf16[2,128,512]{2,1,0:T(8,128)(2,1)S(1)}, u32[]{:S(2)}, u32[]{:S(2)}) collective-permute-start(bf16[2,128,512]{2,1,0:T(8,128)(2,1)S(1)} %pad_maximum_fusion.1.refs_1_), channel_id=1, source_target_pairs={{0,8},{1,9},{2,10},{3,11},{4,12},{5,13},{6,14},{7,15},{8,16},{9,17... | collective-permute-start | bytes 786440 | tf_op jit(solution)/shard_map/ppermute | solution.py:27
  52.8 2.2 %collective-permute-start.12 = (bf16[2,128,512]{2,1,0:T(8,128)(2,1)S(1)}, bf16[2,128,512]{2,1,0:T(8,128)(2,1)S(1)}, u32[]{:S(2)}, u32[]{:S(2)}) collective-permute-start(bf16[2,128,512]{2,1,0:T(8,128)(2,1)S(1)} %get-tuple-element.94), channel_id=1, source_target_pairs={{0,16},{1,17},{2,18},{3,19},{4,20},{5,21},{6,22},{7,23},{8,24},{9,... | collective-permute-start | bytes 786440 | tf_op jit(solution)/shard_map/ppermute | solution.py:27
  55.0 4.3 %collective-permute-start.13 = (bf16[2,128,512]{2,1,0:T(8,128)(2,1)S(1)}, bf16[2,128,512]{2,1,0:T(8,128)(2,1)S(1)}, u32[]{:S(2)}, u32[]{:S(2)}) collective-permute-start(bf16[2,128,512]{2,1,0:T(8,128)(2,1)S(1)} %get-tuple-element.94), channel_id=1, source_target_pairs={{0,20},{1,21},{2,22},{3,23},{4,16},{5,17},{6,18},{7,19},{8,28},{9,... | collective-permute-start | bytes 786440 | tf_op jit(solution)/shard_map/ppermute | solution.py:27
  59.4 1.5 %collective-permute-start.9 = (bf16[2,128,512]{2,1,0:T(8,128)(2,1)S(1)}, bf16[2,128,512]{2,1,0:T(8,128)(2,1)S(1)}, u32[]{:S(2)}, u32[]{:S(2)}) collective-permute-start(bf16[2,128,512]{2,1,0:T(8,128)(2,1)S(1)} %pad_maximum_fusion.1.refs_1_), channel_id=1, source_target_pairs={{0,3},{1,0},{2,1},{3,2},{4,7},{5,4},{6,5},{7,6},{8,11},{9,8},{10,9... | collective-permute-start | bytes 786440 | tf_op jit(solution)/shard_map/ppermute | solution.py:27
  60.9 0.9 collective-permute-done.12.own
  61.8 14.2 %collective-permute-done.13.other = bf16[2,128,512]{2,1,0:T(8,128)(2,1)S(1)} collective-permute-done((bf16[2,128,512]{2,1,0:T(8,128)(2,1)S(1)}, bf16[2,128,512]{2,1,0:T(8,128)(2,1)S(1)}, u32[]{:S(2)}, u32[]{:S(2)}) %collective-permute-start.13) | collective-permute-done | bytes 262176 | tf_op jit(solution)/shard_map/ppermute | solution.py:27
  75.9 0.1 shard_map.123.refs_1_
  76.1 0.1 collective-permute-start.19
  76.2 1.5 %collective-permute-start.20 = (bf16[2,128,512]{2,1,0:T(8,128)(2,1)S(1)}, bf16[2,128,512]{2,1,0:T(8,128)(2,1)S(1)}, u32[]{:S(2)}, u32[]{:S(2)}) collective-permute-start(bf16[2,128,512]{2,1,0:T(8,128)(2,1)S(1)} %shard_map.123.refs_1_), channel_id=1, source_target_pairs={{0,1},{1,2},{2,3},{3,0},{4,5},{5,6},{6,7},{7,4},{8,9},{9,10},{10,1... | collective-permute-start | bytes 786440 | tf_op jit(solution)/shard_map/ppermute | solution.py:27
  77.6 0.0 collective-permute-done.10.refs_3_
  77.6 0.0 collective-permute-start.21
  77.6 0.0 collective-permute-done.9.refs_2_
  77.6 5.9 %shard_map.124 = (bf16[2,128,512]{2,1,0:T(8,128)(2,1)S(1)}, bf16[2,128,512]{2,1,0:T(8,128)(2,1)S(1)}, bf16[2,128,512]{2,1,0:T(8,128)(2,1)S(1)}, bf16[2,128,512]{2,1,0:T(8,128)(2,1)S(1)}) custom-call(s32[5]{0:T(128)S(1)} %pad_add_fusion.refs_0_, bf16[2,128,512]{2,1,0:T(8,128)(2,1)S(1)} %pad_maximum_fusion.1.refs_1_, ...), custom_call_target="tpu_custom_call" | custom-call | flops 1342177280 | bytes 41943040 | tf_op jit(solution)/shard_map/pallas_call | solution.py:148
  83.5 1.8 %collective-permute-start.16 = (bf16[2,128,512]{2,1,0:T(8,128)(2,1)S(1)}, bf16[2,128,512]{2,1,0:T(8,128)(2,1)S(1)}, u32[]{:S(2)}, u32[]{:S(2)}) collective-permute-start(bf16[2,128,512]{2,1,0:T(8,128)(2,1)S(1)} %get-tuple-element.74), channel_id=1, source_target_pairs={{0,3},{1,0},{2,1},{3,2},{4,7},{5,4},{6,5},{7,6},{8,11},{9,8},{10,9... | collective-permute-start | bytes 786440 | tf_op jit(solution)/shard_map/ppermute | solution.py:27
  85.4 3.9 %collective-permute-done.19.refs_2_ = bf16[2,128,512]{2,1,0:T(8,128)(2,1)S(1)} collective-permute-done((bf16[2,128,512]{2,1,0:T(8,128)(2,1)S(1)}, bf16[2,128,512]{2,1,0:T(8,128)(2,1)S(1)}, u32[]{:S(2)}, u32[]{:S(2)}) %collective-permute-start.19) | collective-permute-done | bytes 262176 | tf_op jit(solution)/shard_map/ppermute | solution.py:27
  89.2 0.1 collective-permute-start.18
  89.3 0.0 collective-permute-done.20.refs_3_
  89.3 1.3 %collective-permute-start.15 = (bf16[128,512]{1,0:T(8,128)(2,1)S(1)}, bf16[128,512]{1,0:T(8,128)(2,1)S(1)}, u32[]{:S(2)}, u32[]{:S(2)}) collective-permute-start(bf16[128,512]{1,0:T(8,128)(2,1)S(1)} %slice_bitcast_fusion.3), channel_id=1, source_target_pairs={{0,4},{1,5},{2,6},{3,7},{4,0},{5,1},{6,2},{7,3},{8,12},{9,13},{10,... | collective-permute-start | bytes 393224 | tf_op jit(solution)/shard_map/ppermute | solution.py:27
  90.7 0.0 collective-permute-done.21.refs_4_
  90.7 5.9 %shard_map.125 = (bf16[2,128,512]{2,1,0:T(8,128)(2,1)S(1)}, bf16[2,128,512]{2,1,0:T(8,128)(2,1)S(1)}, bf16[2,128,512]{2,1,0:T(8,128)(2,1)S(1)}, bf16[2,128,512]{2,1,0:T(8,128)(2,1)S(1)}) custom-call(s32[5]{0:T(128)S(1)} %pad_add_fusion.refs_0_, bf16[2,128,512]{2,1,0:T(8,128)(2,1)S(1)} %shard_map.123.refs_1_, ...), custom_call_target="tpu_custom_call" | custom-call | flops 1342177280 | bytes 41943040 | tf_op jit(solution)/shard_map/pallas_call | solution.py:148
  96.6 0.4 collective-permute-start.25
  96.9 0.1 collective-permute-done.15
  97.0 1.1 collective-permute-start.26
  98.1 2.3 %collective-permute-done.16 = bf16[2,128,512]{2,1,0:T(8,128)(2,1)S(1)} collective-permute-done((bf16[2,128,512]{2,1,0:T(8,128)(2,1)S(1)}, bf16[2,128,512]{2,1,0:T(8,128)(2,1)S(1)}, u32[]{:S(2)}, u32[]{:S(2)}) %collective-permute-start.16) | collective-permute-done | bytes 262176 | tf_op jit(solution)/shard_map/ppermute | solution.py:27
  100.4 0.5 collective-permute-start.27
  101.0 0.1 convert_add_fusion.1
  101.1 5.3 %collective-permute-start.23 = (bf16[128,512]{1,0:T(8,128)(2,1)S(1)}, bf16[128,512]{1,0:T(8,128)(2,1)S(1)}, u32[]{:S(2)}, u32[]{:S(2)}) collective-permute-start(bf16[128,512]{1,0:T(8,128)(2,1)S(1)} %fusion.10), channel_id=1, source_target_pairs={{0,4},{1,5},{2,6},{3,7},{4,0},{5,1},{6,2},{7,3},{8,12},{9,13},{10,... | collective-permute-start | bytes 393224 | tf_op jit(solution)/shard_map/ppermute | solution.py:27
  106.5 6.6 %collective-permute-start.22 = (bf16[128,512]{1,0:T(8,128)(2,1)S(1)}, bf16[128,512]{1,0:T(8,128)(2,1)S(1)}, u32[]{:S(2)}, u32[]{:S(2)}) collective-permute-start(bf16[128,512]{1,0:T(8,128)(2,1)S(1)} %fusion.5), channel_id=1, source_target_pairs={{0,8},{1,9},{2,10},{3,11},{4,12},{5,13},{6,14},{7,15},{8,16},{9,17... | collective-permute-start | bytes 393224 | tf_op jit(solution)/shard_map/ppermute | solution.py:27
  113.2 0.0 collective-permute-done.23
  113.2 10.3 %collective-permute-start.24 = (bf16[128,512]{1,0:T(8,128)(2,1)S(1)}, bf16[128,512]{1,0:T(8,128)(2,1)S(1)}, u32[]{:S(2)}, u32[]{:S(2)}) collective-permute-start(bf16[128,512]{1,0:T(8,128)(2,1)S(1)} %fusion.3), channel_id=1, source_target_pairs={{0,8},{1,9},{2,10},{3,11},{4,12},{5,13},{6,14},{7,15},{8,16},{9,17... | collective-permute-start | bytes 393224 | tf_op jit(solution)/shard_map/ppermute | solution.py:27
  123.5 0.0 collective-permute-done.27
  123.5 0.1 convert_add_fusion
  123.7 0.1 collective-permute-start.28
  123.8 1.7 %collective-permute-done.24 = bf16[128,512]{1,0:T(8,128)(2,1)S(1)} collective-permute-done((bf16[128,512]{1,0:T(8,128)(2,1)S(1)}, bf16[128,512]{1,0:T(8,128)(2,1)S(1)}, u32[]{:S(2)}, u32[]{:S(2)}) %collective-permute-start.24) | collective-permute-done | bytes 131104 | tf_op jit(solution)/shard_map/ppermute | solution.py:27
  125.5 0.1 fusion.7
  125.7 0.8 maximum_bitcast_fusion
  126.4 5.0 %collective-permute-done.28 = bf16[128,512]{1,0:T(8,128)(2,1)S(1)} collective-permute-done((bf16[128,512]{1,0:T(8,128)(2,1)S(1)}, bf16[128,512]{1,0:T(8,128)(2,1)S(1)}, u32[]{:S(2)}, u32[]{:S(2)}) %collective-permute-start.28) | collective-permute-done | bytes 131104 | tf_op jit(solution)/shard_map/ppermute | solution.py:27
  131.5 0.8 maximum_bitcast_fusion.1
  (36 shorter events, 0.3 us)
Async XLA Ops:
  0.6 11.9 %copy-start.3 = (bf16[1,128,512]{2,1,0:T(8,128)(2,1)S(1)}, bf16[1,128,512]{2,1,0:T(8,128)(2,1)}, u32[]{:S(2)}) copy-start(bf16[1,128,512]{2,1,0:T(8,128)(2,1)} %param.11) | copy-start | bytes 393220
  0.6 25.5 %copy-start.2 = (bf16[1,4096]{1,0:T(2,128)(2,1)S(1)}, bf16[1,4096]{1,0:T(2,128)(2,1)}, u32[]{:S(2)}) copy-start(bf16[1,4096]{1,0:T(2,128)(2,1)} %refs_5_.5) | copy-start | bytes 24580
  0.7 25.5 %copy-start = (bf16[1,3,512,128]{3,2,1,0:T(8,128)(2,1)S(1)}, bf16[1,3,512,128]{3,2,1,0:T(8,128)(2,1)}, u32[]{:S(2)}) copy-start(bf16[1,3,512,128]{3,2,1,0:T(8,128)(2,1)} %refs_11_.5) | copy-start | bytes 1179652
  0.7 25.5 %copy-start.1 = (bf16[1,3,512,128]{3,2,1,0:T(8,128)(2,1)S(1)}, bf16[1,3,512,128]{3,2,1,0:T(8,128)(2,1)}, u32[]{:S(2)}) copy-start(bf16[1,3,512,128]{3,2,1,0:T(8,128)(2,1)} %refs_12_.5) | copy-start | bytes 1179652
  0.7 11.9 %collective-permute-start = (bf16[128,512]{1,0:T(8,128)(2,1)}, bf16[128,512]{1,0:T(8,128)(2,1)S(1)}, u32[]{:S(2)}, u32[]{:S(2)}) collective-permute-start(bf16[128,512]{1,0:T(8,128)(2,1)} %bitcast.89), channel_id=1, source_target_pairs={{0,4},{1,5},{2,6},{3,7},{4,0},{5,1},{6,2},{7,3},{8,12},{9,13},{10,... | collective-permute-start | bytes 393224 | tf_op jit(solution)/shard_map/ppermute | solution.py:27
  12.6 6.9 %collective-permute-start.1 = (bf16[2,128,512]{2,1,0:T(8,128)(2,1)S(1)}, bf16[2,128,512]{2,1,0:T(8,128)(2,1)S(1)}, u32[]{:S(2)}, u32[]{:S(2)}) collective-permute-start(bf16[2,128,512]{2,1,0:T(8,128)(2,1)S(1)} %pad_maximum_fusion.refs_1_), channel_id=1, source_target_pairs={{0,3},{1,0},{2,1},{3,2},{4,7},{5,4},{6,5},{7,6},{8,11},{9,8},{10,9... | collective-permute-start | bytes 786440 | tf_op jit(solution)/shard_map/ppermute | solution.py:27
  12.9 8.1 %collective-permute-start.2 = (bf16[2,128,512]{2,1,0:T(8,128)(2,1)S(1)}, bf16[2,128,512]{2,1,0:T(8,128)(2,1)S(1)}, u32[]{:S(2)}, u32[]{:S(2)}) collective-permute-start(bf16[2,128,512]{2,1,0:T(8,128)(2,1)S(1)} %pad_maximum_fusion.refs_1_), channel_id=1, source_target_pairs={{0,1},{1,2},{2,3},{3,0},{4,5},{5,6},{6,7},{7,4},{8,9},{9,10},{10,1... | collective-permute-start | bytes 786440 | tf_op jit(solution)/shard_map/ppermute | solution.py:27
  14.2 12.0 %collective-permute-start.3 = (bf16[2,128,512]{2,1,0:T(8,128)(2,1)S(1)}, bf16[2,128,512]{2,1,0:T(8,128)(2,1)S(1)}, u32[]{:S(2)}, u32[]{:S(2)}) collective-permute-start(bf16[2,128,512]{2,1,0:T(8,128)(2,1)S(1)} %pad_maximum_fusion.refs_1_), channel_id=1, source_target_pairs={{0,2},{1,3},{2,0},{3,1},{4,6},{5,7},{6,4},{7,5},{8,10},{9,11},{10,... | collective-permute-start | bytes 786440 | tf_op jit(solution)/shard_map/ppermute | solution.py:27
  26.2 9.8 %copy-start.4 = (bf16[2,128,512]{2,1,0:T(8,128)(2,1)S(1)}, bf16[2,128,512]{2,1,0:T(8,128)(2,1)}, u32[]{:S(2)}) copy-start(bf16[2,128,512]{2,1,0:T(8,128)(2,1)} %param.13) | copy-start | bytes 786436
  26.2 9.8 %copy-start.6 = (bf16[1,128,512]{2,1,0:T(8,128)(2,1)S(1)}, bf16[1,128,512]{2,1,0:T(8,128)(2,1)}, u32[]{:S(2)}) copy-start(bf16[1,128,512]{2,1,0:T(8,128)(2,1)} %param.12) | copy-start | bytes 393220
  26.2 17.8 %copy-start.5 = (bf16[2,128,512]{2,1,0:T(8,128)(2,1)S(1)}, bf16[2,128,512]{2,1,0:T(8,128)(2,1)}, u32[]{:S(2)}) copy-start(bf16[2,128,512]{2,1,0:T(8,128)(2,1)} %param.14) | copy-start | bytes 786436
  32.1 11.9 %collective-permute-start.6 = (bf16[2,128,512]{2,1,0:T(8,128)(2,1)S(1)}, bf16[2,128,512]{2,1,0:T(8,128)(2,1)S(1)}, u32[]{:S(2)}, u32[]{:S(2)}) collective-permute-start(bf16[2,128,512]{2,1,0:T(8,128)(2,1)S(1)} %get-tuple-element.56), channel_id=1, source_target_pairs={{0,3},{1,0},{2,1},{3,2},{4,7},{5,4},{6,5},{7,6},{8,11},{9,8},{10,9... | collective-permute-start | bytes 786440 | tf_op jit(solution)/shard_map/ppermute | solution.py:27
  34.0 10.0 %collective-permute-start.7 = (bf16[2,128,512]{2,1,0:T(8,128)(2,1)S(1)}, bf16[2,128,512]{2,1,0:T(8,128)(2,1)S(1)}, u32[]{:S(2)}, u32[]{:S(2)}) collective-permute-start(bf16[2,128,512]{2,1,0:T(8,128)(2,1)S(1)} %get-tuple-element.54), channel_id=1, source_target_pairs={{0,1},{1,2},{2,3},{3,0},{4,5},{5,6},{6,7},{7,4},{8,9},{9,10},{10,1... | collective-permute-start | bytes 786440 | tf_op jit(solution)/shard_map/ppermute | solution.py:27
  34.0 11.0 %collective-permute-start.8 = (bf16[2,128,512]{2,1,0:T(8,128)(2,1)S(1)}, bf16[2,128,512]{2,1,0:T(8,128)(2,1)S(1)}, u32[]{:S(2)}, u32[]{:S(2)}) collective-permute-start(bf16[2,128,512]{2,1,0:T(8,128)(2,1)S(1)} %get-tuple-element.55), channel_id=1, source_target_pairs={{0,2},{1,3},{2,0},{3,1},{4,6},{5,7},{6,4},{7,5},{8,10},{9,11},{10,... | collective-permute-start | bytes 786440 | tf_op jit(solution)/shard_map/ppermute | solution.py:27
  36.0 9.2 %collective-permute-start.4 = (bf16[128,512]{1,0:T(8,128)(2,1)S(1)}, bf16[128,512]{1,0:T(8,128)(2,1)S(1)}, u32[]{:S(2)}, u32[]{:S(2)}) collective-permute-start(bf16[128,512]{1,0:T(8,128)(2,1)S(1)} %fusion.8), channel_id=1, source_target_pairs={{0,8},{1,9},{2,10},{3,11},{4,12},{5,13},{6,14},{7,15},{8,16},{9,17... | collective-permute-start | bytes 393224 | tf_op jit(solution)/shard_map/ppermute | solution.py:27
  40.7 8.6 %collective-permute-start.5 = (bf16[128,512]{1,0:T(8,128)(2,1)S(1)}, bf16[128,512]{1,0:T(8,128)(2,1)S(1)}, u32[]{:S(2)}, u32[]{:S(2)}) collective-permute-start(bf16[128,512]{1,0:T(8,128)(2,1)S(1)} %fusion.8), channel_id=1, source_target_pairs={{0,12},{1,13},{2,14},{3,15},{4,8},{5,9},{6,10},{7,11},{8,20},{9,21... | collective-permute-start | bytes 393224 | tf_op jit(solution)/shard_map/ppermute | solution.py:27
  49.4 10.0 %collective-permute-start.14 = (bf16[2,128,512]{2,1,0:T(8,128)(2,1)S(1)}, bf16[2,128,512]{2,1,0:T(8,128)(2,1)S(1)}, u32[]{:S(2)}, u32[]{:S(2)}) collective-permute-start(bf16[2,128,512]{2,1,0:T(8,128)(2,1)S(1)} %pad_maximum_fusion.1.refs_1_), channel_id=1, source_target_pairs={{0,8},{1,9},{2,10},{3,11},{4,12},{5,13},{6,14},{7,15},{8,16},{9,17... | collective-permute-start | bytes 786440 | tf_op jit(solution)/shard_map/ppermute | solution.py:27
  52.8 9.0 %collective-permute-start.12 = (bf16[2,128,512]{2,1,0:T(8,128)(2,1)S(1)}, bf16[2,128,512]{2,1,0:T(8,128)(2,1)S(1)}, u32[]{:S(2)}, u32[]{:S(2)}) collective-permute-start(bf16[2,128,512]{2,1,0:T(8,128)(2,1)S(1)} %get-tuple-element.94), channel_id=1, source_target_pairs={{0,16},{1,17},{2,18},{3,19},{4,20},{5,21},{6,22},{7,23},{8,24},{9,... | collective-permute-start | bytes 786440 | tf_op jit(solution)/shard_map/ppermute | solution.py:27
  55.0 20.9 %collective-permute-start.13 = (bf16[2,128,512]{2,1,0:T(8,128)(2,1)S(1)}, bf16[2,128,512]{2,1,0:T(8,128)(2,1)S(1)}, u32[]{:S(2)}, u32[]{:S(2)}) collective-permute-start(bf16[2,128,512]{2,1,0:T(8,128)(2,1)S(1)} %get-tuple-element.94), channel_id=1, source_target_pairs={{0,20},{1,21},{2,22},{3,23},{4,16},{5,17},{6,18},{7,19},{8,28},{9,... | collective-permute-start | bytes 786440 | tf_op jit(solution)/shard_map/ppermute | solution.py:27
  59.4 18.2 %collective-permute-start.10 = (bf16[2,128,512]{2,1,0:T(8,128)(2,1)S(1)}, bf16[2,128,512]{2,1,0:T(8,128)(2,1)S(1)}, u32[]{:S(2)}, u32[]{:S(2)}) collective-permute-start(bf16[2,128,512]{2,1,0:T(8,128)(2,1)S(1)} %pad_maximum_fusion.1.refs_1_), channel_id=1, source_target_pairs={{0,1},{1,2},{2,3},{3,0},{4,5},{5,6},{6,7},{7,4},{8,9},{9,10},{10,1... | collective-permute-start | bytes 786440 | tf_op jit(solution)/shard_map/ppermute | solution.py:27
  59.4 18.2 %collective-permute-start.11 = (bf16[2,128,512]{2,1,0:T(8,128)(2,1)S(1)}, bf16[2,128,512]{2,1,0:T(8,128)(2,1)S(1)}, u32[]{:S(2)}, u32[]{:S(2)}) collective-permute-start(bf16[2,128,512]{2,1,0:T(8,128)(2,1)S(1)} %pad_maximum_fusion.1.refs_1_), channel_id=1, source_target_pairs={{0,2},{1,3},{2,0},{3,1},{4,6},{5,7},{6,4},{7,5},{8,10},{9,11},{10,... | collective-permute-start | bytes 786440 | tf_op jit(solution)/shard_map/ppermute | solution.py:27
  59.4 18.2 %collective-permute-start.9 = (bf16[2,128,512]{2,1,0:T(8,128)(2,1)S(1)}, bf16[2,128,512]{2,1,0:T(8,128)(2,1)S(1)}, u32[]{:S(2)}, u32[]{:S(2)}) collective-permute-start(bf16[2,128,512]{2,1,0:T(8,128)(2,1)S(1)} %pad_maximum_fusion.1.refs_1_), channel_id=1, source_target_pairs={{0,3},{1,0},{2,1},{3,2},{4,7},{5,4},{6,5},{7,6},{8,11},{9,8},{10,9... | collective-permute-start | bytes 786440 | tf_op jit(solution)/shard_map/ppermute | solution.py:27
  76.1 13.1 %collective-permute-start.19 = (bf16[2,128,512]{2,1,0:T(8,128)(2,1)S(1)}, bf16[2,128,512]{2,1,0:T(8,128)(2,1)S(1)}, u32[]{:S(2)}, u32[]{:S(2)}) collective-permute-start(bf16[2,128,512]{2,1,0:T(8,128)(2,1)S(1)} %shard_map.123.refs_1_), channel_id=1, source_target_pairs={{0,3},{1,0},{2,1},{3,2},{4,7},{5,4},{6,5},{7,6},{8,11},{9,8},{10,9... | collective-permute-start | bytes 786440 | tf_op jit(solution)/shard_map/ppermute | solution.py:27
  76.2 13.2 %collective-permute-start.20 = (bf16[2,128,512]{2,1,0:T(8,128)(2,1)S(1)}, bf16[2,128,512]{2,1,0:T(8,128)(2,1)S(1)}, u32[]{:S(2)}, u32[]{:S(2)}) collective-permute-start(bf16[2,128,512]{2,1,0:T(8,128)(2,1)S(1)} %shard_map.123.refs_1_), channel_id=1, source_target_pairs={{0,1},{1,2},{2,3},{3,0},{4,5},{5,6},{6,7},{7,4},{8,9},{9,10},{10,1... | collective-permute-start | bytes 786440 | tf_op jit(solution)/shard_map/ppermute | solution.py:27
  77.6 13.1 %collective-permute-start.21 = (bf16[2,128,512]{2,1,0:T(8,128)(2,1)S(1)}, bf16[2,128,512]{2,1,0:T(8,128)(2,1)S(1)}, u32[]{:S(2)}, u32[]{:S(2)}) collective-permute-start(bf16[2,128,512]{2,1,0:T(8,128)(2,1)S(1)} %shard_map.123.refs_1_), channel_id=1, source_target_pairs={{0,2},{1,3},{2,0},{3,1},{4,6},{5,7},{6,4},{7,5},{8,10},{9,11},{10,... | collective-permute-start | bytes 786440 | tf_op jit(solution)/shard_map/ppermute | solution.py:27
  83.5 16.9 %collective-permute-start.16 = (bf16[2,128,512]{2,1,0:T(8,128)(2,1)S(1)}, bf16[2,128,512]{2,1,0:T(8,128)(2,1)S(1)}, u32[]{:S(2)}, u32[]{:S(2)}) collective-permute-start(bf16[2,128,512]{2,1,0:T(8,128)(2,1)S(1)} %get-tuple-element.74), channel_id=1, source_target_pairs={{0,3},{1,0},{2,1},{3,2},{4,7},{5,4},{6,5},{7,6},{8,11},{9,8},{10,9... | collective-permute-start | bytes 786440 | tf_op jit(solution)/shard_map/ppermute | solution.py:27
  85.3 15.6 %collective-permute-start.17 = (bf16[2,128,512]{2,1,0:T(8,128)(2,1)S(1)}, bf16[2,128,512]{2,1,0:T(8,128)(2,1)S(1)}, u32[]{:S(2)}, u32[]{:S(2)}) collective-permute-start(bf16[2,128,512]{2,1,0:T(8,128)(2,1)S(1)} %get-tuple-element.75), channel_id=1, source_target_pairs={{0,1},{1,2},{2,3},{3,0},{4,5},{5,6},{6,7},{7,4},{8,9},{9,10},{10,1... | collective-permute-start | bytes 786440 | tf_op jit(solution)/shard_map/ppermute | solution.py:27
  89.2 11.8 %collective-permute-start.18 = (bf16[2,128,512]{2,1,0:T(8,128)(2,1)S(1)}, bf16[2,128,512]{2,1,0:T(8,128)(2,1)S(1)}, u32[]{:S(2)}, u32[]{:S(2)}) collective-permute-start(bf16[2,128,512]{2,1,0:T(8,128)(2,1)S(1)} %get-tuple-element.76), channel_id=1, source_target_pairs={{0,2},{1,3},{2,0},{3,1},{4,6},{5,7},{6,4},{7,5},{8,10},{9,11},{10,... | collective-permute-start | bytes 786440 | tf_op jit(solution)/shard_map/ppermute | solution.py:27
  89.3 7.7 %collective-permute-start.15 = (bf16[128,512]{1,0:T(8,128)(2,1)S(1)}, bf16[128,512]{1,0:T(8,128)(2,1)S(1)}, u32[]{:S(2)}, u32[]{:S(2)}) collective-permute-start(bf16[128,512]{1,0:T(8,128)(2,1)S(1)} %slice_bitcast_fusion.3), channel_id=1, source_target_pairs={{0,4},{1,5},{2,6},{3,7},{4,0},{5,1},{6,2},{7,3},{8,12},{9,13},{10,... | collective-permute-start | bytes 393224 | tf_op jit(solution)/shard_map/ppermute | solution.py:27
  96.6 26.9 %collective-permute-start.25 = (bf16[2,128,512]{2,1,0:T(8,128)(2,1)S(1)}, bf16[2,128,512]{2,1,0:T(8,128)(2,1)S(1)}, u32[]{:S(2)}, u32[]{:S(2)}) collective-permute-start(bf16[2,128,512]{2,1,0:T(8,128)(2,1)S(1)} %get-tuple-element.84), channel_id=1, source_target_pairs={{0,3},{1,0},{2,1},{3,2},{4,7},{5,4},{6,5},{7,6},{8,11},{9,8},{10,9... | collective-permute-start | bytes 786440 | tf_op jit(solution)/shard_map/ppermute | solution.py:27
  97.0 26.5 %collective-permute-start.26 = (bf16[2,128,512]{2,1,0:T(8,128)(2,1)S(1)}, bf16[2,128,512]{2,1,0:T(8,128)(2,1)S(1)}, u32[]{:S(2)}, u32[]{:S(2)}) collective-permute-start(bf16[2,128,512]{2,1,0:T(8,128)(2,1)S(1)} %get-tuple-element.82), channel_id=1, source_target_pairs={{0,1},{1,2},{2,3},{3,0},{4,5},{5,6},{6,7},{7,4},{8,9},{9,10},{10,1... | collective-permute-start | bytes 786440 | tf_op jit(solution)/shard_map/ppermute | solution.py:27
  100.4 23.1 %collective-permute-start.27 = (bf16[2,128,512]{2,1,0:T(8,128)(2,1)S(1)}, bf16[2,128,512]{2,1,0:T(8,128)(2,1)S(1)}, u32[]{:S(2)}, u32[]{:S(2)}) collective-permute-start(bf16[2,128,512]{2,1,0:T(8,128)(2,1)S(1)} %get-tuple-element.83), channel_id=1, source_target_pairs={{0,2},{1,3},{2,0},{3,1},{4,6},{5,7},{6,4},{7,5},{8,10},{9,11},{10,... | collective-permute-start | bytes 786440 | tf_op jit(solution)/shard_map/ppermute | solution.py:27
  101.1 12.0 %collective-permute-start.23 = (bf16[128,512]{1,0:T(8,128)(2,1)S(1)}, bf16[128,512]{1,0:T(8,128)(2,1)S(1)}, u32[]{:S(2)}, u32[]{:S(2)}) collective-permute-start(bf16[128,512]{1,0:T(8,128)(2,1)S(1)} %fusion.10), channel_id=1, source_target_pairs={{0,4},{1,5},{2,6},{3,7},{4,0},{5,1},{6,2},{7,3},{8,12},{9,13},{10,... | collective-permute-start | bytes 393224 | tf_op jit(solution)/shard_map/ppermute | solution.py:27
  106.5 17.3 %collective-permute-start.22 = (bf16[128,512]{1,0:T(8,128)(2,1)S(1)}, bf16[128,512]{1,0:T(8,128)(2,1)S(1)}, u32[]{:S(2)}, u32[]{:S(2)}) collective-permute-start(bf16[128,512]{1,0:T(8,128)(2,1)S(1)} %fusion.5), channel_id=1, source_target_pairs={{0,8},{1,9},{2,10},{3,11},{4,12},{5,13},{6,14},{7,15},{8,16},{9,17... | collective-permute-start | bytes 393224 | tf_op jit(solution)/shard_map/ppermute | solution.py:27
  113.2 12.3 %collective-permute-start.24 = (bf16[128,512]{1,0:T(8,128)(2,1)S(1)}, bf16[128,512]{1,0:T(8,128)(2,1)S(1)}, u32[]{:S(2)}, u32[]{:S(2)}) collective-permute-start(bf16[128,512]{1,0:T(8,128)(2,1)S(1)} %fusion.3), channel_id=1, source_target_pairs={{0,8},{1,9},{2,10},{3,11},{4,12},{5,13},{6,14},{7,15},{8,16},{9,17... | collective-permute-start | bytes 393224 | tf_op jit(solution)/shard_map/ppermute | solution.py:27
  123.7 7.8 %collective-permute-start.28 = (bf16[128,512]{1,0:T(8,128)(2,1)S(1)}, bf16[128,512]{1,0:T(8,128)(2,1)S(1)}, u32[]{:S(2)}, u32[]{:S(2)}) collective-permute-start(bf16[128,512]{1,0:T(8,128)(2,1)S(1)} %fusion.12), channel_id=1, source_target_pairs={{0,4},{1,5},{2,6},{3,7},{4,0},{5,1},{6,2},{7,3},{8,12},{9,13},{10,... | collective-permute-start | bytes 393224 | tf_op jit(solution)/shard_map/ppermute | solution.py:27

commit v3 on v2

--- a/solution.py
+++ b/solution.py
@@ -240,16 +240,17 @@
             wq, wkv, wo, keys_cache, values_cache,
         )
 
+    early = after(block_last, all0[1])
+    other1 = jnp.where(final, incoming_two[0], add(x0, early[0]))
+    z1 = send(other1, hop(1, True))
+
     parts0 = block(0, all0)
     got0 = exchange(parts0)
-    block_late, enter_two, enter_last = after(
-        (block_last, incoming_two, incoming_last), parts0
-    )
-    out1 = jnp.where(final, enter_two[0], add(x0, block_late[0]))
-    a1, z1 = send(out1, hop(1)), send(out1, hop(1, True))
+    own1, enter_two, enter_last = after((other1, incoming_two, incoming_last), parts0)
+    a1 = send(own1, hop(1))
     local = jnp.where(first, enter_two[1], enter_last[0])
     entering = jnp.where(final, enter_last[0], enter_two[1])
-    got0, local, entering = lax.optimization_barrier((got0, local, entering))
+    got0, local, entering, a1 = lax.optimization_barrier((got0, local, entering, a1))
     sums0 = sum(g.astype(f32) for g in got0).astype(bf16)
     out2 = jnp.where(sid >= last - 1, entering[None], sums0)
     own, other = send(out2, hop(2)), send(out2, hop(2, True))
@@ -260,21 +261,23 @@
     all1 = gather(pair1)
     pair2 = combine(sid.astype(jnp.int32)[None], own, other, base, local)
     all2 = gather(pair2)
-    late0, all1 = after((sums0, all1), pair2)
-    swapped0 = send(late0[1], hop(0, True))
-    parts1 = block(1, all1)
+    parts1 = block(1, after(all1, pair2))
     got1 = exchange(parts1)
     parts2 = block(2, after(all2, parts1))
-    swapped0, got1 = after((swapped0, got1), parts2)
+    sums0, got1 = after((sums0, got1), parts2)
     got2 = lax.optimization_barrier(exchange(parts2))
-
+    mine2, theirs2 = halves(got2)
+
+    swapped0 = send(sums0[1], hop(0, True))
     mine1, theirs1 = halves(got1)
-    b1 = (mine1 + send(theirs1, hop(0, True)).astype(f32)).astype(bf16)
-    b0 = add(late0[0], swapped0)
+    swapped1 = send(theirs1, hop(0, True))
+    swapped0, swapped1 = after((swapped0, swapped1), theirs2)
+    b0 = add(sums0[0], swapped0)
+    b1 = (mine1 + swapped1.astype(f32)).astype(bf16)
     s0 = add(x0, block_last[0])
-    t1 = add(a1, jnp.where(first, incoming_last[0], send(b0, hop(1))))
-    t2 = add(pair2[0], jnp.where(first, incoming_last[1], send(b1, hop(1))))
-    mine2, theirs2 = halves(got2)
+    back = send(jnp.stack([b0, b1]), hop(1))
+    t1 = add(a1, jnp.where(first, incoming_last[0], back[0]))
+    t2 = add(pair2[0], jnp.where(first, incoming_last[1], back[1]))
     b2 = (mine2 + send(theirs2, hop(0, True)).astype(f32)).astype(bf16)
     return jnp.stack([s0, t1, t2])[None], jnp.stack([b0, b1, b2])[None]
 

time: 132 us -> 125 us (0.947)
  the two profiles are of different devices: /device:TPU:15 before, /device:TPU:16 now
where the time goes in v3:
time: 125 us
  starting transfers between devices  52.3 us (42%)
  waiting for transfers between devices  46.5 us (37%)
  Pallas kernels  17.7 us (14%)
  local copies, waits for them, and re-layouts  4.03 us (3%)
  other arithmetic  3.35 us (3%)
    ppermute x28, starting transfers between devices, move(): return lax.ppermute(value, ('section', 'tensor'), pairs)  52.3 us
    ppermute x28, waiting for transfers between devices, move(): return lax.ppermute(value, ('section', 'tensor'), pairs)  46.5 us
    pallas_call x3, Pallas kernels, attend(): pl.pallas_call(functools.partial(attend_kernel, tick), out_shape=out_shap...  17.5 us
    unnamed x15, local copies, waits for them, and re-layouts  3.25 us
  transfers between devices with their start and end apart: 28, of which 12 were waited for; matrix products, arithmetic and copies ran while one was open for 5% of the time, Pallas kernels for 9%

profile of v3, /device:TPU:16, one launch (start us, length us, event | category | flops | bytes accessed | tf_op | source)
XLA Modules:
  0.0 124.8 jit_solution(14052044162885960297)
XLA Ops:
  0.7 7.3 %collective-permute-start = (bf16[128,512]{1,0:T(8,128)(2,1)}, bf16[128,512]{1,0:T(8,128)(2,1)S(1)}, u32[]{:S(2)}, u32[]{:S(2)}) collective-permute-start(bf16[128,512]{1,0:T(8,128)(2,1)} %bitcast.82), channel_id=1, source_target_pairs={{0,4},{1,5},{2,6},{3,7},{4,0},{5,1},{6,2},{7,3},{8,12},{9,13},{10,... | collective-permute-start | bytes 393224 | tf_op jit(solution)/shard_map/ppermute | solution.py:27
  8.0 0.7 dynamic_slice.3
  8.7 0.1 add_convert_fusion.3
  8.8 0.8 multiply_sine_fusion
  9.5 3.2 %copy.15 = bf16[512,8,2,128]{3,1,2,0:T(8,128)(2,1)} copy(bf16[512,8,2,128]{3,2,1,0:T(2,128)(2,1)} %bitcast.81) | data formatting | bytes 4194304
  12.8 0.1 pad_add_fusion.refs_0_
  12.8 0.0 collective-permute-done
  12.9 0.5 collective-permute-start.1
  13.4 1.6 %collective-permute-start.2 = (bf16[2,128,512]{2,1,0:T(8,128)(2,1)S(1)}, bf16[2,128,512]{2,1,0:T(8,128)(2,1)S(1)}, u32[]{:S(2)}, u32[]{:S(2)}) collective-permute-start(bf16[2,128,512]{2,1,0:T(8,128)(2,1)S(1)} %pad_maximum_fusion.refs_1_), channel_id=1, source_target_pairs={{0,1},{1,2},{2,3},{3,0},{4,5},{5,6},{6,7},{7,4},{8,9},{9,10},{10,1... | collective-permute-start | bytes 786440 | tf_op jit(solution)/shard_map/ppermute | solution.py:27
  15.0 1.3 %collective-permute-start.3 = (bf16[2,128,512]{2,1,0:T(8,128)(2,1)S(1)}, bf16[2,128,512]{2,1,0:T(8,128)(2,1)S(1)}, u32[]{:S(2)}, u32[]{:S(2)}) collective-permute-start(bf16[2,128,512]{2,1,0:T(8,128)(2,1)S(1)} %pad_maximum_fusion.refs_1_), channel_id=1, source_target_pairs={{0,2},{1,3},{2,0},{3,1},{4,6},{5,7},{6,4},{7,5},{8,10},{9,11},{10,... | collective-permute-start | bytes 786440 | tf_op jit(solution)/shard_map/ppermute | solution.py:27
  16.3 5.9 %collective-permute-done.1.refs_2_ = bf16[2,128,512]{2,1,0:T(8,128)(2,1)S(1)} collective-permute-done((bf16[2,128,512]{2,1,0:T(8,128)(2,1)S(1)}, bf16[2,128,512]{2,1,0:T(8,128)(2,1)S(1)}, u32[]{:S(2)}, u32[]{:S(2)}) %collective-permute-start.1) | collective-permute-done | bytes 262176 | tf_op jit(solution)/shard_map/ppermute | solution.py:27
  22.2 0.0 collective-permute-done.2.refs_3_
  22.2 5.5 %collective-permute-done.3.refs_4_ = bf16[2,128,512]{2,1,0:T(8,128)(2,1)S(1)} collective-permute-done((bf16[2,128,512]{2,1,0:T(8,128)(2,1)S(1)}, bf16[2,128,512]{2,1,0:T(8,128)(2,1)S(1)}, u32[]{:S(2)}, u32[]{:S(2)}) %collective-permute-start.3) | collective-permute-done | bytes 262176 | tf_op jit(solution)/shard_map/ppermute | solution.py:27
  27.7 0.0 copy-start.4
  27.7 0.0 copy-start.6
  27.7 0.0 copy-start.5
  27.7 5.9 %shard_map.122 = (bf16[2,128,512]{2,1,0:T(8,128)(2,1)S(1)}, bf16[2,128,512]{2,1,0:T(8,128)(2,1)S(1)}, bf16[2,128,512]{2,1,0:T(8,128)(2,1)S(1)}, bf16[2,128,512]{2,1,0:T(8,128)(2,1)S(1)}) custom-call(s32[5]{0:T(128)S(1)} %pad_add_fusion.refs_0_, bf16[2,128,512]{2,1,0:T(8,128)(2,1)S(1)} %pad_maximum_fusion.refs_1_, ...), custom_call_target="tpu_custom_call" | custom-call | flops 1342177280 | bytes 41943040 | tf_op jit(solution)/shard_map/pallas_call | solution.py:148
  33.6 0.2 collective-permute-start.4
  33.8 1.9 %collective-permute-start.5 = (bf16[2,128,512]{2,1,0:T(8,128)(2,1)S(1)}, bf16[2,128,512]{2,1,0:T(8,128)(2,1)S(1)}, u32[]{:S(2)}, u32[]{:S(2)}) collective-permute-start(bf16[2,128,512]{2,1,0:T(8,128)(2,1)S(1)} %get-tuple-element.58), channel_id=1, source_target_pairs={{0,1},{1,2},{2,3},{3,0},{4,5},{5,6},{6,7},{7,4},{8,9},{9,10},{10,1... | collective-permute-start | bytes 786440 | tf_op jit(solution)/shard_map/ppermute | solution.py:27
  35.7 3.0 %collective-permute-start.6 = (bf16[2,128,512]{2,1,0:T(8,128)(2,1)S(1)}, bf16[2,128,512]{2,1,0:T(8,128)(2,1)S(1)}, u32[]{:S(2)}, u32[]{:S(2)}) collective-permute-start(bf16[2,128,512]{2,1,0:T(8,128)(2,1)S(1)} %get-tuple-element.59), channel_id=1, source_target_pairs={{0,2},{1,3},{2,0},{3,1},{4,6},{5,7},{6,4},{7,5},{8,10},{9,11},{10,... | collective-permute-start | bytes 786440 | tf_op jit(solution)/shard_map/ppermute | solution.py:27
  38.6 0.1 fusion.7
  38.7 0.1 collective-permute-start.8
  38.8 4.9 %collective-permute-start.7 = (bf16[128,512]{1,0:T(8,128)(2,1)S(1)}, bf16[128,512]{1,0:T(8,128)(2,1)S(1)}, u32[]{:S(2)}, u32[]{:S(2)}) collective-permute-start(bf16[128,512]{1,0:T(8,128)(2,1)S(1)} %fusion.7), channel_id=1, source_target_pairs={{0,8},{1,9},{2,10},{3,11},{4,12},{5,13},{6,14},{7,15},{8,16},{9,17... | collective-permute-start | bytes 393224 | tf_op jit(solution)/shard_map/ppermute | solution.py:27
  43.7 6.5 %collective-permute-done.7 = bf16[128,512]{1,0:T(8,128)(2,1)S(1)} collective-permute-done((bf16[128,512]{1,0:T(8,128)(2,1)S(1)}, bf16[128,512]{1,0:T(8,128)(2,1)S(1)}, u32[]{:S(2)}, u32[]{:S(2)}) %collective-permute-start.7) | collective-permute-done | bytes 131104 | tf_op jit(solution)/shard_map/ppermute | solution.py:27
  50.2 0.0 collective-permute-done.4
  50.2 0.0 collective-permute-done.5
  50.2 0.2 broadcast_select_fusion
  50.4 0.1 collective-permute-start.12
  50.5 2.1 %collective-permute-start.13 = (bf16[2,128,512]{2,1,0:T(8,128)(2,1)S(1)}, bf16[2,128,512]{2,1,0:T(8,128)(2,1)S(1)}, u32[]{:S(2)}, u32[]{:S(2)}) collective-permute-start(bf16[2,128,512]{2,1,0:T(8,128)(2,1)S(1)} %get-tuple-element.100), channel_id=1, source_target_pairs={{0,20},{1,21},{2,22},{3,23},{4,16},{5,17},{6,18},{7,19},{8,28},{9,... | collective-permute-start | bytes 786440 | tf_op jit(solution)/shard_map/ppermute | solution.py:27
  52.7 0.1 collective-permute-start.14
  52.8 0.1 collective-permute-start.9
  52.9 2.0 %collective-permute-start.10 = (bf16[2,128,512]{2,1,0:T(8,128)(2,1)S(1)}, bf16[2,128,512]{2,1,0:T(8,128)(2,1)S(1)}, u32[]{:S(2)}, u32[]{:S(2)}) collective-permute-start(bf16[2,128,512]{2,1,0:T(8,128)(2,1)S(1)} %pad_maximum_fusion.1.refs_1_), channel_id=1, source_target_pairs={{0,1},{1,2},{2,3},{3,0},{4,5},{5,6},{6,7},{7,4},{8,9},{9,10},{10,1... | collective-permute-start | bytes 786440 | tf_op jit(solution)/shard_map/ppermute | solution.py:27
  54.9 6.5 %collective-permute-done.12.own = bf16[2,128,512]{2,1,0:T(8,128)(2,1)S(1)} collective-permute-done((bf16[2,128,512]{2,1,0:T(8,128)(2,1)S(1)}, bf16[2,128,512]{2,1,0:T(8,128)(2,1)S(1)}, u32[]{:S(2)}, u32[]{:S(2)}) %collective-permute-start.12) | collective-permute-done | bytes 262176 | tf_op jit(solution)/shard_map/ppermute | solution.py:27
  61.4 3.4 %collective-permute-start.11 = (bf16[2,128,512]{2,1,0:T(8,128)(2,1)S(1)}, bf16[2,128,512]{2,1,0:T(8,128)(2,1)S(1)}, u32[]{:S(2)}, u32[]{:S(2)}) collective-permute-start(bf16[2,128,512]{2,1,0:T(8,128)(2,1)S(1)} %pad_maximum_fusion.1.refs_1_), channel_id=1, source_target_pairs={{0,2},{1,3},{2,0},{3,1},{4,6},{5,7},{6,4},{7,5},{8,10},{9,11},{10,... | collective-permute-start | bytes 786440 | tf_op jit(solution)/shard_map/ppermute | solution.py:27
  64.8 1.0 collective-permute-done.13.other
  65.9 0.1 shard_map.123.refs_1_
  66.0 2.6 %collective-permute-start.18 = (bf16[2,128,512]{2,1,0:T(8,128)(2,1)S(1)}, bf16[2,128,512]{2,1,0:T(8,128)(2,1)S(1)}, u32[]{:S(2)}, u32[]{:S(2)}) collective-permute-start(bf16[2,128,512]{2,1,0:T(8,128)(2,1)S(1)} %shard_map.123.refs_1_), channel_id=1, source_target_pairs={{0,3},{1,0},{2,1},{3,2},{4,7},{5,4},{6,5},{7,6},{8,11},{9,8},{10,9... | collective-permute-start | bytes 786440 | tf_op jit(solution)/shard_map/ppermute | solution.py:27
  68.7 2.9 %collective-permute-start.20 = (bf16[2,128,512]{2,1,0:T(8,128)(2,1)S(1)}, bf16[2,128,512]{2,1,0:T(8,128)(2,1)S(1)}, u32[]{:S(2)}, u32[]{:S(2)}) collective-permute-start(bf16[2,128,512]{2,1,0:T(8,128)(2,1)S(1)} %shard_map.123.refs_1_), channel_id=1, source_target_pairs={{0,2},{1,3},{2,0},{3,1},{4,6},{5,7},{6,4},{7,5},{8,10},{9,11},{10,... | collective-permute-start | bytes 786440 | tf_op jit(solution)/shard_map/ppermute | solution.py:27
  71.6 0.6 collective-permute-done.11.refs_4_
  72.2 5.8 %shard_map.124 = (bf16[2,128,512]{2,1,0:T(8,128)(2,1)S(1)}, bf16[2,128,512]{2,1,0:T(8,128)(2,1)S(1)}, bf16[2,128,512]{2,1,0:T(8,128)(2,1)S(1)}, bf16[2,128,512]{2,1,0:T(8,128)(2,1)S(1)}) custom-call(s32[5]{0:T(128)S(1)} %pad_add_fusion.refs_0_, bf16[2,128,512]{2,1,0:T(8,128)(2,1)S(1)} %pad_maximum_fusion.1.refs_1_, ...), custom_call_target="tpu_custom_call" | custom-call | flops 1342177280 | bytes 41943040 | tf_op jit(solution)/shard_map/pallas_call | solution.py:148
  78.0 2.3 %collective-permute-start.15 = (bf16[2,128,512]{2,1,0:T(8,128)(2,1)S(1)}, bf16[2,128,512]{2,1,0:T(8,128)(2,1)S(1)}, u32[]{:S(2)}, u32[]{:S(2)}) collective-permute-start(bf16[2,128,512]{2,1,0:T(8,128)(2,1)S(1)} %get-tuple-element.78), channel_id=1, source_target_pairs={{0,3},{1,0},{2,1},{3,2},{4,7},{5,4},{6,5},{7,6},{8,11},{9,8},{10,9... | collective-permute-start | bytes 786440 | tf_op jit(solution)/shard_map/ppermute | solution.py:27
  80.3 0.1 collective-permute-start.16
  80.5 3.0 %collective-permute-start.17 = (bf16[2,128,512]{2,1,0:T(8,128)(2,1)S(1)}, bf16[2,128,512]{2,1,0:T(8,128)(2,1)S(1)}, u32[]{:S(2)}, u32[]{:S(2)}) collective-permute-start(bf16[2,128,512]{2,1,0:T(8,128)(2,1)S(1)} %get-tuple-element.80), channel_id=1, source_target_pairs={{0,2},{1,3},{2,0},{3,1},{4,6},{5,7},{6,4},{7,5},{8,10},{9,11},{10,... | collective-permute-start | bytes 786440 | tf_op jit(solution)/shard_map/ppermute | solution.py:27
  83.6 0.9 collective-permute-done.20.refs_4_
  84.4 5.8 %shard_map.125 = (bf16[2,128,512]{2,1,0:T(8,128)(2,1)S(1)}, bf16[2,128,512]{2,1,0:T(8,128)(2,1)S(1)}, bf16[2,128,512]{2,1,0:T(8,128)(2,1)S(1)}, bf16[2,128,512]{2,1,0:T(8,128)(2,1)S(1)}) custom-call(s32[5]{0:T(128)S(1)} %pad_add_fusion.refs_0_, bf16[2,128,512]{2,1,0:T(8,128)(2,1)S(1)} %shard_map.123.refs_1_, ...), custom_call_target="tpu_custom_call" | custom-call | flops 1342177280 | bytes 41943040 | tf_op jit(solution)/shard_map/pallas_call | solution.py:148
  90.3 0.8 collective-permute-start.23
  91.1 1.3 %collective-permute-start.24 = (bf16[2,128,512]{2,1,0:T(8,128)(2,1)S(1)}, bf16[2,128,512]{2,1,0:T(8,128)(2,1)S(1)}, u32[]{:S(2)}, u32[]{:S(2)}) collective-permute-start(bf16[2,128,512]{2,1,0:T(8,128)(2,1)S(1)} %get-tuple-element.86), channel_id=1, source_target_pairs={{0,1},{1,2},{2,3},{3,0},{4,5},{5,6},{6,7},{7,4},{8,9},{9,10},{10,1... | collective-permute-start | bytes 786440 | tf_op jit(solution)/shard_map/ppermute | solution.py:27
  92.4 1.3 %collective-permute-start.25 = (bf16[2,128,512]{2,1,0:T(8,128)(2,1)S(1)}, bf16[2,128,512]{2,1,0:T(8,128)(2,1)S(1)}, u32[]{:S(2)}, u32[]{:S(2)}) collective-permute-start(bf16[2,128,512]{2,1,0:T(8,128)(2,1)S(1)} %get-tuple-element.87), channel_id=1, source_target_pairs={{0,2},{1,3},{2,0},{3,1},{4,6},{5,7},{6,4},{7,5},{8,10},{9,11},{10,... | collective-permute-start | bytes 786440 | tf_op jit(solution)/shard_map/ppermute | solution.py:27
  93.7 2.7 %collective-permute-done.17 = bf16[2,128,512]{2,1,0:T(8,128)(2,1)S(1)} collective-permute-done((bf16[2,128,512]{2,1,0:T(8,128)(2,1)S(1)}, bf16[2,128,512]{2,1,0:T(8,128)(2,1)S(1)}, u32[]{:S(2)}, u32[]{:S(2)}) %collective-permute-start.17) | collective-permute-done | bytes 262176 | tf_op jit(solution)/shard_map/ppermute | solution.py:27
  96.5 2.3 %collective-permute-start.21 = (bf16[128,512]{1,0:T(8,128)(2,1)S(1)}, bf16[128,512]{1,0:T(8,128)(2,1)S(1)}, u32[]{:S(2)}, u32[]{:S(2)}) collective-permute-start(bf16[128,512]{1,0:T(8,128)(2,1)S(1)} %slice_bitcast_fusion.2), channel_id=1, source_target_pairs={{0,4},{1,5},{2,6},{3,7},{4,0},{5,1},{6,2},{7,3},{8,12},{9,13},{10,... | collective-permute-start | bytes 393224 | tf_op jit(solution)/shard_map/ppermute | solution.py:27
  98.8 0.1 convert_add_fusion.1
  98.9 3.8 %collective-permute-start.22 = (bf16[128,512]{1,0:T(8,128)(2,1)S(1)}, bf16[128,512]{1,0:T(8,128)(2,1)S(1)}, u32[]{:S(2)}, u32[]{:S(2)}) collective-permute-start(bf16[128,512]{1,0:T(8,128)(2,1)S(1)} %fusion.10), channel_id=1, source_target_pairs={{0,4},{1,5},{2,6},{3,7},{4,0},{5,1},{6,2},{7,3},{8,12},{9,13},{10,... | collective-permute-start | bytes 393224 | tf_op jit(solution)/shard_map/ppermute | solution.py:27
  102.7 1.6 %collective-permute-done.25 = bf16[2,128,512]{2,1,0:T(8,128)(2,1)S(1)} collective-permute-done((bf16[2,128,512]{2,1,0:T(8,128)(2,1)S(1)}, bf16[2,128,512]{2,1,0:T(8,128)(2,1)S(1)}, u32[]{:S(2)}, u32[]{:S(2)}) %collective-permute-start.25) | collective-permute-done | bytes 262176 | tf_op jit(solution)/shard_map/ppermute | solution.py:27
  104.3 0.1 convert_add_fusion
  104.5 3.1 %collective-permute-start.27 = (bf16[128,512]{1,0:T(8,128)(2,1)S(1)}, bf16[128,512]{1,0:T(8,128)(2,1)S(1)}, u32[]{:S(2)}, u32[]{:S(2)}) collective-permute-start(bf16[128,512]{1,0:T(8,128)(2,1)S(1)} %fusion.11), channel_id=1, source_target_pairs={{0,4},{1,5},{2,6},{3,7},{4,0},{5,1},{6,2},{7,3},{8,12},{9,13},{10,... | collective-permute-start | bytes 393224 | tf_op jit(solution)/shard_map/ppermute | solution.py:27
  107.5 7.0 %collective-permute-done.22 = bf16[128,512]{1,0:T(8,128)(2,1)S(1)} collective-permute-done((bf16[128,512]{1,0:T(8,128)(2,1)S(1)}, bf16[128,512]{1,0:T(8,128)(2,1)S(1)}, u32[]{:S(2)}, u32[]{:S(2)}) %collective-permute-start.22) | collective-permute-done | bytes 131104 | tf_op jit(solution)/shard_map/ppermute | solution.py:27
  114.5 0.1 fusion.8
  114.7 0.1 collective-permute-start.26
  114.7 1.4 %collective-permute-done.27 = bf16[128,512]{1,0:T(8,128)(2,1)S(1)} collective-permute-done((bf16[128,512]{1,0:T(8,128)(2,1)S(1)}, bf16[128,512]{1,0:T(8,128)(2,1)S(1)}, u32[]{:S(2)}, u32[]{:S(2)}) %collective-permute-start.27) | collective-permute-done | bytes 131104 | tf_op jit(solution)/shard_map/ppermute | solution.py:27
  116.2 0.8 maximum_bitcast_fusion.1
  117.0 6.9 %collective-permute-done.26 = bf16[2,128,512]{2,1,0:T(8,128)(2,1)S(1)} collective-permute-done((bf16[2,128,512]{2,1,0:T(8,128)(2,1)S(1)}, bf16[2,128,512]{2,1,0:T(8,128)(2,1)S(1)}, u32[]{:S(2)}, u32[]{:S(2)}) %collective-permute-start.26) | collective-permute-done | bytes 262176 | tf_op jit(solution)/shard_map/ppermute | solution.py:27
  123.8 0.1 add_convert_fusion.1
  123.9 0.1 fusion.9
  124.0 0.8 maximum_bitcast_fusion
  (35 shorter events, 0.3 us)
Async XLA Ops:
  0.6 12.2 %copy-start.3 = (bf16[1,128,512]{2,1,0:T(8,128)(2,1)S(1)}, bf16[1,128,512]{2,1,0:T(8,128)(2,1)}, u32[]{:S(2)}) copy-start(bf16[1,128,512]{2,1,0:T(8,128)(2,1)} %param.11) | copy-start | bytes 393220
  0.6 27.0 %copy-start.2 = (bf16[1,4096]{1,0:T(2,128)(2,1)S(1)}, bf16[1,4096]{1,0:T(2,128)(2,1)}, u32[]{:S(2)}) copy-start(bf16[1,4096]{1,0:T(2,128)(2,1)} %refs_5_.5) | copy-start | bytes 24580
  0.7 27.0 %copy-start = (bf16[1,3,512,128]{3,2,1,0:T(8,128)(2,1)S(1)}, bf16[1,3,512,128]{3,2,1,0:T(8,128)(2,1)}, u32[]{:S(2)}) copy-start(bf16[1,3,512,128]{3,2,1,0:T(8,128)(2,1)} %refs_11_.5) | copy-start | bytes 1179652
  0.7 27.0 %copy-start.1 = (bf16[1,3,512,128]{3,2,1,0:T(8,128)(2,1)S(1)}, bf16[1,3,512,128]{3,2,1,0:T(8,128)(2,1)}, u32[]{:S(2)}) copy-start(bf16[1,3,512,128]{3,2,1,0:T(8,128)(2,1)} %refs_12_.5) | copy-start | bytes 1179652
  0.7 12.2 %collective-permute-start = (bf16[128,512]{1,0:T(8,128)(2,1)}, bf16[128,512]{1,0:T(8,128)(2,1)S(1)}, u32[]{:S(2)}, u32[]{:S(2)}) collective-permute-start(bf16[128,512]{1,0:T(8,128)(2,1)} %bitcast.82), channel_id=1, source_target_pairs={{0,4},{1,5},{2,6},{3,7},{4,0},{5,1},{6,2},{7,3},{8,12},{9,13},{10,... | collective-permute-start | bytes 393224 | tf_op jit(solution)/shard_map/ppermute | solution.py:27
  12.9 9.3 %collective-permute-start.1 = (bf16[2,128,512]{2,1,0:T(8,128)(2,1)S(1)}, bf16[2,128,512]{2,1,0:T(8,128)(2,1)S(1)}, u32[]{:S(2)}, u32[]{:S(2)}) collective-permute-start(bf16[2,128,512]{2,1,0:T(8,128)(2,1)S(1)} %pad_maximum_fusion.refs_1_), channel_id=1, source_target_pairs={{0,3},{1,0},{2,1},{3,2},{4,7},{5,4},{6,5},{7,6},{8,11},{9,8},{10,9... | collective-permute-start | bytes 786440 | tf_op jit(solution)/shard_map/ppermute | solution.py:27
  13.4 8.8 %collective-permute-start.2 = (bf16[2,128,512]{2,1,0:T(8,128)(2,1)S(1)}, bf16[2,128,512]{2,1,0:T(8,128)(2,1)S(1)}, u32[]{:S(2)}, u32[]{:S(2)}) collective-permute-start(bf16[2,128,512]{2,1,0:T(8,128)(2,1)S(1)} %pad_maximum_fusion.refs_1_), channel_id=1, source_target_pairs={{0,1},{1,2},{2,3},{3,0},{4,5},{5,6},{6,7},{7,4},{8,9},{9,10},{10,1... | collective-permute-start | bytes 786440 | tf_op jit(solution)/shard_map/ppermute | solution.py:27
  15.0 12.7 %collective-permute-start.3 = (bf16[2,128,512]{2,1,0:T(8,128)(2,1)S(1)}, bf16[2,128,512]{2,1,0:T(8,128)(2,1)S(1)}, u32[]{:S(2)}, u32[]{:S(2)}) collective-permute-start(bf16[2,128,512]{2,1,0:T(8,128)(2,1)S(1)} %pad_maximum_fusion.refs_1_), channel_id=1, source_target_pairs={{0,2},{1,3},{2,0},{3,1},{4,6},{5,7},{6,4},{7,5},{8,10},{9,11},{10,... | collective-permute-start | bytes 786440 | tf_op jit(solution)/shard_map/ppermute | solution.py:27
  27.7 11.0 %copy-start.4 = (bf16[2,128,512]{2,1,0:T(8,128)(2,1)S(1)}, bf16[2,128,512]{2,1,0:T(8,128)(2,1)}, u32[]{:S(2)}) copy-start(bf16[2,128,512]{2,1,0:T(8,128)(2,1)} %param.13) | copy-start | bytes 786436
  27.7 11.0 %copy-start.6 = (bf16[1,128,512]{2,1,0:T(8,128)(2,1)S(1)}, bf16[1,128,512]{2,1,0:T(8,128)(2,1)}, u32[]{:S(2)}) copy-start(bf16[1,128,512]{2,1,0:T(8,128)(2,1)} %param.12) | copy-start | bytes 393220
  27.7 16.0 %copy-start.5 = (bf16[2,128,512]{2,1,0:T(8,128)(2,1)S(1)}, bf16[2,128,512]{2,1,0:T(8,128)(2,1)}, u32[]{:S(2)}) copy-start(bf16[2,128,512]{2,1,0:T(8,128)(2,1)} %param.14) | copy-start | bytes 786436
  33.6 16.7 %collective-permute-start.4 = (bf16[2,128,512]{2,1,0:T(8,128)(2,1)S(1)}, bf16[2,128,512]{2,1,0:T(8,128)(2,1)S(1)}, u32[]{:S(2)}, u32[]{:S(2)}) collective-permute-start(bf16[2,128,512]{2,1,0:T(8,128)(2,1)S(1)} %get-tuple-element.57), channel_id=1, source_target_pairs={{0,3},{1,0},{2,1},{3,2},{4,7},{5,4},{6,5},{7,6},{8,11},{9,8},{10,9... | collective-permute-start | bytes 786440 | tf_op jit(solution)/shard_map/ppermute | solution.py:27
  33.8 16.4 %collective-permute-start.5 = (bf16[2,128,512]{2,1,0:T(8,128)(2,1)S(1)}, bf16[2,128,512]{2,1,0:T(8,128)(2,1)S(1)}, u32[]{:S(2)}, u32[]{:S(2)}) collective-permute-start(bf16[2,128,512]{2,1,0:T(8,128)(2,1)S(1)} %get-tuple-element.58), channel_id=1, source_target_pairs={{0,1},{1,2},{2,3},{3,0},{4,5},{5,6},{6,7},{7,4},{8,9},{9,10},{10,1... | collective-permute-start | bytes 786440 | tf_op jit(solution)/shard_map/ppermute | solution.py:27
  35.7 14.6 %collective-permute-start.6 = (bf16[2,128,512]{2,1,0:T(8,128)(2,1)S(1)}, bf16[2,128,512]{2,1,0:T(8,128)(2,1)S(1)}, u32[]{:S(2)}, u32[]{:S(2)}) collective-permute-start(bf16[2,128,512]{2,1,0:T(8,128)(2,1)S(1)} %get-tuple-element.59), channel_id=1, source_target_pairs={{0,2},{1,3},{2,0},{3,1},{4,6},{5,7},{6,4},{7,5},{8,10},{9,11},{10,... | collective-permute-start | bytes 786440 | tf_op jit(solution)/shard_map/ppermute | solution.py:27
  38.7 13.9 %collective-permute-start.8 = (bf16[128,512]{1,0:T(8,128)(2,1)S(1)}, bf16[128,512]{1,0:T(8,128)(2,1)S(1)}, u32[]{:S(2)}, u32[]{:S(2)}) collective-permute-start(bf16[128,512]{1,0:T(8,128)(2,1)S(1)} %fusion.7), channel_id=1, source_target_pairs={{0,12},{1,13},{2,14},{3,15},{4,8},{5,9},{6,10},{7,11},{8,20},{9,21... | collective-permute-start | bytes 393224 | tf_op jit(solution)/shard_map/ppermute | solution.py:27
  38.8 11.4 %collective-permute-start.7 = (bf16[128,512]{1,0:T(8,128)(2,1)S(1)}, bf16[128,512]{1,0:T(8,128)(2,1)S(1)}, u32[]{:S(2)}, u32[]{:S(2)}) collective-permute-start(bf16[128,512]{1,0:T(8,128)(2,1)S(1)} %fusion.7), channel_id=1, source_target_pairs={{0,8},{1,9},{2,10},{3,11},{4,12},{5,13},{6,14},{7,15},{8,16},{9,17... | collective-permute-start | bytes 393224 | tf_op jit(solution)/shard_map/ppermute | solution.py:27
  50.4 11.0 %collective-permute-start.12 = (bf16[2,128,512]{2,1,0:T(8,128)(2,1)S(1)}, bf16[2,128,512]{2,1,0:T(8,128)(2,1)S(1)}, u32[]{:S(2)}, u32[]{:S(2)}) collective-permute-start(bf16[2,128,512]{2,1,0:T(8,128)(2,1)S(1)} %get-tuple-element.100), channel_id=1, source_target_pairs={{0,16},{1,17},{2,18},{3,19},{4,20},{5,21},{6,22},{7,23},{8,24},{9,... | collective-permute-start | bytes 786440 | tf_op jit(solution)/shard_map/ppermute | solution.py:27
  50.5 15.4 %collective-permute-start.13 = (bf16[2,128,512]{2,1,0:T(8,128)(2,1)S(1)}, bf16[2,128,512]{2,1,0:T(8,128)(2,1)S(1)}, u32[]{:S(2)}, u32[]{:S(2)}) collective-permute-start(bf16[2,128,512]{2,1,0:T(8,128)(2,1)S(1)} %get-tuple-element.100), channel_id=1, source_target_pairs={{0,20},{1,21},{2,22},{3,23},{4,16},{5,17},{6,18},{7,19},{8,28},{9,... | collective-permute-start | bytes 786440 | tf_op jit(solution)/shard_map/ppermute | solution.py:27
  52.7 13.2 %collective-permute-start.14 = (bf16[2,128,512]{2,1,0:T(8,128)(2,1)S(1)}, bf16[2,128,512]{2,1,0:T(8,128)(2,1)S(1)}, u32[]{:S(2)}, u32[]{:S(2)}) collective-permute-start(bf16[2,128,512]{2,1,0:T(8,128)(2,1)S(1)} %pad_maximum_fusion.1.refs_1_), channel_id=1, source_target_pairs={{0,8},{1,9},{2,10},{3,11},{4,12},{5,13},{6,14},{7,15},{8,16},{9,17... | collective-permute-start | bytes 786440 | tf_op jit(solution)/shard_map/ppermute | solution.py:27
  52.8 15.9 %collective-permute-start.9 = (bf16[2,128,512]{2,1,0:T(8,128)(2,1)S(1)}, bf16[2,128,512]{2,1,0:T(8,128)(2,1)S(1)}, u32[]{:S(2)}, u32[]{:S(2)}) collective-permute-start(bf16[2,128,512]{2,1,0:T(8,128)(2,1)S(1)} %pad_maximum_fusion.1.refs_1_), channel_id=1, source_target_pairs={{0,3},{1,0},{2,1},{3,2},{4,7},{5,4},{6,5},{7,6},{8,11},{9,8},{10,9... | collective-permute-start | bytes 786440 | tf_op jit(solution)/shard_map/ppermute | solution.py:27
  52.9 18.7 %collective-permute-start.10 = (bf16[2,128,512]{2,1,0:T(8,128)(2,1)S(1)}, bf16[2,128,512]{2,1,0:T(8,128)(2,1)S(1)}, u32[]{:S(2)}, u32[]{:S(2)}) collective-permute-start(bf16[2,128,512]{2,1,0:T(8,128)(2,1)S(1)} %pad_maximum_fusion.1.refs_1_), channel_id=1, source_target_pairs={{0,1},{1,2},{2,3},{3,0},{4,5},{5,6},{6,7},{7,4},{8,9},{9,10},{10,1... | collective-permute-start | bytes 786440 | tf_op jit(solution)/shard_map/ppermute | solution.py:27
  61.4 10.8 %collective-permute-start.11 = (bf16[2,128,512]{2,1,0:T(8,128)(2,1)S(1)}, bf16[2,128,512]{2,1,0:T(8,128)(2,1)S(1)}, u32[]{:S(2)}, u32[]{:S(2)}) collective-permute-start(bf16[2,128,512]{2,1,0:T(8,128)(2,1)S(1)} %pad_maximum_fusion.1.refs_1_), channel_id=1, source_target_pairs={{0,2},{1,3},{2,0},{3,1},{4,6},{5,7},{6,4},{7,5},{8,10},{9,11},{10,... | collective-permute-start | bytes 786440 | tf_op jit(solution)/shard_map/ppermute | solution.py:27
  66.0 14.5 %collective-permute-start.18 = (bf16[2,128,512]{2,1,0:T(8,128)(2,1)S(1)}, bf16[2,128,512]{2,1,0:T(8,128)(2,1)S(1)}, u32[]{:S(2)}, u32[]{:S(2)}) collective-permute-start(bf16[2,128,512]{2,1,0:T(8,128)(2,1)S(1)} %shard_map.123.refs_1_), channel_id=1, source_target_pairs={{0,3},{1,0},{2,1},{3,2},{4,7},{5,4},{6,5},{7,6},{8,11},{9,8},{10,9... | collective-permute-start | bytes 786440 | tf_op jit(solution)/shard_map/ppermute | solution.py:27
  68.7 14.9 %collective-permute-start.19 = (bf16[2,128,512]{2,1,0:T(8,128)(2,1)S(1)}, bf16[2,128,512]{2,1,0:T(8,128)(2,1)S(1)}, u32[]{:S(2)}, u32[]{:S(2)}) collective-permute-start(bf16[2,128,512]{2,1,0:T(8,128)(2,1)S(1)} %shard_map.123.refs_1_), channel_id=1, source_target_pairs={{0,1},{1,2},{2,3},{3,0},{4,5},{5,6},{6,7},{7,4},{8,9},{9,10},{10,1... | collective-permute-start | bytes 786440 | tf_op jit(solution)/shard_map/ppermute | solution.py:27
  68.7 15.8 %collective-permute-start.20 = (bf16[2,128,512]{2,1,0:T(8,128)(2,1)S(1)}, bf16[2,128,512]{2,1,0:T(8,128)(2,1)S(1)}, u32[]{:S(2)}, u32[]{:S(2)}) collective-permute-start(bf16[2,128,512]{2,1,0:T(8,128)(2,1)S(1)} %shard_map.123.refs_1_), channel_id=1, source_target_pairs={{0,2},{1,3},{2,0},{3,1},{4,6},{5,7},{6,4},{7,5},{8,10},{9,11},{10,... | collective-permute-start | bytes 786440 | tf_op jit(solution)/shard_map/ppermute | solution.py:27
  78.0 14.4 %collective-permute-start.15 = (bf16[2,128,512]{2,1,0:T(8,128)(2,1)S(1)}, bf16[2,128,512]{2,1,0:T(8,128)(2,1)S(1)}, u32[]{:S(2)}, u32[]{:S(2)}) collective-permute-start(bf16[2,128,512]{2,1,0:T(8,128)(2,1)S(1)} %get-tuple-element.78), channel_id=1, source_target_pairs={{0,3},{1,0},{2,1},{3,2},{4,7},{5,4},{6,5},{7,6},{8,11},{9,8},{10,9... | collective-permute-start | bytes 786440 | tf_op jit(solution)/shard_map/ppermute | solution.py:27
  80.3 13.4 %collective-permute-start.16 = (bf16[2,128,512]{2,1,0:T(8,128)(2,1)S(1)}, bf16[2,128,512]{2,1,0:T(8,128)(2,1)S(1)}, u32[]{:S(2)}, u32[]{:S(2)}) collective-permute-start(bf16[2,128,512]{2,1,0:T(8,128)(2,1)S(1)} %get-tuple-element.79), channel_id=1, source_target_pairs={{0,1},{1,2},{2,3},{3,0},{4,5},{5,6},{6,7},{7,4},{8,9},{9,10},{10,1... | collective-permute-start | bytes 786440 | tf_op jit(solution)/shard_map/ppermute | solution.py:27
  80.5 15.9 %collective-permute-start.17 = (bf16[2,128,512]{2,1,0:T(8,128)(2,1)S(1)}, bf16[2,128,512]{2,1,0:T(8,128)(2,1)S(1)}, u32[]{:S(2)}, u32[]{:S(2)}) collective-permute-start(bf16[2,128,512]{2,1,0:T(8,128)(2,1)S(1)} %get-tuple-element.80), channel_id=1, source_target_pairs={{0,2},{1,3},{2,0},{3,1},{4,6},{5,7},{6,4},{7,5},{8,10},{9,11},{10,... | collective-permute-start | bytes 786440 | tf_op jit(solution)/shard_map/ppermute | solution.py:27
  90.3 12.4 %collective-permute-start.23 = (bf16[2,128,512]{2,1,0:T(8,128)(2,1)S(1)}, bf16[2,128,512]{2,1,0:T(8,128)(2,1)S(1)}, u32[]{:S(2)}, u32[]{:S(2)}) collective-permute-start(bf16[2,128,512]{2,1,0:T(8,128)(2,1)S(1)} %get-tuple-element.88), channel_id=1, source_target_pairs={{0,3},{1,0},{2,1},{3,2},{4,7},{5,4},{6,5},{7,6},{8,11},{9,8},{10,9... | collective-permute-start | bytes 786440 | tf_op jit(solution)/shard_map/ppermute | solution.py:27
  91.1 11.6 %collective-permute-start.24 = (bf16[2,128,512]{2,1,0:T(8,128)(2,1)S(1)}, bf16[2,128,512]{2,1,0:T(8,128)(2,1)S(1)}, u32[]{:S(2)}, u32[]{:S(2)}) collective-permute-start(bf16[2,128,512]{2,1,0:T(8,128)(2,1)S(1)} %get-tuple-element.86), channel_id=1, source_target_pairs={{0,1},{1,2},{2,3},{3,0},{4,5},{5,6},{6,7},{7,4},{8,9},{9,10},{10,1... | collective-permute-start | bytes 786440 | tf_op jit(solution)/shard_map/ppermute | solution.py:27
  92.4 11.9 %collective-permute-start.25 = (bf16[2,128,512]{2,1,0:T(8,128)(2,1)S(1)}, bf16[2,128,512]{2,1,0:T(8,128)(2,1)S(1)}, u32[]{:S(2)}, u32[]{:S(2)}) collective-permute-start(bf16[2,128,512]{2,1,0:T(8,128)(2,1)S(1)} %get-tuple-element.87), channel_id=1, source_target_pairs={{0,2},{1,3},{2,0},{3,1},{4,6},{5,7},{6,4},{7,5},{8,10},{9,11},{10,... | collective-permute-start | bytes 786440 | tf_op jit(solution)/shard_map/ppermute | solution.py:27
  96.5 11.1 %collective-permute-start.21 = (bf16[128,512]{1,0:T(8,128)(2,1)S(1)}, bf16[128,512]{1,0:T(8,128)(2,1)S(1)}, u32[]{:S(2)}, u32[]{:S(2)}) collective-permute-start(bf16[128,512]{1,0:T(8,128)(2,1)S(1)} %slice_bitcast_fusion.2), channel_id=1, source_target_pairs={{0,4},{1,5},{2,6},{3,7},{4,0},{5,1},{6,2},{7,3},{8,12},{9,13},{10,... | collective-permute-start | bytes 393224 | tf_op jit(solution)/shard_map/ppermute | solution.py:27
  98.9 15.6 %collective-permute-start.22 = (bf16[128,512]{1,0:T(8,128)(2,1)S(1)}, bf16[128,512]{1,0:T(8,128)(2,1)S(1)}, u32[]{:S(2)}, u32[]{:S(2)}) collective-permute-start(bf16[128,512]{1,0:T(8,128)(2,1)S(1)} %fusion.10), channel_id=1, source_target_pairs={{0,4},{1,5},{2,6},{3,7},{4,0},{5,1},{6,2},{7,3},{8,12},{9,13},{10,... | collective-permute-start | bytes 393224 | tf_op jit(solution)/shard_map/ppermute | solution.py:27
  104.5 11.7 %collective-permute-start.27 = (bf16[128,512]{1,0:T(8,128)(2,1)S(1)}, bf16[128,512]{1,0:T(8,128)(2,1)S(1)}, u32[]{:S(2)}, u32[]{:S(2)}) collective-permute-start(bf16[128,512]{1,0:T(8,128)(2,1)S(1)} %fusion.11), channel_id=1, source_target_pairs={{0,4},{1,5},{2,6},{3,7},{4,0},{5,1},{6,2},{7,3},{8,12},{9,13},{10,... | collective-permute-start | bytes 393224 | tf_op jit(solution)/shard_map/ppermute | solution.py:27
  114.7 9.2 %collective-permute-start.26 = (bf16[2,128,512]{2,1,0:T(8,128)(2,1)S(1)}, bf16[2,128,512]{2,1,0:T(8,128)(2,1)S(1)}, u32[]{:S(2)}, u32[]{:S(2)}) collective-permute-start(bf16[2,128,512]{2,1,0:T(8,128)(2,1)S(1)} %pad_maximum_fusion.2), channel_id=1, source_target_pairs={{0,8},{1,9},{2,10},{3,11},{4,12},{5,13},{6,14},{7,15},{8,16},{9,17... | collective-permute-start | bytes 786440 | tf_op jit(solution)/shard_map/ppermute | solution.py:27

commit v4 on v3

--- a/solution.py
+++ b/solution.py
@@ -44,11 +44,15 @@
     return jnp.cos(angles), jnp.sin(angles)
 
 
-def attend_kernel(tick, *refs):
+def attend_kernel(tick, held, *refs):
     scalars, pieces, refs = refs[0], refs[1 : 1 + Y], refs[1 + Y :]
     gain, cos, sin, wq_hbm, wkv_hbm, wo_hbm, kc_hbm, vc_hbm = refs[:8]
     outs, refs = refs[8 : 8 + Y], refs[8 + Y :]
-    wq, wkv, wo, kc, vc, att, sems = refs
+    if held:
+        wq, wkv, wo = wq_hbm, wkv_hbm, wo_hbm
+    else:
+        wq, wkv, wo = refs[:3]
+    kc, vc, att, sems = refs[-4:]
     length, high, low = scalars[tick], scalars[3], scalars[4]
 
     taken = {k: [ref.at[0], ref.at[1]] for k, ref in zip((0,) + ORDER, pieces)}
@@ -62,7 +66,7 @@
     order = [(k, slot) for k in range(Y) for slot in range(2)]
     spots = [chunk(slot, low - k + Y) for k, slot in order]
     loads = []
-    for i, at in enumerate(spots):
+    for i, at in enumerate(() if held else spots):
         loads.append(
             (
                 pltpu.make_async_copy(wq_hbm.at[at], wq.at[at], sems.at[2 * i]),
@@ -72,13 +76,16 @@
     n = 2 * len(order)
     load_k = pltpu.make_async_copy(kc_hbm.at[0, tick], kc, sems.at[n])
     load_v = pltpu.make_async_copy(vc_hbm.at[0, tick], vc, sems.at[n + 1])
-    load_o = pltpu.make_async_copy(wo_hbm, wo, sems.at[n + 2])
-    for a, b in loads:
-        a.start()
-        b.start()
+    if not held:
+        load_o = pltpu.make_async_copy(wo_hbm, wo, sems.at[n + 2])
+    if not held:
+        for a, b in loads:
+            a.start()
+            b.start()
     load_k.start()
     load_v.start()
-    load_o.start()
+    if not held:
+        load_o.start()
 
     total = jnp.zeros((rows, width), f32)
     for k, slot in order:
@@ -92,8 +99,9 @@
         at = spots[i]
         v = taken[k][slot][...].astype(f32)
         normed = (v * inverse * gain[:, at].astype(f32)).astype(bf16)
-        loads[i][0].wait()
-        loads[i][1].wait()
+        if not held:
+            loads[i][0].wait()
+            loads[i][1].wait()
         q = q + jnp.dot(normed, wq[at, :], preferred_element_type=f32)
         kv = kv + jnp.dot(normed, wkv[at, :], preferred_element_type=f32)
     c, s = cos[tick], sin[tick]
@@ -132,30 +140,30 @@
     for h in range(heads):
         att[:, h * HD : (h + 1) * HD] = out[h * rows : (h + 1) * rows]
     a = att[...]
-    load_o.wait()
+    if not held:
+        load_o.wait()
     for slot in (1, 0):
         for k in range(Y):
             at = chunk(slot, low + k)
             given[k][slot][...] = jnp.dot(a, wo[:, at], preferred_element_type=f32).astype(bf16)
 
 
-def attend(tick, scalars, gathered, gain, cos, sin, wq, wkv, wo, kc, vc):
+def attend(tick, held, scalars, gathered, gain, cos, sin, wq, wkv, wo, kc, vc):
     rows, width = gathered[0].shape[-2:]
     vmem, hbm = pl.BlockSpec(memory_space=pltpu.VMEM), pl.BlockSpec(memory_space=pltpu.HBM)
     cols = wq.shape[0]
     out_shape = [jax.ShapeDtypeStruct((2, rows, width), bf16)] * Y
     flops = 2 * rows * cols * (2 * wq.shape[1] + wkv.shape[1])
     return pl.pallas_call(
-        functools.partial(attend_kernel, tick),
+        functools.partial(attend_kernel, tick, held),
         out_shape=out_shape,
         in_specs=[pl.BlockSpec(memory_space=pltpu.SMEM)]
         + [vmem] * (len(gathered) + 3)
-        + [hbm] * 5,
+        + [vmem if held else hbm] * 3
+        + [hbm] * 2,
         out_specs=[vmem] * len(out_shape),
-        scratch_shapes=[
-            pltpu.VMEM(wq.shape, bf16),
-            pltpu.VMEM(wkv.shape, bf16),
-            pltpu.VMEM(wo.shape, bf16),
+        scratch_shapes=([] if held else [pltpu.VMEM(w.shape, bf16) for w in (wq, wkv, wo)])
+        + [
             pltpu.VMEM(kc.shape[2:], bf16),
             pltpu.VMEM(vc.shape[2:], bf16),
             pltpu.VMEM((rows, wq.shape[1]), bf16),
@@ -166,6 +174,29 @@
             flops=flops, bytes_accessed=40 * 1024 * 1024, transcendentals=512 * 640
         ),
     )(scalars, *gathered, gain, cos, sin, wq, wkv, wo, kc, vc)
+
+
+def load_kernel(wq, wkv, wo, wq_out, wkv_out, wo_out, sems):
+    copies = [
+        pltpu.make_async_copy(a, b, sems.at[i])
+        for i, (a, b) in enumerate(((wq, wq_out), (wkv, wkv_out), (wo, wo_out)))
+    ]
+    for copy in copies:
+        copy.start()
+    for copy in copies:
+        copy.wait()
+
+
+def load(wq, wkv, wo):
+    hbm, vmem = pl.BlockSpec(memory_space=pltpu.HBM), pl.BlockSpec(memory_space=pltpu.VMEM)
+    return pl.pallas_call(
+        load_kernel,
+        out_shape=[pltpu.VMEM(w.shape, w.dtype) for w in (wq, wkv, wo)],
+        in_specs=[hbm] * 3,
+        out_specs=[vmem] * 3,
+        scratch_shapes=[pltpu.SemaphoreType.DMA((3,))],
+        compiler_params=pltpu.CompilerParams(vmem_limit_bytes=2 * 1024 * 1024),
+    )(wq, wkv, wo)
 
 
 def combine_kernel(where, own, other, base, local, out):
@@ -234,17 +265,19 @@
     all0 = gather(pair0)
     wkv = pltpu.with_memory_space_constraint(wkv, pltpu.HBM)
 
-    def block(tick, gathered):
+    held = load(wq, wkv, wo)
+
+    def block(tick, gathered, weights=None):
         return attend(
-            tick, scalars, gathered, norm_gain, cos, sin,
-            wq, wkv, wo, keys_cache, values_cache,
+            tick, weights is not None, scalars, gathered, norm_gain, cos, sin,
+            *(weights or (wq, wkv, wo)), keys_cache, values_cache,
         )
 
     early = after(block_last, all0[1])
     other1 = jnp.where(final, incoming_two[0], add(x0, early[0]))
     z1 = send(other1, hop(1, True))
 
-    parts0 = block(0, all0)
+    parts0 = block(0, all0, held)
     got0 = exchange(parts0)
     own1, enter_two, enter_last = after((other1, incoming_two, incoming_last), parts0)
     a1 = send(own1, hop(1))
@@ -254,7 +287,7 @@
     sums0 = sum(g.astype(f32) for g in got0).astype(bf16)
     out2 = jnp.where(sid >= last - 1, entering[None], sums0)
     own, other = send(out2, hop(2)), send(out2, hop(2, True))
-    a1, z1 = after((a1, z1), out2)
+    a1, z1 = after((a1, z1), own)
     a1 = jnp.where(first, incoming_two[0], a1)
     pair1 = jnp.stack([a1, z1])
     base = send(pair1, hop(1))

time: 125 us -> 135 us (1.080)
  waiting for transfers between devices: 46.5 us -> 58.7 us
  starting transfers between devices: 52.3 us -> 46.7 us
  Pallas kernels: 17.7 us -> 20.5 us
    ppermute x28, waiting for transfers between devices: 46.5 us -> 58.7 us  [move(): return lax.ppermute(value, ('section', 'tensor'), pairs)]
    ppermute x28, starting transfers between devices: 52.3 us -> 46.7 us  [move(): return lax.ppermute(value, ('section', 'tensor'), pairs)]
    pallas_call x3 -> x4, Pallas kernels: 17.5 us -> 20.4 us  [the longest x3 16.2 us: attend(): pl.pallas_call(functools.partial(attend_kernel, tick, held), out_shape=ou...]
  transfers between devices with their start and end apart: 28 -> 28, of which waited for: 12 -> 14; matrix products, arithmetic and copies ran while one was open for 5% -> 5% of each run, Pallas kernels for 9% -> 12%
where the time goes in v4:
time: 135 us; the launch traced here: 134 us
  waiting for transfers between devices  58.7 us (43%)
  starting transfers between devices  46.7 us (35%)
  Pallas kernels  20.5 us (15%)
  local copies, waits for them, and re-layouts  4.05 us (3%)
  other arithmetic  3.34 us (2%)
    ppermute x28, waiting for transfers between devices, move(): return lax.ppermute(value, ('section', 'tensor'), pairs)  58.7 us
    ppermute x28, starting transfers between devices, move(): return lax.ppermute(value, ('section', 'tensor'), pairs)  46.7 us
    pallas_call x3, Pallas kernels, attend(): pl.pallas_call(functools.partial(attend_kernel, tick, held), out_shape=ou...  16.2 us
    pallas_call x1, Pallas kernels, load(): pl.pallas_call(load_kernel, out_shape=[pltpu.VMEM(w.shape, w.dtype) for w...  4.15 us
    unnamed x15, local copies, waits for them, and re-layouts  3.26 us
  transfers between devices with their start and end apart: 28, of which 14 were waited for; matrix products, arithmetic and copies ran while one was open for 5% of the time, Pallas kernels for 12%

profile of v4, /device:TPU:16, one launch (start us, length us, event | category | flops | bytes accessed | tf_op | source)
XLA Modules:
  0.0 134.2 jit_solution(15744386304870549284)
XLA Ops:
  0.6 7.3 %collective-permute-start = (bf16[128,512]{1,0:T(8,128)(2,1)}, bf16[128,512]{1,0:T(8,128)(2,1)S(1)}, u32[]{:S(2)}, u32[]{:S(2)}) collective-permute-start(bf16[128,512]{1,0:T(8,128)(2,1)} %bitcast.82), channel_id=1, source_target_pairs={{0,4},{1,5},{2,6},{3,7},{4,0},{5,1},{6,2},{7,3},{8,12},{9,13},{10,... | collective-permute-start | bytes 393224 | tf_op jit(solution)/shard_map/ppermute | solution.py:27
  7.9 0.7 dynamic_slice.3
  8.7 0.1 add_convert_fusion.3
  8.7 0.8 multiply_sine_fusion
  9.5 3.2 %copy.15 = bf16[512,8,2,128]{3,1,2,0:T(8,128)(2,1)} copy(bf16[512,8,2,128]{3,2,1,0:T(2,128)(2,1)} %bitcast.81) | data formatting | bytes 4194304
  12.7 0.1 pad_add_fusion.refs_0_
  12.8 0.0 collective-permute-done
  12.9 0.5 collective-permute-start.1
  13.4 1.6 %collective-permute-start.2 = (bf16[2,128,512]{2,1,0:T(8,128)(2,1)S(1)}, bf16[2,128,512]{2,1,0:T(8,128)(2,1)S(1)}, u32[]{:S(2)}, u32[]{:S(2)}) collective-permute-start(bf16[2,128,512]{2,1,0:T(8,128)(2,1)S(1)} %pad_maximum_fusion.refs_1_), channel_id=1, source_target_pairs={{0,1},{1,2},{2,3},{3,0},{4,5},{5,6},{6,7},{7,4},{8,9},{9,10},{10,1... | collective-permute-start | bytes 786440 | tf_op jit(solution)/shard_map/ppermute | solution.py:27
  15.0 1.3 collective-permute-start.3
  16.3 4.2 %shard_map.122 = (bf16[4096,512]{1,0:T(8,128)(2,1)S(1)}, bf16[4096,256]{1,0:T(8,128)(2,1)S(1)}, bf16[512,4096]{1,0:T(8,128)(2,1)S(1)}) custom-call(bf16[4096,512]{1,0:T(8,128)(2,1)} %bitcast.72, bf16[4096,256]{1,0:T(8,128)(2,1)} %bitcast.78, bf16[512,4096]{1,0:T(8,128)(2,1)} %bitcast.75), custom_call_target="tpu_custom_call" | custom-call | tf_op jit(solution)/shard_map/pallas_call | solution.py:192
  20.5 1.7 %collective-permute-done.1.refs_2_ = bf16[2,128,512]{2,1,0:T(8,128)(2,1)S(1)} collective-permute-done((bf16[2,128,512]{2,1,0:T(8,128)(2,1)S(1)}, bf16[2,128,512]{2,1,0:T(8,128)(2,1)S(1)}, u32[]{:S(2)}, u32[]{:S(2)}) %collective-permute-start.1) | collective-permute-done | bytes 262176 | tf_op jit(solution)/shard_map/ppermute | solution.py:27
  22.2 5.5 %collective-permute-done.3.refs_4_ = bf16[2,128,512]{2,1,0:T(8,128)(2,1)S(1)} collective-permute-done((bf16[2,128,512]{2,1,0:T(8,128)(2,1)S(1)}, bf16[2,128,512]{2,1,0:T(8,128)(2,1)S(1)}, u32[]{:S(2)}, u32[]{:S(2)}) %collective-permute-start.3) | collective-permute-done | bytes 262176 | tf_op jit(solution)/shard_map/ppermute | solution.py:27
  27.7 0.0 copy-start.4
  27.7 0.0 copy-start.6
  27.7 0.0 copy-start.5
  27.7 4.5 %shard_map.123 = (bf16[2,128,512]{2,1,0:T(8,128)(2,1)S(1)}, bf16[2,128,512]{2,1,0:T(8,128)(2,1)S(1)}, bf16[2,128,512]{2,1,0:T(8,128)(2,1)S(1)}, bf16[2,128,512]{2,1,0:T(8,128)(2,1)S(1)}) custom-call(s32[5]{0:T(128)S(1)} %pad_add_fusion.refs_0_, bf16[2,128,512]{2,1,0:T(8,128)(2,1)S(1)} %pad_maximum_fusion.refs_1_, ...), custom_call_target="tpu_custom_call" | custom-call | flops 1342177280 | bytes 41943040 | tf_op jit(solution)/shard_map/pallas_call | solution.py:157
  32.2 0.2 collective-permute-start.4
  32.5 1.9 %collective-permute-start.5 = (bf16[2,128,512]{2,1,0:T(8,128)(2,1)S(1)}, bf16[2,128,512]{2,1,0:T(8,128)(2,1)S(1)}, u32[]{:S(2)}, u32[]{:S(2)}) collective-permute-start(bf16[2,128,512]{2,1,0:T(8,128)(2,1)S(1)} %get-tuple-element.64), channel_id=1, source_target_pairs={{0,1},{1,2},{2,3},{3,0},{4,5},{5,6},{6,7},{7,4},{8,9},{9,10},{10,1... | collective-permute-start | bytes 786440 | tf_op jit(solution)/shard_map/ppermute | solution.py:27
  34.3 3.0 %collective-permute-start.6 = (bf16[2,128,512]{2,1,0:T(8,128)(2,1)S(1)}, bf16[2,128,512]{2,1,0:T(8,128)(2,1)S(1)}, u32[]{:S(2)}, u32[]{:S(2)}) collective-permute-start(bf16[2,128,512]{2,1,0:T(8,128)(2,1)S(1)} %get-tuple-element.65), channel_id=1, source_target_pairs={{0,2},{1,3},{2,0},{3,1},{4,6},{5,7},{6,4},{7,5},{8,10},{9,11},{10,... | collective-permute-start | bytes 786440 | tf_op jit(solution)/shard_map/ppermute | solution.py:27
  37.3 0.1 fusion.7
  37.4 0.1 collective-permute-start.7
  37.5 7.7 %collective-permute-done.7 = bf16[128,512]{1,0:T(8,128)(2,1)S(1)} collective-permute-done((bf16[128,512]{1,0:T(8,128)(2,1)S(1)}, bf16[128,512]{1,0:T(8,128)(2,1)S(1)}, u32[]{:S(2)}, u32[]{:S(2)}) %collective-permute-start.7) | collective-permute-done | bytes 131104 | tf_op jit(solution)/shard_map/ppermute | solution.py:27
  45.2 1.1 collective-permute-done.6
  46.2 0.2 broadcast_select_fusion
  46.4 1.6 %collective-permute-start.9 = (bf16[2,128,512]{2,1,0:T(8,128)(2,1)S(1)}, bf16[2,128,512]{2,1,0:T(8,128)(2,1)S(1)}, u32[]{:S(2)}, u32[]{:S(2)}) collective-permute-start(bf16[2,128,512]{2,1,0:T(8,128)(2,1)S(1)} %get-tuple-element.106), channel_id=1, source_target_pairs={{0,16},{1,17},{2,18},{3,19},{4,20},{5,21},{6,22},{7,23},{8,24},{9,... | collective-permute-start | bytes 786440 | tf_op jit(solution)/shard_map/ppermute | solution.py:27
  48.0 3.3 %collective-permute-start.13 = (bf16[2,128,512]{2,1,0:T(8,128)(2,1)S(1)}, bf16[2,128,512]{2,1,0:T(8,128)(2,1)S(1)}, u32[]{:S(2)}, u32[]{:S(2)}) collective-permute-start(bf16[2,128,512]{2,1,0:T(8,128)(2,1)S(1)} %get-tuple-element.106), channel_id=1, source_target_pairs={{0,20},{1,21},{2,22},{3,23},{4,16},{5,17},{6,18},{7,19},{8,28},{9,... | collective-permute-start | bytes 786440 | tf_op jit(solution)/shard_map/ppermute | solution.py:27
  51.3 6.6 %collective-permute-done.8 = bf16[128,512]{1,0:T(8,128)(2,1)S(1)} collective-permute-done((bf16[128,512]{1,0:T(8,128)(2,1)S(1)}, bf16[128,512]{1,0:T(8,128)(2,1)S(1)}, u32[]{:S(2)}, u32[]{:S(2)}) %collective-permute-start.8) | collective-permute-done | bytes 131104 | tf_op jit(solution)/shard_map/ppermute | solution.py:27
  57.9 5.5 %collective-permute-done.9.own = bf16[2,128,512]{2,1,0:T(8,128)(2,1)S(1)} collective-permute-done((bf16[2,128,512]{2,1,0:T(8,128)(2,1)S(1)}, bf16[2,128,512]{2,1,0:T(8,128)(2,1)S(1)}, u32[]{:S(2)}, u32[]{:S(2)}) %collective-permute-start.9) | collective-permute-done | bytes 262176 | tf_op jit(solution)/shard_map/ppermute | solution.py:27
  63.4 0.1 collective-permute-start.14
  63.5 0.3 collective-permute-start.10
  63.8 1.8 %collective-permute-start.11 = (bf16[2,128,512]{2,1,0:T(8,128)(2,1)S(1)}, bf16[2,128,512]{2,1,0:T(8,128)(2,1)S(1)}, u32[]{:S(2)}, u32[]{:S(2)}) collective-permute-start(bf16[2,128,512]{2,1,0:T(8,128)(2,1)S(1)} %pad_maximum_fusion.1.refs_1_), channel_id=1, source_target_pairs={{0,1},{1,2},{2,3},{3,0},{4,5},{5,6},{6,7},{7,4},{8,9},{9,10},{10,1... | collective-permute-start | bytes 786440 | tf_op jit(solution)/shard_map/ppermute | solution.py:27
  65.6 2.3 %collective-permute-start.12 = (bf16[2,128,512]{2,1,0:T(8,128)(2,1)S(1)}, bf16[2,128,512]{2,1,0:T(8,128)(2,1)S(1)}, u32[]{:S(2)}, u32[]{:S(2)}) collective-permute-start(bf16[2,128,512]{2,1,0:T(8,128)(2,1)S(1)} %pad_maximum_fusion.1.refs_1_), channel_id=1, source_target_pairs={{0,2},{1,3},{2,0},{3,1},{4,6},{5,7},{6,4},{7,5},{8,10},{9,11},{10,... | collective-permute-start | bytes 786440 | tf_op jit(solution)/shard_map/ppermute | solution.py:27
  67.9 4.7 %collective-permute-done.14.base = bf16[2,128,512]{2,1,0:T(8,128)(2,1)S(1)} collective-permute-done((bf16[2,128,512]{2,1,0:T(8,128)(2,1)S(1)}, bf16[2,128,512]{2,1,0:T(8,128)(2,1)S(1)}, u32[]{:S(2)}, u32[]{:S(2)}) %collective-permute-start.14) | collective-permute-done | bytes 262176 | tf_op jit(solution)/shard_map/ppermute | solution.py:27
  72.6 0.1 shard_map.124.refs_1_
  72.8 0.3 collective-permute-start.18
  73.1 1.8 %collective-permute-start.19 = (bf16[2,128,512]{2,1,0:T(8,128)(2,1)S(1)}, bf16[2,128,512]{2,1,0:T(8,128)(2,1)S(1)}, u32[]{:S(2)}, u32[]{:S(2)}) collective-permute-start(bf16[2,128,512]{2,1,0:T(8,128)(2,1)S(1)} %shard_map.124.refs_1_), channel_id=1, source_target_pairs={{0,1},{1,2},{2,3},{3,0},{4,5},{5,6},{6,7},{7,4},{8,9},{9,10},{10,1... | collective-permute-start | bytes 786440 | tf_op jit(solution)/shard_map/ppermute | solution.py:27
  74.9 2.3 %collective-permute-start.20 = (bf16[2,128,512]{2,1,0:T(8,128)(2,1)S(1)}, bf16[2,128,512]{2,1,0:T(8,128)(2,1)S(1)}, u32[]{:S(2)}, u32[]{:S(2)}) collective-permute-start(bf16[2,128,512]{2,1,0:T(8,128)(2,1)S(1)} %shard_map.124.refs_1_), channel_id=1, source_target_pairs={{0,2},{1,3},{2,0},{3,1},{4,6},{5,7},{6,4},{7,5},{8,10},{9,11},{10,... | collective-permute-start | bytes 786440 | tf_op jit(solution)/shard_map/ppermute | solution.py:27
  77.2 3.7 %collective-permute-done.12.refs_4_ = bf16[2,128,512]{2,1,0:T(8,128)(2,1)S(1)} collective-permute-done((bf16[2,128,512]{2,1,0:T(8,128)(2,1)S(1)}, bf16[2,128,512]{2,1,0:T(8,128)(2,1)S(1)}, u32[]{:S(2)}, u32[]{:S(2)}) %collective-permute-start.12) | collective-permute-done | bytes 262176 | tf_op jit(solution)/shard_map/ppermute | solution.py:27
  80.8 5.8 %shard_map.125 = (bf16[2,128,512]{2,1,0:T(8,128)(2,1)S(1)}, bf16[2,128,512]{2,1,0:T(8,128)(2,1)S(1)}, bf16[2,128,512]{2,1,0:T(8,128)(2,1)S(1)}, bf16[2,128,512]{2,1,0:T(8,128)(2,1)S(1)}) custom-call(s32[5]{0:T(128)S(1)} %pad_add_fusion.refs_0_, bf16[2,128,512]{2,1,0:T(8,128)(2,1)S(1)} %pad_maximum_fusion.1.refs_1_, ...), custom_call_target="tpu_custom_call" | custom-call | flops 1342177280 | bytes 41943040 | tf_op jit(solution)/shard_map/pallas_call | solution.py:157
  86.7 0.1 collective-permute-start.15
  86.8 2.0 %collective-permute-start.16 = (bf16[2,128,512]{2,1,0:T(8,128)(2,1)S(1)}, bf16[2,128,512]{2,1,0:T(8,128)(2,1)S(1)}, u32[]{:S(2)}, u32[]{:S(2)}) collective-permute-start(bf16[2,128,512]{2,1,0:T(8,128)(2,1)S(1)} %get-tuple-element.85), channel_id=1, source_target_pairs={{0,1},{1,2},{2,3},{3,0},{4,5},{5,6},{6,7},{7,4},{8,9},{9,10},{10,1... | collective-permute-start | bytes 786440 | tf_op jit(solution)/shard_map/ppermute | solution.py:27
  88.8 1.3 collective-permute-start.17
  90.1 2.0 %collective-permute-done.20.refs_4_ = bf16[2,128,512]{2,1,0:T(8,128)(2,1)S(1)} collective-permute-done((bf16[2,128,512]{2,1,0:T(8,128)(2,1)S(1)}, bf16[2,128,512]{2,1,0:T(8,128)(2,1)S(1)}, u32[]{:S(2)}, u32[]{:S(2)}) %collective-permute-start.20) | collective-permute-done | bytes 262176 | tf_op jit(solution)/shard_map/ppermute | solution.py:27
  92.1 5.8 %shard_map.126 = (bf16[2,128,512]{2,1,0:T(8,128)(2,1)S(1)}, bf16[2,128,512]{2,1,0:T(8,128)(2,1)S(1)}, bf16[2,128,512]{2,1,0:T(8,128)(2,1)S(1)}, bf16[2,128,512]{2,1,0:T(8,128)(2,1)S(1)}) custom-call(s32[5]{0:T(128)S(1)} %pad_add_fusion.refs_0_, bf16[2,128,512]{2,1,0:T(8,128)(2,1)S(1)} %shard_map.124.refs_1_, ...), custom_call_target="tpu_custom_call" | custom-call | flops 1342177280 | bytes 41943040 | tf_op jit(solution)/shard_map/pallas_call | solution.py:157
  98.0 0.1 collective-permute-start.23
  98.1 2.0 %collective-permute-start.24 = (bf16[2,128,512]{2,1,0:T(8,128)(2,1)S(1)}, bf16[2,128,512]{2,1,0:T(8,128)(2,1)S(1)}, u32[]{:S(2)}, u32[]{:S(2)}) collective-permute-start(bf16[2,128,512]{2,1,0:T(8,128)(2,1)S(1)} %get-tuple-element.92), channel_id=1, source_target_pairs={{0,1},{1,2},{2,3},{3,0},{4,5},{5,6},{6,7},{7,4},{8,9},{9,10},{10,1... | collective-permute-start | bytes 786440 | tf_op jit(solution)/shard_map/ppermute | solution.py:27
  100.1 1.3 collective-permute-start.25
  101.3 2.0 %collective-permute-done.17 = bf16[2,128,512]{2,1,0:T(8,128)(2,1)S(1)} collective-permute-done((bf16[2,128,512]{2,1,0:T(8,128)(2,1)S(1)}, bf16[2,128,512]{2,1,0:T(8,128)(2,1)S(1)}, u32[]{:S(2)}, u32[]{:S(2)}) %collective-permute-start.17) | collective-permute-done | bytes 262176 | tf_op jit(solution)/shard_map/ppermute | solution.py:27
  103.4 0.1 convert_add_fusion.1
  103.5 0.6 collective-permute-start.22
  104.1 5.6 %collective-permute-start.21 = (bf16[128,512]{1,0:T(8,128)(2,1)S(1)}, bf16[128,512]{1,0:T(8,128)(2,1)S(1)}, u32[]{:S(2)}, u32[]{:S(2)}) collective-permute-start(bf16[128,512]{1,0:T(8,128)(2,1)S(1)} %slice_bitcast_fusion.2), channel_id=1, source_target_pairs={{0,4},{1,5},{2,6},{3,7},{4,0},{5,1},{6,2},{7,3},{8,12},{9,13},{10,... | collective-permute-start | bytes 393224 | tf_op jit(solution)/shard_map/ppermute | solution.py:27
  109.7 1.3 collective-permute-done.25
  110.9 0.1 convert_add_fusion
  111.1 4.2 %collective-permute-start.27 = (bf16[128,512]{1,0:T(8,128)(2,1)S(1)}, bf16[128,512]{1,0:T(8,128)(2,1)S(1)}, u32[]{:S(2)}, u32[]{:S(2)}) collective-permute-start(bf16[128,512]{1,0:T(8,128)(2,1)S(1)} %fusion.11), channel_id=1, source_target_pairs={{0,4},{1,5},{2,6},{3,7},{4,0},{5,1},{6,2},{7,3},{8,12},{9,13},{10,... | collective-permute-start | bytes 393224 | tf_op jit(solution)/shard_map/ppermute | solution.py:27
  115.2 2.0 %collective-permute-done.21 = bf16[128,512]{1,0:T(8,128)(2,1)S(1)} collective-permute-done((bf16[128,512]{1,0:T(8,128)(2,1)S(1)}, bf16[128,512]{1,0:T(8,128)(2,1)S(1)}, u32[]{:S(2)}, u32[]{:S(2)}) %collective-permute-start.21) | collective-permute-done | bytes 131104 | tf_op jit(solution)/shard_map/ppermute | solution.py:27
  117.2 0.1 fusion.8
  117.3 0.1 collective-permute-start.26
  117.4 5.3 %collective-permute-done.27 = bf16[128,512]{1,0:T(8,128)(2,1)S(1)} collective-permute-done((bf16[128,512]{1,0:T(8,128)(2,1)S(1)}, bf16[128,512]{1,0:T(8,128)(2,1)S(1)}, u32[]{:S(2)}, u32[]{:S(2)}) %collective-permute-start.27) | collective-permute-done | bytes 131104 | tf_op jit(solution)/shard_map/ppermute | solution.py:27
  122.7 0.8 maximum_bitcast_fusion.1
  123.5 9.8 %collective-permute-done.26 = bf16[2,128,512]{2,1,0:T(8,128)(2,1)S(1)} collective-permute-done((bf16[2,128,512]{2,1,0:T(8,128)(2,1)S(1)}, bf16[2,128,512]{2,1,0:T(8,128)(2,1)S(1)}, u32[]{:S(2)}, u32[]{:S(2)}) %collective-permute-start.26) | collective-permute-done | bytes 262176 | tf_op jit(solution)/shard_map/ppermute | solution.py:27
  133.2 0.1 fusion.9
  133.3 0.1 add_convert_fusion.1
  133.4 0.8 maximum_bitcast_fusion
  (36 shorter events, 0.3 us)
Async XLA Ops:
  0.6 12.2 %copy-start.3 = (bf16[1,128,512]{2,1,0:T(8,128)(2,1)S(1)}, bf16[1,128,512]{2,1,0:T(8,128)(2,1)}, u32[]{:S(2)}) copy-start(bf16[1,128,512]{2,1,0:T(8,128)(2,1)} %param.11) | copy-start | bytes 393220
  0.6 12.2 %collective-permute-start = (bf16[128,512]{1,0:T(8,128)(2,1)}, bf16[128,512]{1,0:T(8,128)(2,1)S(1)}, u32[]{:S(2)}, u32[]{:S(2)}) collective-permute-start(bf16[128,512]{1,0:T(8,128)(2,1)} %bitcast.82), channel_id=1, source_target_pairs={{0,4},{1,5},{2,6},{3,7},{4,0},{5,1},{6,2},{7,3},{8,12},{9,13},{10,... | collective-permute-start | bytes 393224 | tf_op jit(solution)/shard_map/ppermute | solution.py:27
  12.9 9.3 %collective-permute-start.1 = (bf16[2,128,512]{2,1,0:T(8,128)(2,1)S(1)}, bf16[2,128,512]{2,1,0:T(8,128)(2,1)S(1)}, u32[]{:S(2)}, u32[]{:S(2)}) collective-permute-start(bf16[2,128,512]{2,1,0:T(8,128)(2,1)S(1)} %pad_maximum_fusion.refs_1_), channel_id=1, source_target_pairs={{0,3},{1,0},{2,1},{3,2},{4,7},{5,4},{6,5},{7,6},{8,11},{9,8},{10,9... | collective-permute-start | bytes 786440 | tf_op jit(solution)/shard_map/ppermute | solution.py:27
  13.4 8.8 %collective-permute-start.2 = (bf16[2,128,512]{2,1,0:T(8,128)(2,1)S(1)}, bf16[2,128,512]{2,1,0:T(8,128)(2,1)S(1)}, u32[]{:S(2)}, u32[]{:S(2)}) collective-permute-start(bf16[2,128,512]{2,1,0:T(8,128)(2,1)S(1)} %pad_maximum_fusion.refs_1_), channel_id=1, source_target_pairs={{0,1},{1,2},{2,3},{3,0},{4,5},{5,6},{6,7},{7,4},{8,9},{9,10},{10,1... | collective-permute-start | bytes 786440 | tf_op jit(solution)/shard_map/ppermute | solution.py:27
  15.0 12.7 %collective-permute-start.3 = (bf16[2,128,512]{2,1,0:T(8,128)(2,1)S(1)}, bf16[2,128,512]{2,1,0:T(8,128)(2,1)S(1)}, u32[]{:S(2)}, u32[]{:S(2)}) collective-permute-start(bf16[2,128,512]{2,1,0:T(8,128)(2,1)S(1)} %pad_maximum_fusion.refs_1_), channel_id=1, source_target_pairs={{0,2},{1,3},{2,0},{3,1},{4,6},{5,7},{6,4},{7,5},{8,10},{9,11},{10,... | collective-permute-start | bytes 786440 | tf_op jit(solution)/shard_map/ppermute | solution.py:27
  16.3 11.4 %copy-start = (bf16[1,3,512,128]{3,2,1,0:T(8,128)(2,1)S(1)}, bf16[1,3,512,128]{3,2,1,0:T(8,128)(2,1)}, u32[]{:S(2)}) copy-start(bf16[1,3,512,128]{3,2,1,0:T(8,128)(2,1)} %refs_11_.5) | copy-start | bytes 1179652
  16.3 11.4 %copy-start.1 = (bf16[1,3,512,128]{3,2,1,0:T(8,128)(2,1)S(1)}, bf16[1,3,512,128]{3,2,1,0:T(8,128)(2,1)}, u32[]{:S(2)}) copy-start(bf16[1,3,512,128]{3,2,1,0:T(8,128)(2,1)} %refs_12_.5) | copy-start | bytes 1179652
  16.3 11.4 %copy-start.2 = (bf16[1,4096]{1,0:T(2,128)(2,1)S(1)}, bf16[1,4096]{1,0:T(2,128)(2,1)}, u32[]{:S(2)}) copy-start(bf16[1,4096]{1,0:T(2,128)(2,1)} %refs_5_.5) | copy-start | bytes 24580
  27.7 9.7 %copy-start.4 = (bf16[2,128,512]{2,1,0:T(8,128)(2,1)S(1)}, bf16[2,128,512]{2,1,0:T(8,128)(2,1)}, u32[]{:S(2)}) copy-start(bf16[2,128,512]{2,1,0:T(8,128)(2,1)} %param.13) | copy-start | bytes 786436
  27.7 9.7 %copy-start.6 = (bf16[1,128,512]{2,1,0:T(8,128)(2,1)S(1)}, bf16[1,128,512]{2,1,0:T(8,128)(2,1)}, u32[]{:S(2)}) copy-start(bf16[1,128,512]{2,1,0:T(8,128)(2,1)} %param.12) | copy-start | bytes 393220
  27.7 9.8 %copy-start.5 = (bf16[2,128,512]{2,1,0:T(8,128)(2,1)S(1)}, bf16[2,128,512]{2,1,0:T(8,128)(2,1)}, u32[]{:S(2)}) copy-start(bf16[2,128,512]{2,1,0:T(8,128)(2,1)} %param.14) | copy-start | bytes 786436
  32.2 12.9 %collective-permute-start.4 = (bf16[2,128,512]{2,1,0:T(8,128)(2,1)S(1)}, bf16[2,128,512]{2,1,0:T(8,128)(2,1)S(1)}, u32[]{:S(2)}, u32[]{:S(2)}) collective-permute-start(bf16[2,128,512]{2,1,0:T(8,128)(2,1)S(1)} %get-tuple-element.63), channel_id=1, source_target_pairs={{0,3},{1,0},{2,1},{3,2},{4,7},{5,4},{6,5},{7,6},{8,11},{9,8},{10,9... | collective-permute-start | bytes 786440 | tf_op jit(solution)/shard_map/ppermute | solution.py:27
  32.5 12.7 %collective-permute-start.5 = (bf16[2,128,512]{2,1,0:T(8,128)(2,1)S(1)}, bf16[2,128,512]{2,1,0:T(8,128)(2,1)S(1)}, u32[]{:S(2)}, u32[]{:S(2)}) collective-permute-start(bf16[2,128,512]{2,1,0:T(8,128)(2,1)S(1)} %get-tuple-element.64), channel_id=1, source_target_pairs={{0,1},{1,2},{2,3},{3,0},{4,5},{5,6},{6,7},{7,4},{8,9},{9,10},{10,1... | collective-permute-start | bytes 786440 | tf_op jit(solution)/shard_map/ppermute | solution.py:27
  34.3 11.9 %collective-permute-start.6 = (bf16[2,128,512]{2,1,0:T(8,128)(2,1)S(1)}, bf16[2,128,512]{2,1,0:T(8,128)(2,1)S(1)}, u32[]{:S(2)}, u32[]{:S(2)}) collective-permute-start(bf16[2,128,512]{2,1,0:T(8,128)(2,1)S(1)} %get-tuple-element.65), channel_id=1, source_target_pairs={{0,2},{1,3},{2,0},{3,1},{4,6},{5,7},{6,4},{7,5},{8,10},{9,11},{10,... | collective-permute-start | bytes 786440 | tf_op jit(solution)/shard_map/ppermute | solution.py:27
  37.4 7.8 %collective-permute-start.7 = (bf16[128,512]{1,0:T(8,128)(2,1)S(1)}, bf16[128,512]{1,0:T(8,128)(2,1)S(1)}, u32[]{:S(2)}, u32[]{:S(2)}) collective-permute-start(bf16[128,512]{1,0:T(8,128)(2,1)S(1)} %fusion.7), channel_id=1, source_target_pairs={{0,8},{1,9},{2,10},{3,11},{4,12},{5,13},{6,14},{7,15},{8,16},{9,17... | collective-permute-start | bytes 393224 | tf_op jit(solution)/shard_map/ppermute | solution.py:27
  46.4 17.0 %collective-permute-start.9 = (bf16[2,128,512]{2,1,0:T(8,128)(2,1)S(1)}, bf16[2,128,512]{2,1,0:T(8,128)(2,1)S(1)}, u32[]{:S(2)}, u32[]{:S(2)}) collective-permute-start(bf16[2,128,512]{2,1,0:T(8,128)(2,1)S(1)} %get-tuple-element.106), channel_id=1, source_target_pairs={{0,16},{1,17},{2,18},{3,19},{4,20},{5,21},{6,22},{7,23},{8,24},{9,... | collective-permute-start | bytes 786440 | tf_op jit(solution)/shard_map/ppermute | solution.py:27
  48.0 9.9 %collective-permute-start.8 = (bf16[128,512]{1,0:T(8,128)(2,1)S(1)}, bf16[128,512]{1,0:T(8,128)(2,1)S(1)}, u32[]{:S(2)}, u32[]{:S(2)}) collective-permute-start(bf16[128,512]{1,0:T(8,128)(2,1)S(1)} %fusion.7), channel_id=1, source_target_pairs={{0,12},{1,13},{2,14},{3,15},{4,8},{5,9},{6,10},{7,11},{8,20},{9,21... | collective-permute-start | bytes 393224 | tf_op jit(solution)/shard_map/ppermute | solution.py:27
  48.0 19.9 %collective-permute-start.13 = (bf16[2,128,512]{2,1,0:T(8,128)(2,1)S(1)}, bf16[2,128,512]{2,1,0:T(8,128)(2,1)S(1)}, u32[]{:S(2)}, u32[]{:S(2)}) collective-permute-start(bf16[2,128,512]{2,1,0:T(8,128)(2,1)S(1)} %get-tuple-element.106), channel_id=1, source_target_pairs={{0,20},{1,21},{2,22},{3,23},{4,16},{5,17},{6,18},{7,19},{8,28},{9,... | collective-permute-start | bytes 786440 | tf_op jit(solution)/shard_map/ppermute | solution.py:27
  63.4 9.2 %collective-permute-start.14 = (bf16[2,128,512]{2,1,0:T(8,128)(2,1)S(1)}, bf16[2,128,512]{2,1,0:T(8,128)(2,1)S(1)}, u32[]{:S(2)}, u32[]{:S(2)}) collective-permute-start(bf16[2,128,512]{2,1,0:T(8,128)(2,1)S(1)} %pad_maximum_fusion.1.refs_1_), channel_id=1, source_target_pairs={{0,8},{1,9},{2,10},{3,11},{4,12},{5,13},{6,14},{7,15},{8,16},{9,17... | collective-permute-start | bytes 786440 | tf_op jit(solution)/shard_map/ppermute | solution.py:27
  63.5 11.4 %collective-permute-start.10 = (bf16[2,128,512]{2,1,0:T(8,128)(2,1)S(1)}, bf16[2,128,512]{2,1,0:T(8,128)(2,1)S(1)}, u32[]{:S(2)}, u32[]{:S(2)}) collective-permute-start(bf16[2,128,512]{2,1,0:T(8,128)(2,1)S(1)} %pad_maximum_fusion.1.refs_1_), channel_id=1, source_target_pairs={{0,3},{1,0},{2,1},{3,2},{4,7},{5,4},{6,5},{7,6},{8,11},{9,8},{10,9... | collective-permute-start | bytes 786440 | tf_op jit(solution)/shard_map/ppermute | solution.py:27
  63.8 13.4 %collective-permute-start.11 = (bf16[2,128,512]{2,1,0:T(8,128)(2,1)S(1)}, bf16[2,128,512]{2,1,0:T(8,128)(2,1)S(1)}, u32[]{:S(2)}, u32[]{:S(2)}) collective-permute-start(bf16[2,128,512]{2,1,0:T(8,128)(2,1)S(1)} %pad_maximum_fusion.1.refs_1_), channel_id=1, source_target_pairs={{0,1},{1,2},{2,3},{3,0},{4,5},{5,6},{6,7},{7,4},{8,9},{9,10},{10,1... | collective-permute-start | bytes 786440 | tf_op jit(solution)/shard_map/ppermute | solution.py:27
  65.6 15.2 %collective-permute-start.12 = (bf16[2,128,512]{2,1,0:T(8,128)(2,1)S(1)}, bf16[2,128,512]{2,1,0:T(8,128)(2,1)S(1)}, u32[]{:S(2)}, u32[]{:S(2)}) collective-permute-start(bf16[2,128,512]{2,1,0:T(8,128)(2,1)S(1)} %pad_maximum_fusion.1.refs_1_), channel_id=1, source_target_pairs={{0,2},{1,3},{2,0},{3,1},{4,6},{5,7},{6,4},{7,5},{8,10},{9,11},{10,... | collective-permute-start | bytes 786440 | tf_op jit(solution)/shard_map/ppermute | solution.py:27
  72.8 16.0 %collective-permute-start.18 = (bf16[2,128,512]{2,1,0:T(8,128)(2,1)S(1)}, bf16[2,128,512]{2,1,0:T(8,128)(2,1)S(1)}, u32[]{:S(2)}, u32[]{:S(2)}) collective-permute-start(bf16[2,128,512]{2,1,0:T(8,128)(2,1)S(1)} %shard_map.124.refs_1_), channel_id=1, source_target_pairs={{0,3},{1,0},{2,1},{3,2},{4,7},{5,4},{6,5},{7,6},{8,11},{9,8},{10,9... | collective-permute-start | bytes 786440 | tf_op jit(solution)/shard_map/ppermute | solution.py:27
  73.1 17.0 %collective-permute-start.19 = (bf16[2,128,512]{2,1,0:T(8,128)(2,1)S(1)}, bf16[2,128,512]{2,1,0:T(8,128)(2,1)S(1)}, u32[]{:S(2)}, u32[]{:S(2)}) collective-permute-start(bf16[2,128,512]{2,1,0:T(8,128)(2,1)S(1)} %shard_map.124.refs_1_), channel_id=1, source_target_pairs={{0,1},{1,2},{2,3},{3,0},{4,5},{5,6},{6,7},{7,4},{8,9},{9,10},{10,1... | collective-permute-start | bytes 786440 | tf_op jit(solution)/shard_map/ppermute | solution.py:27
  74.9 17.2 %collective-permute-start.20 = (bf16[2,128,512]{2,1,0:T(8,128)(2,1)S(1)}, bf16[2,128,512]{2,1,0:T(8,128)(2,1)S(1)}, u32[]{:S(2)}, u32[]{:S(2)}) collective-permute-start(bf16[2,128,512]{2,1,0:T(8,128)(2,1)S(1)} %shard_map.124.refs_1_), channel_id=1, source_target_pairs={{0,2},{1,3},{2,0},{3,1},{4,6},{5,7},{6,4},{7,5},{8,10},{9,11},{10,... | collective-permute-start | bytes 786440 | tf_op jit(solution)/shard_map/ppermute | solution.py:27
  86.7 13.4 %collective-permute-start.15 = (bf16[2,128,512]{2,1,0:T(8,128)(2,1)S(1)}, bf16[2,128,512]{2,1,0:T(8,128)(2,1)S(1)}, u32[]{:S(2)}, u32[]{:S(2)}) collective-permute-start(bf16[2,128,512]{2,1,0:T(8,128)(2,1)S(1)} %get-tuple-element.84), channel_id=1, source_target_pairs={{0,3},{1,0},{2,1},{3,2},{4,7},{5,4},{6,5},{7,6},{8,11},{9,8},{10,9... | collective-permute-start | bytes 786440 | tf_op jit(solution)/shard_map/ppermute | solution.py:27
  86.8 14.5 %collective-permute-start.16 = (bf16[2,128,512]{2,1,0:T(8,128)(2,1)S(1)}, bf16[2,128,512]{2,1,0:T(8,128)(2,1)S(1)}, u32[]{:S(2)}, u32[]{:S(2)}) collective-permute-start(bf16[2,128,512]{2,1,0:T(8,128)(2,1)S(1)} %get-tuple-element.85), channel_id=1, source_target_pairs={{0,1},{1,2},{2,3},{3,0},{4,5},{5,6},{6,7},{7,4},{8,9},{9,10},{10,1... | collective-permute-start | bytes 786440 | tf_op jit(solution)/shard_map/ppermute | solution.py:27
  88.8 14.6 %collective-permute-start.17 = (bf16[2,128,512]{2,1,0:T(8,128)(2,1)S(1)}, bf16[2,128,512]{2,1,0:T(8,128)(2,1)S(1)}, u32[]{:S(2)}, u32[]{:S(2)}) collective-permute-start(bf16[2,128,512]{2,1,0:T(8,128)(2,1)S(1)} %get-tuple-element.86), channel_id=1, source_target_pairs={{0,2},{1,3},{2,0},{3,1},{4,6},{5,7},{6,4},{7,5},{8,10},{9,11},{10,... | collective-permute-start | bytes 786440 | tf_op jit(solution)/shard_map/ppermute | solution.py:27
  98.0 11.7 %collective-permute-start.23 = (bf16[2,128,512]{2,1,0:T(8,128)(2,1)S(1)}, bf16[2,128,512]{2,1,0:T(8,128)(2,1)S(1)}, u32[]{:S(2)}, u32[]{:S(2)}) collective-permute-start(bf16[2,128,512]{2,1,0:T(8,128)(2,1)S(1)} %get-tuple-element.94), channel_id=1, source_target_pairs={{0,3},{1,0},{2,1},{3,2},{4,7},{5,4},{6,5},{7,6},{8,11},{9,8},{10,9... | collective-permute-start | bytes 786440 | tf_op jit(solution)/shard_map/ppermute | solution.py:27
  98.1 11.6 %collective-permute-start.24 = (bf16[2,128,512]{2,1,0:T(8,128)(2,1)S(1)}, bf16[2,128,512]{2,1,0:T(8,128)(2,1)S(1)}, u32[]{:S(2)}, u32[]{:S(2)}) collective-permute-start(bf16[2,128,512]{2,1,0:T(8,128)(2,1)S(1)} %get-tuple-element.92), channel_id=1, source_target_pairs={{0,1},{1,2},{2,3},{3,0},{4,5},{5,6},{6,7},{7,4},{8,9},{9,10},{10,1... | collective-permute-start | bytes 786440 | tf_op jit(solution)/shard_map/ppermute | solution.py:27
  100.1 10.8 %collective-permute-start.25 = (bf16[2,128,512]{2,1,0:T(8,128)(2,1)S(1)}, bf16[2,128,512]{2,1,0:T(8,128)(2,1)S(1)}, u32[]{:S(2)}, u32[]{:S(2)}) collective-permute-start(bf16[2,128,512]{2,1,0:T(8,128)(2,1)S(1)} %get-tuple-element.93), channel_id=1, source_target_pairs={{0,2},{1,3},{2,0},{3,1},{4,6},{5,7},{6,4},{7,5},{8,10},{9,11},{10,... | collective-permute-start | bytes 786440 | tf_op jit(solution)/shard_map/ppermute | solution.py:27
  103.5 11.7 %collective-permute-start.22 = (bf16[128,512]{1,0:T(8,128)(2,1)S(1)}, bf16[128,512]{1,0:T(8,128)(2,1)S(1)}, u32[]{:S(2)}, u32[]{:S(2)}) collective-permute-start(bf16[128,512]{1,0:T(8,128)(2,1)S(1)} %fusion.10), channel_id=1, source_target_pairs={{0,4},{1,5},{2,6},{3,7},{4,0},{5,1},{6,2},{7,3},{8,12},{9,13},{10,... | collective-permute-start | bytes 393224 | tf_op jit(solution)/shard_map/ppermute | solution.py:27
  104.1 13.1 %collective-permute-start.21 = (bf16[128,512]{1,0:T(8,128)(2,1)S(1)}, bf16[128,512]{1,0:T(8,128)(2,1)S(1)}, u32[]{:S(2)}, u32[]{:S(2)}) collective-permute-start(bf16[128,512]{1,0:T(8,128)(2,1)S(1)} %slice_bitcast_fusion.2), channel_id=1, source_target_pairs={{0,4},{1,5},{2,6},{3,7},{4,0},{5,1},{6,2},{7,3},{8,12},{9,13},{10,... | collective-permute-start | bytes 393224 | tf_op jit(solution)/shard_map/ppermute | solution.py:27
  111.1 11.6 %collective-permute-start.27 = (bf16[128,512]{1,0:T(8,128)(2,1)S(1)}, bf16[128,512]{1,0:T(8,128)(2,1)S(1)}, u32[]{:S(2)}, u32[]{:S(2)}) collective-permute-start(bf16[128,512]{1,0:T(8,128)(2,1)S(1)} %fusion.11), channel_id=1, source_target_pairs={{0,4},{1,5},{2,6},{3,7},{4,0},{5,1},{6,2},{7,3},{8,12},{9,13},{10,... | collective-permute-start | bytes 393224 | tf_op jit(solution)/shard_map/ppermute | solution.py:27
  117.3 15.9 %collective-permute-start.26 = (bf16[2,128,512]{2,1,0:T(8,128)(2,1)S(1)}, bf16[2,128,512]{2,1,0:T(8,128)(2,1)S(1)}, u32[]{:S(2)}, u32[]{:S(2)}) collective-permute-start(bf16[2,128,512]{2,1,0:T(8,128)(2,1)S(1)} %pad_maximum_fusion.2), channel_id=1, source_target_pairs={{0,8},{1,9},{2,10},{3,11},{4,12},{5,13},{6,14},{7,15},{8,16},{9,17... | collective-permute-start | bytes 786440 | tf_op jit(solution)/shard_map/ppermute | solution.py:27
